TPU v7x, 256 devices: a whole 4x4x8 slice. The times are simulated.
256 devices in a mesh: dom: 64 (over z, x, core), rep: 4 (over y).
Axes of the slice: x: 4, y: 4, z: 8, core: 2. Of those that a mesh axis runs over, the one named last changes fastest.
Arguments:
- features: bfloat16 [262144, 256], P(('dom', 'rep')), may hold values from -6 to 6
- history: bfloat16 [4, 262144, 256], P(None, 'dom'), may hold values from -6 to 6
- tiles: bfloat16 [8192, 128, 128], P(('dom', 'rep')), may hold values from -0.25 to 0.25
- tile_cols: int32 [8192], P(('dom', 'rep')), may hold values from 0 to 7
- halo_ids: int32 [4, 393216], P(None, ('dom', 'rep')), may hold values from 0 to 4095
- halo_counts: int32 [4, 16384], P(None, ('dom', 'rep')), may hold values from 1 to 24, as said below
- halo_dst: int32 [4, 393216], P(None, ('dom', 'rep')), may hold values from 0 to 1023
- halo_wt: bfloat16 [4, 393216], P(None, ('dom', 'rep')), may hold values from 0.25 to 1
- weights: bfloat16 [4, 256, 256], replicated, may hold values from -0.375 to 0.375
- cotangent: bfloat16 [262144, 256], P(('dom', 'rep')), may hold values from -0.03125 to 0.03125
Outputs:
- embeddings: bfloat16 [262144, 256], P(('dom', 'rep'))
- new_history: bfloat16 [3, 262144, 256], P(None, 'dom')
- weight_grad: float32 [4, 256, 256], replicated
Inputs may be any that keep to these rules, and one draw needn't show every extreme that they name: `halo_counts`: in every layer, every device has some owner with 24 live slots, and some owner receives 24 live slots from every device; the other counts are independent. Slots past the count hold valid but unused ids.
All inputs are finite; a program needn't handle non-finite values.
Results may differ from a plain program's by a relative error of at most 0.02.
Values may be sent and summed in bfloat16 or wider, within the bound.
No kernel may reach another device: no remote copies, remote signals or barrier semaphores. Data moves between devices by JAX's collectives and lax.ppermute only.
A program may use at most 128 MiB of HBM per device.

v0:
```python
import jax
import jax.numpy as jnp
from jax import lax
from jax.sharding import PartitionSpec as P

restart_rate = 0.1
beta_table = [
    0.4054651081081644,
    0.22314355131420976,
    0.15415067982725836,
    0.11778303565638346,
    0.09531017980432493,
    0.08004270767353637,
    0.06899287148695142,
    0.06062462181643484,
]


def block_sum(tiles, tile_cols, hidden):
    row_count, feat_width = hidden.shape
    block_count = row_count // 128
    per_block = tiles.shape[0] // block_count
    blocks = hidden.reshape(block_count, 128, feat_width)
    gathered = blocks[tile_cols]
    product = jnp.einsum("tij,tjw->tiw", tiles, gathered, preferred_element_type=jnp.float32)
    return (
        product.reshape(block_count, per_block, 128, feat_width)
        .sum(axis=1)
        .reshape(row_count, feat_width)
    )


def block_back(tiles, tile_cols, grad_bf):
    row_count, feat_width = grad_bf.shape
    block_count = row_count // 128
    per_block = tiles.shape[0] // block_count
    blocks = grad_bf.reshape(block_count, 128, feat_width)
    spread = jnp.broadcast_to(blocks[:, None], (block_count, per_block, 128, feat_width)).reshape(
        block_count * per_block, 128, feat_width
    )
    product = jnp.einsum("tji,tjw->tiw", tiles, spread, preferred_element_type=jnp.float32)
    select = (tile_cols[:, None] == jnp.arange(block_count, dtype=jnp.int32)[None, :]).astype(
        jnp.float32
    )
    summed = jnp.einsum("tn,tiw->niw", select, product, precision=lax.Precision.HIGHEST)
    return summed.reshape(row_count, feat_width)


def body(
    features,
    history,
    tiles,
    tile_cols,
    halo_ids,
    halo_counts,
    halo_dst,
    halo_wt,
    weights,
    cotangent,
):
    row_count, feat_width = features.shape
    layer_count = weights.shape[0]
    part_count = lax.axis_size("dom")
    slot_count = halo_ids.shape[1]
    capacity = slot_count // part_count
    slot_ids = halo_ids.reshape(layer_count, part_count, capacity)
    position = jnp.arange(row_count, dtype=jnp.int32)
    slot_rank = jnp.arange(capacity, dtype=jnp.int32)
    hidden = features
    saved = []
    fresh = []
    for depth in range(layer_count):
        beta = beta_table[depth]
        layer_table = history[depth]

        def fetch_layer(portion, layer_table=layer_table):
            picked = jnp.take(layer_table, portion, axis=0)
            return lax.all_to_all(picked, "dom", split_axis=0, concat_axis=0, tiled=True)

        pulled = fetch_layer(
            lax.all_to_all(slot_ids[depth], "dom", split_axis=0, concat_axis=0, tiled=True)
        ).reshape(slot_count, feat_width)
        live = (slot_rank[None, :] < halo_counts[depth][:, None]).reshape(slot_count)
        slot_weight = jnp.where(live, halo_wt[depth], jnp.zeros_like(halo_wt[depth]))
        scatter_matrix = jnp.where(
            halo_dst[depth][None, :] == position[:, None],
            slot_weight[None, :],
            jnp.zeros((), jnp.bfloat16),
        )
        halo_term = jnp.dot(scatter_matrix, pulled, preferred_element_type=jnp.float32)
        support = (1.0 - restart_rate) * (
            block_sum(tiles, tile_cols, hidden) + halo_term
        ) + restart_rate * features.astype(jnp.float32)
        support_bf = support.astype(jnp.bfloat16)
        preact = (1.0 - beta) * support + beta * jnp.dot(
            support_bf, weights[depth], preferred_element_type=jnp.float32
        )
        saved.append((support_bf, preact))
        hidden = jax.nn.gelu(preact).astype(jnp.bfloat16)
        if depth + 1 < layer_count:
            fresh.append(hidden)
    new_history = lax.all_gather(jnp.stack(fresh), "rep", axis=1, tiled=True)
    grad_out = cotangent
    partial_value = []
    for depth in range(layer_count - 1, -1, -1):
        beta = beta_table[depth]
        support_bf, preact = saved[depth]
        gelu_grad = jax.vjp(jax.nn.gelu, preact)[1](grad_out.astype(jnp.float32))[0]
        grad_bf = gelu_grad.astype(jnp.bfloat16)
        partial_value.append(
            beta
            * lax.dot_general(
                support_bf, grad_bf, (((0,), (0,)), ((), ())), preferred_element_type=jnp.float32
            )
        )
        if depth > 0:
            grad_support = (1.0 - beta) * gelu_grad + beta * jnp.dot(
                grad_bf, weights[depth].T, preferred_element_type=jnp.float32
            )
            grad_out = (
                (1.0 - restart_rate)
                * block_back(tiles, tile_cols, grad_support.astype(jnp.bfloat16))
            ).astype(jnp.bfloat16)
    local_grads = jnp.stack(partial_value[::-1])
    weight_grad = lax.psum(local_grads, ("dom", "rep"))
    return (hidden, new_history, weight_grad)


def solution(mesh):
    in_specs = (
        P(("dom", "rep"), None),
        P(None, "dom", None),
        P(("dom", "rep"), None, None),
        P(("dom", "rep")),
        P(None, ("dom", "rep")),
        P(None, ("dom", "rep")),
        P(None, ("dom", "rep")),
        P(None, ("dom", "rep")),
        P(),
        P(("dom", "rep"), None),
    )
    out_specs = (P(("dom", "rep"), None), P(None, "dom", None), P())
    return jax.shard_map(body, mesh=mesh, in_specs=in_specs, out_specs=out_specs, check_vma=False)
```

profile of v0, /device:TPU:2, one launch (start us, length us, event | category | flops | bytes accessed | tf_op | source)
XLA Modules:
  0.0 553.8 jit_solution(14496655330043295842)
XLA Ops:
  9.7 12.0 %all-to-all-start = ((s32[64,1,24]{2,1,0:T(1,128)}), s32[64,1,24]{2,1,0:T(1,128)S(1)}, u32[]{:S(2)}, u32[]{:S(2)}) async-start(s32[64,1,24]{2,1,0:T(1,128)} %bitcast.5), calls=%async_computation | async-start | bytes 65536 | tf_op jit(solution)/shard_map/all_to_all | solution.py:81
  21.7 5.7 %slice_bitcast_fusion = (bf16[4096,256]{1,0:T(8,128)(2,1)S(1)}, bf16[4096,256]{1,0:T(8,128)(2,1)}, bf16[4096,256]{1,0:T(8,128)(2,1)}, bf16[4096,256]{1,0:T(8,128)(2,1)}) fusion(bf16[4,4096,256]{2,1,0:T(8,128)(2,1)} %param.13), kind=kLoop, calls=%fused_computation.31 | loop fusion | bytes 16777216 | tf_op jit(solution)/shard_map/squeeze | solution.py:74
  28.8 3.0 gather_fusion
  31.9 10.3 %all-to-all-start.2 = ((s32[64,1,24]{2,1,0:T(1,128)}), s32[64,1,24]{2,1,0:T(1,128)S(1)}, u32[]{:S(2)}, u32[]{:S(2)}) async-start(s32[64,1,24]{2,1,0:T(1,128)} %bitcast.16), calls=%async_computation.2 | async-start | bytes 65536 | tf_op jit(solution)/shard_map/all_to_all | solution.py:81
  42.3 6.4 %gather_fusion.4 = bf16[1536,256]{1,0:T(8,128)(2,1)} fusion(bf16[4096,256]{1,0:T(8,128)(2,1)} %get-tuple-element.18, s32[2048]{0:T(1024)S(1)} %pad_clamp_fusion.3), kind=kCustom, calls=%fused_computation.clone | custom fusion | bytes 1579008 | tf_op jit(solution)/shard_map/jit(_take)/gather | solution.py:77
  48.7 2.0 all-to-all-done.2
  50.8 8.4 %all-to-all-start.4 = ((s32[64,1,24]{2,1,0:T(1,128)}), s32[64,1,24]{2,1,0:T(1,128)S(1)}, u32[]{:S(2)}, u32[]{:S(2)}) async-start(s32[64,1,24]{2,1,0:T(1,128)} %bitcast.27), calls=%async_computation.4 | async-start | bytes 65536 | tf_op jit(solution)/shard_map/all_to_all | solution.py:81
  59.2 2.3 broadcast_select_fusion.3
  61.5 6.3 %all-to-all-done.4 = s32[64,1,24]{2,1,0:T(1,128)S(1)} async-done(((s32[64,1,24]{2,1,0:T(1,128)}), s32[64,1,24]{2,1,0:T(1,128)S(1)}, u32[]{:S(2)}, u32[]{:S(2)}) %all-to-all-start.4) | async-done | bytes 6176 | tf_op jit(solution)/shard_map/all_to_all | solution.py:81
  67.7 6.3 %all-to-all-start.1 = ((bf16[64,24,256]{2,1,0:T(8,128)(2,1)}), bf16[64,24,256]{2,1,0:T(8,128)(2,1)}, u32[]{:S(2)}, u32[]{:S(2)}) async-start(bf16[64,24,256]{2,1,0:T(8,128)(2,1)} %broadcast_select_fusion.3), calls=%async_computation.1 | async-start | bytes 1572864 | tf_op jit(solution)/shard_map/all_to_all | solution.py:78
  74.2 3.4 bitcast_reduce_fusion.3
  77.7 6.4 %gather_fusion.5 = bf16[1536,256]{1,0:T(8,128)(2,1)} fusion(bf16[4096,256]{1,0:T(8,128)(2,1)} %get-tuple-element.17, s32[2048]{0:T(1024)S(1)} %pad_clamp_fusion.2), kind=kCustom, calls=%fused_computation.1.clone | custom fusion | bytes 1579008 | tf_op jit(solution)/shard_map/jit(_take)/gather | solution.py:77
  84.1 2.3 broadcast_select_fusion.2
  86.5 10.8 %all-to-all-done.1 = bf16[64,24,256]{2,1,0:T(8,128)(2,1)} async-done(((bf16[64,24,256]{2,1,0:T(8,128)(2,1)}), bf16[64,24,256]{2,1,0:T(8,128)(2,1)}, u32[]{:S(2)}, u32[]{:S(2)}) %all-to-all-start.1) | async-done | bytes 786464 | tf_op jit(solution)/shard_map/all_to_all | solution.py:78
  97.3 6.0 %all-to-all-start.3 = ((bf16[64,24,256]{2,1,0:T(8,128)(2,1)}), bf16[64,24,256]{2,1,0:T(8,128)(2,1)}, u32[]{:S(2)}, u32[]{:S(2)}) async-start(bf16[64,24,256]{2,1,0:T(8,128)(2,1)} %broadcast_select_fusion.2), calls=%async_computation.3 | async-start | bytes 1572864 | tf_op jit(solution)/shard_map/all_to_all | solution.py:78
  103.8 2.5 copy.24
  106.6 6.4 %gather_fusion.6 = bf16[1536,256]{1,0:T(8,128)(2,1)} fusion(bf16[4096,256]{1,0:T(8,128)(2,1)} %get-tuple-element.19, s32[2048]{0:T(1024)S(1)} %pad_clamp_fusion.1), kind=kCustom, calls=%fused_computation.2.clone | custom fusion | bytes 1579008 | tf_op jit(solution)/shard_map/jit(_take)/gather | solution.py:77
  113.0 2.3 broadcast_select_fusion.1
  115.3 3.6 fusion.37
  118.9 7.5 %all-to-all-done.3 = bf16[64,24,256]{2,1,0:T(8,128)(2,1)} async-done(((bf16[64,24,256]{2,1,0:T(8,128)(2,1)}), bf16[64,24,256]{2,1,0:T(8,128)(2,1)}, u32[]{:S(2)}, u32[]{:S(2)}) %all-to-all-start.3) | async-done | bytes 786464 | tf_op jit(solution)/shard_map/all_to_all | solution.py:78
  126.4 6.2 %all-to-all-start.5 = ((bf16[64,24,256]{2,1,0:T(8,128)(2,1)}), bf16[64,24,256]{2,1,0:T(8,128)(2,1)}, u32[]{:S(2)}, u32[]{:S(2)}) async-start(bf16[64,24,256]{2,1,0:T(8,128)(2,1)} %broadcast_select_fusion.1), calls=%async_computation.5 | async-start | bytes 1572864 | tf_op jit(solution)/shard_map/all_to_all | solution.py:78
  132.6 3.4 multiply_convert_fusion.3
  136.0 3.0 gather_fusion.1
  139.0 3.4 bitcast_reduce_fusion.2
  142.4 2.5 copy.27
  145.0 2.6 fusion.46
  148.6 2.7 multiply_convert_fusion.2
  151.2 3.0 gather_fusion.2
  154.3 3.5 bitcast_reduce_fusion.1
  157.7 2.5 copy.30
  160.2 2.6 fusion.55
  162.9 1.0 copy-done.12
  163.9 2.6 multiply_convert_fusion.1
  167.2 1.3 pad_maximum_fusion
  168.6 18.7 %all_to_all.68 = s32[64,1,24]{2,1,0:T(1,128)S(1)} all-to-all(s32[64,1,24]{2,1,0:T(1,128)S(1)} %bitcast.200), channel_id=1, replica_groups=mesh['dom'=64,'rep'=4] {'dom'}, dimensions={0} | all-to-all | bytes 12288 | tf_op jit(solution)/shard_map/all_to_all | solution.py:81
  187.5 5.4 gather_fusion.7
  192.8 2.4 broadcast_select_fusion
  195.2 6.3 %all-to-all-start.7 = ((bf16[64,24,256]{2,1,0:T(8,128)(2,1)}), bf16[64,24,256]{2,1,0:T(8,128)(2,1)}, u32[]{:S(2)}, u32[]{:S(2)}) async-start(bf16[64,24,256]{2,1,0:T(8,128)(2,1)} %broadcast_select_fusion), calls=%async_computation.7 | async-start | bytes 1572864 | tf_op jit(solution)/shard_map/all_to_all | solution.py:78
  201.8 2.0 gather_fusion.3
  203.8 2.5 bitcast_reduce_fusion
  206.3 1.3 copy.33
  207.6 17.2 %all-to-all-done.7 = bf16[64,24,256]{2,1,0:T(8,128)(2,1)} async-done(((bf16[64,24,256]{2,1,0:T(8,128)(2,1)}), bf16[64,24,256]{2,1,0:T(8,128)(2,1)}, u32[]{:S(2)}, u32[]{:S(2)}) %all-to-all-start.7) | async-done | bytes 786464 | tf_op jit(solution)/shard_map/all_to_all | solution.py:78
  224.8 2.5 fusion.64
  227.3 1.4 multiply_convert_fusion
  228.7 1.6 fusion.67
  230.4 1.0 copy.35
  231.4 1.5 broadcast_in_dim.103
  232.9 2.7 convolution_bitcast_fusion.2
  235.6 5.5 copy.36
  241.1 3.6 fusion.75
  246.7 1.2 fusion.69
  248.7 2.7 convolution_bitcast_fusion.1
  251.4 5.5 copy.39
  256.9 3.6 fusion.74
  262.4 2.0 fusion.71
  264.5 2.1 copy.41
  266.5 1.5 broadcast_in_dim.107
  268.0 2.7 convolution_bitcast_fusion
  270.8 5.7 %copy.42 = f32[32,128,256]{2,0,1:T(8,128)} copy(f32[32,128,256]{1,2,0:T(8,128)} %convolution_bitcast_fusion) | data formatting | bytes 8388608 | tf_op jit(solution)/shard_map/tji,tjw->tiw/dot_general | solution.py:41
  276.5 3.7 fusion.73
  285.4 1.0 pad_maximum_fusion.1
  286.5 252.4 %all-reduce.2.cloned.1.call-done = f32[4,256,256]{2,1,0:T(8,128)} async-done(((f32[4,256,256]{2,1,0:T(8,128)}), f32[4,256,256]{2,1,0:T(8,128)}) %all-reduce.2.cloned.1.call-update) | async-done | bytes 1048592 | tf_op jit(solution)/shard_map/psum | solution.py:125
  539.0 6.0 %copy.50 = bf16[3,4096,256]{2,1,0:T(8,128)(2,1)} copy(bf16[3,4096,256]{2,1,0:T(8,128)(2,1)} %all-gather.2.cloned.1.call-done) | data formatting | bytes 12582912
  544.9 1.0 copy.51
  (102 shorter events, 16.2 us)
Async XLA Ops:
  8.0 66.2 %copy-start = (bf16[32,128,128]{2,1,0:T(8,128)(2,1)S(1)}, bf16[32,128,128]{2,1,0:T(8,128)(2,1)}, u32[]{:S(2)}) copy-start(bf16[32,128,128]{2,1,0:T(8,128)(2,1)} %param.14) | copy-start | bytes 3145732
  9.7 22.2 %all-to-all-start = ((s32[64,1,24]{2,1,0:T(1,128)}), s32[64,1,24]{2,1,0:T(1,128)S(1)}, u32[]{:S(2)}, u32[]{:S(2)}) async-start(s32[64,1,24]{2,1,0:T(1,128)} %bitcast.5), calls=%async_computation | async-start | bytes 65536 | tf_op jit(solution)/shard_map/all_to_all | solution.py:81
  21.7 5.7 %copy-start.18 = (s32[32]{0:T(128)S(1)}, s32[32]{0:T(128)}, u32[]{:S(2)}) copy-start(s32[32]{0:T(128)} %param.15) | copy-start | bytes 388
  31.9 18.9 %all-to-all-start.2 = ((s32[64,1,24]{2,1,0:T(1,128)}), s32[64,1,24]{2,1,0:T(1,128)S(1)}, u32[]{:S(2)}, u32[]{:S(2)}) async-start(s32[64,1,24]{2,1,0:T(1,128)} %bitcast.16), calls=%async_computation.2 | async-start | bytes 65536 | tf_op jit(solution)/shard_map/all_to_all | solution.py:81
  48.7 25.4 %copy-start.19 = (s32[4,64]{1,0:T(4,128)S(1)}, s32[4,64]{1,0:T(4,128)}, u32[]{:S(2)}) copy-start(s32[4,64]{1,0:T(4,128)} %param.17) | copy-start | bytes 3076
  50.8 17.0 %all-to-all-start.4 = ((s32[64,1,24]{2,1,0:T(1,128)}), s32[64,1,24]{2,1,0:T(1,128)S(1)}, u32[]{:S(2)}, u32[]{:S(2)}) async-start(s32[64,1,24]{2,1,0:T(1,128)} %bitcast.27), calls=%async_computation.4 | async-start | bytes 65536 | tf_op jit(solution)/shard_map/all_to_all | solution.py:81
  67.7 29.6 %all-to-all-start.1 = ((bf16[64,24,256]{2,1,0:T(8,128)(2,1)}), bf16[64,24,256]{2,1,0:T(8,128)(2,1)}, u32[]{:S(2)}, u32[]{:S(2)}) async-start(bf16[64,24,256]{2,1,0:T(8,128)(2,1)} %broadcast_select_fusion.3), calls=%async_computation.1 | async-start | bytes 1572864 | tf_op jit(solution)/shard_map/all_to_all | solution.py:78
  86.5 19.9 %copy-start.17 = (s32[4,1536]{1,0:T(4,128)S(1)}, s32[4,1536]{1,0:T(4,128)}, u32[]{:S(2)}) copy-start(s32[4,1536]{1,0:T(4,128)} %param.18) | copy-start | bytes 73732
  86.5 19.9 %copy-start.16 = (bf16[4,1536]{1,0:T(4,128)(2,1)S(1)}, bf16[4,1536]{1,0:T(4,128)(2,1)}, u32[]{:S(2)}) copy-start(bf16[4,1536]{1,0:T(4,128)(2,1)} %param.19) | copy-start | bytes 36868
  97.3 29.1 %all-to-all-start.3 = ((bf16[64,24,256]{2,1,0:T(8,128)(2,1)}), bf16[64,24,256]{2,1,0:T(8,128)(2,1)}, u32[]{:S(2)}, u32[]{:S(2)}) async-start(bf16[64,24,256]{2,1,0:T(8,128)(2,1)} %broadcast_select_fusion.2), calls=%async_computation.3 | async-start | bytes 1572864 | tf_op jit(solution)/shard_map/all_to_all | solution.py:78
  126.4 33.9 %all-to-all-start.5 = ((bf16[64,24,256]{2,1,0:T(8,128)(2,1)}), bf16[64,24,256]{2,1,0:T(8,128)(2,1)}, u32[]{:S(2)}, u32[]{:S(2)}) async-start(bf16[64,24,256]{2,1,0:T(8,128)(2,1)} %broadcast_select_fusion.1), calls=%async_computation.5 | async-start | bytes 1572864 | tf_op jit(solution)/shard_map/all_to_all | solution.py:78
  132.6 154.0 %all-gather.2.cloned.1.call-start = ((), (), s32[]{:S(2)}) async-start(), calls=%async_computation.8 | async-start | bytes 7864320 | tf_op jit(solution)/shard_map/all_gather | solution.py:102
  147.6 1.0 copy-start.10
  162.9 1.0 copy-start.12
  163.9 3.4 copy-start.3
  163.9 3.4 copy-start.4
  166.4 0.8 copy-start.1
  192.8 9.0 %copy-start.2 = (bf16[1024,256]{1,0:T(8,128)(2,1)S(1)}, bf16[1024,256]{1,0:T(8,128)(2,1)}, u32[]{:S(2)}) copy-start(bf16[1024,256]{1,0:T(8,128)(2,1)} %copy-done.1) | copy-start | bytes 1572868
  195.2 29.5 %all-to-all-start.7 = ((bf16[64,24,256]{2,1,0:T(8,128)(2,1)}), bf16[64,24,256]{2,1,0:T(8,128)(2,1)}, u32[]{:S(2)}, u32[]{:S(2)}) async-start(bf16[64,24,256]{2,1,0:T(8,128)(2,1)} %broadcast_select_fusion), calls=%async_computation.7 | async-start | bytes 1572864 | tf_op jit(solution)/shard_map/all_to_all | solution.py:78
  201.5 337.4 %all-reduce.2.cloned.1.call-start = ((), (), s32[]{:S(2)}) async-start(), calls=%async_computation.9 | async-start | bytes 2097152 | tf_op jit(solution)/shard_map/psum | solution.py:125
  206.3 18.5 %copy-start.5 = (bf16[1024,256]{1,0:T(8,128)(2,1)S(1)}, bf16[1024,256]{1,0:T(8,128)(2,1)}, u32[]{:S(2)}) copy-start(bf16[1024,256]{1,0:T(8,128)(2,1)} %param.12) | copy-start | bytes 1572868
  224.7 2.5 copy-start.15
  227.3 3.1 copy-start.22
  227.3 1.4 copy-start.20
  228.7 1.7 copy-start.24
  244.7 1.2 copy-start.7
  260.5 1.2 copy-start.6
  280.2 1.2 copy-start.9
  280.2 1.9 copy-start.8
  281.4 1.3 copy-start.11
  282.1 1.3 copy-start.13
  282.7 1.1 copy-start.21
  282.7 1.5 copy-start.23
  282.7 1.8 copy-start.25
  539.0 6.0 %copy-start.14 = (f32[4,256,256]{2,1,0:T(8,128)S(1)}, f32[4,256,256]{2,1,0:T(8,128)}, u32[]{:S(2)}) copy-start(f32[4,256,256]{2,1,0:T(8,128)} %all-reduce.2.cloned.1.call-done) | copy-start | bytes 3145732
Sparse Core Ops, SparseCore 0:
  168.7 69.4 all-gather.1
Sparse Core Ops, SparseCore 1:
  286.6 252.3 all-reduce.1
where the time goes:
time: 564 us; the launch traced here: 554 us
  waiting for transfers between devices  296 us (52%)
  local copies, waits for them, and re-layouts  92.4 us (16%)
  matrix products  60.1 us (11%)
  starting transfers between devices  55.8 us (10%)
  blocking collectives  18.7 us (3%)
  between operations  16.5 us (3%)
  other arithmetic  14.1 us (2%)
    psum x1, waiting for transfers between devices, body(): weight_grad = lax.psum(local_grads, ('dom', 'rep'))  252 us
    all_to_all x4, waiting for transfers between devices, fetch_layer(): lax.all_to_all(picked, 'dom', split_axis=0, concat_axis=0, tiled=True)  35.5 us
    all_to_all x3, starting transfers between devices, body(): lax.all_to_all(slot_ids[depth], 'dom', split_axis=0, concat_axis=0, tiled...  30.7 us
    all_to_all x4, starting transfers between devices, fetch_layer(): lax.all_to_all(picked, 'dom', split_axis=0, concat_axis=0, tiled=True)  24.8 us
    gather x4, local copies, waits for them, and re-layouts, fetch_layer(): picked = jnp.take(layer_table, portion, axis=0)  24.5 us
    all_to_all x1, blocking collectives, body(): lax.all_to_all(slot_ids[depth], 'dom', split_axis=0, concat_axis=0, tiled...  18.7 us
    dot_general x3, local copies, waits for them, and re-layouts, block_back(): jnp.einsum('tji,tjw->tiw', tiles, spread, preferred_element_type=jnp.floa...  16.7 us
    unnamed x54, local copies, waits for them, and re-layouts  13.7 us
  transfers between devices with their start and end apart: 9, of which 6 were waited for; matrix products, arithmetic and copies ran while one was open for 26% of the time, Pallas kernels for 0%

commit v1 on v0

v1 whole, which is shorter than its diff:
```python
import functools

import jax
import jax.numpy as jnp
from jax import lax
from jax.experimental import pallas as pl
from jax.experimental.pallas import tpu as pltpu
from jax.sharding import PartitionSpec as P

restart_rate = 0.1
beta_table = [
    0.4054651081081644,
    0.22314355131420976,
    0.15415067982725836,
    0.11778303565638346,
    0.09531017980432493,
    0.08004270767353637,
    0.06899287148695142,
    0.06062462181643484,
]
f32 = jnp.float32
bf16 = jnp.bfloat16
gelu_c = 0.7978845608028654
gelu_k = 0.044715
vmem_limit = 40 * 1024 * 1024
VMEM = pl.BlockSpec(memory_space=pltpu.VMEM)
SMEM = pl.BlockSpec(memory_space=pltpu.SMEM)
ANY = pl.BlockSpec(memory_space=pl.ANY)


def forward_kernel(beta, cols, hidden, tiles, pulled, dst, wt, features, weight, support_o, slope_o, hidden_o):
    slots = pulled.shape[0]
    row_count = features.shape[0]
    step = 256
    per_block = tiles.shape[0] // (row_count // 128)
    dst_row = dst[...]
    wt_row = wt[...]
    for chunk in range(row_count // step):
        lo = chunk * step
        position = lax.broadcasted_iota(jnp.int32, (step, slots), 0) + lo
        scatter = jnp.where(dst_row == position, wt_row, 0.0).astype(bf16)
        acc = jnp.dot(scatter, pulled[...], preferred_element_type=f32)
        parts = []
        for block in range(lo // 128, (lo + step) // 128):
            picked = jnp.concatenate(
                [
                    hidden[pl.ds(pl.multiple_of(cols[block * per_block + k] * 128, 128), 128), :]
                    for k in range(per_block)
                ],
                axis=0,
            )
            tile_row = jnp.concatenate([tiles[block * per_block + k] for k in range(per_block)], axis=1)
            parts.append(jnp.dot(tile_row, picked, preferred_element_type=f32))
        acc = acc + jnp.concatenate(parts, axis=0)
        support = (1.0 - restart_rate) * acc + restart_rate * features[lo : lo + step, :].astype(f32)
        support_bf = support.astype(bf16)
        support_o[lo : lo + step, :] = support_bf
        pre = (1.0 - beta) * support + beta * jnp.dot(support_bf, weight[...], preferred_element_type=f32)
        square = pre * pre
        th = jnp.tanh(gelu_c * (pre + gelu_k * pre * square))
        half = 0.5 * (1.0 + th)
        hidden_o[lo : lo + step, :] = (pre * half).astype(bf16)
        slope_o[lo : lo + step, :] = half + 0.5 * pre * (1.0 - th * th) * (
            gelu_c * (1.0 + 3.0 * gelu_k * square)
        )


def forward_layer(beta, cols, hidden, tiles, pulled, dst, wt, features, weight):
    rows, width = features.shape
    return pl.pallas_call(
        functools.partial(forward_kernel, beta),
        out_shape=(
            jax.ShapeDtypeStruct((rows, width), bf16),
            jax.ShapeDtypeStruct((rows, width), f32),
            jax.ShapeDtypeStruct((rows, width), bf16),
        ),
        in_specs=[SMEM] + [VMEM] * 7,
        out_specs=(VMEM, VMEM, VMEM),
        compiler_params=pltpu.CompilerParams(vmem_limit_bytes=vmem_limit),
        cost_estimate=pl.CostEstimate(flops=1_300_000_000, bytes_accessed=6_000_000, transcendentals=262144),
    )(cols, hidden, tiles, pulled, dst, wt, features, weight)


def backward_kernel(cols, cot, tiles_t, weights, *rest):
    layer_count = weights.shape[0]
    supports = rest[:layer_count]
    slopes = rest[layer_count : 2 * layer_count]
    grads_o, total, grad_bf, gs_bf = rest[2 * layer_count :]
    row_count, width = cot.shape
    step = 256
    per_block = tiles_t.shape[0] // (row_count // 128)
    for depth in range(layer_count - 1, -1, -1):
        beta = beta_table[depth]
        weight = weights[depth]
        for chunk in range(row_count // step):
            lo = chunk * step
            if depth == layer_count - 1:
                grad_out = cot[lo : lo + step, :].astype(f32)
            else:
                grad_out = ((1.0 - restart_rate) * total[lo : lo + step, :]).astype(bf16).astype(f32)
            gp = grad_out * slopes[depth][lo : lo + step, :]
            gp_bf = gp.astype(bf16)
            grad_bf[lo : lo + step, :] = gp_bf
            if depth > 0:
                gs = (1.0 - beta) * gp + beta * lax.dot_general(
                    gp_bf, weight, (((1,), (1,)), ((), ())), preferred_element_type=f32
                )
                gs_bf[lo : lo + step, :] = gs.astype(bf16)
        grads_o[depth] = (
            beta
            * lax.dot_general(
                supports[depth][...], grad_bf[...], (((0,), (0,)), ((), ())), preferred_element_type=f32
            )
        ).astype(bf16)
        if depth > 0:
            total[...] = jnp.zeros_like(total)
            for block in range(row_count // 128):
                tile_col = jnp.concatenate(
                    [tiles_t[block * per_block + k] for k in range(per_block)], axis=0
                )
                product = jnp.dot(
                    tile_col, gs_bf[block * 128 : (block + 1) * 128, :], preferred_element_type=f32
                )
                for k in range(per_block):
                    at = pl.ds(pl.multiple_of(cols[block * per_block + k] * 128, 128), 128)
                    total[at, :] = total[at, :] + product[k * 128 : (k + 1) * 128, :]


def backward(cols, cot, tiles_t, weights, supports, slopes):
    layer_count, width, _ = weights.shape
    rows = cot.shape[0]
    return pl.pallas_call(
        backward_kernel,
        out_shape=jax.ShapeDtypeStruct((layer_count, width, width), bf16),
        in_specs=[SMEM] + [VMEM] * (3 + 2 * layer_count),
        out_specs=VMEM,
        scratch_shapes=[
            pltpu.VMEM((rows, width), f32),
            pltpu.VMEM((rows, width), bf16),
            pltpu.VMEM((rows, width), bf16),
        ],
        compiler_params=pltpu.CompilerParams(vmem_limit_bytes=vmem_limit),
        cost_estimate=pl.CostEstimate(flops=2_000_000_000, bytes_accessed=9_000_000, transcendentals=0),
    )(cols, cot, tiles_t, weights, *supports, *slopes)


def assemble_kernel(replicas, *rest):
    out, sems = rest[-2:]
    pieces = rest[:-2]
    me = lax.axis_index("rep")
    rows = pieces[0].shape[0]
    copies = []
    for i, piece in enumerate(pieces):
        layer, behind = divmod(i, replicas)
        at = lax.rem(me + replicas - behind, replicas) * rows
        copies.append(
            pltpu.make_async_copy(piece, out.at[layer, pl.ds(pl.multiple_of(at, 128), rows), :], sems.at[i])
        )
    for copy in copies:
        copy.start()
    for copy in copies:
        copy.wait()


def assemble(replicas, pieces):
    layers = len(pieces) // replicas
    rows, width = pieces[0].shape
    return pl.pallas_call(
        functools.partial(assemble_kernel, replicas),
        out_shape=jax.ShapeDtypeStruct((layers, replicas * rows, width), bf16),
        in_specs=[ANY] * len(pieces),
        out_specs=ANY,
        scratch_shapes=[pltpu.SemaphoreType.DMA((len(pieces),))],
        cost_estimate=pl.CostEstimate(flops=0, bytes_accessed=12_600_000, transcendentals=0),
    )(*pieces)


def exchange(value, axis):
    return lax.all_to_all(value, axis, split_axis=0, concat_axis=0, tiled=True)


def body(
    features,
    history,
    tiles,
    tile_cols,
    halo_ids,
    halo_counts,
    halo_dst,
    halo_wt,
    weights,
    cotangent,
):
    row_count, width = features.shape
    layer_count = weights.shape[0]
    parts = lax.axis_size("dom")
    replicas = lax.axis_size("rep")
    slot_count = halo_ids.shape[1]
    capacity = slot_count // parts
    slab = history.shape[1]

    wanted = halo_ids.reshape(layer_count, parts, capacity).transpose(1, 0, 2)
    wanted = exchange(wanted.reshape(parts, layer_count * capacity), "dom")
    wanted = wanted.reshape(parts, layer_count, capacity)
    first = history[0].at[wanted[:, 0].reshape(-1)].get(mode="promise_in_bounds")
    first = exchange(first.reshape(parts, capacity, width), "dom")
    shift = (jnp.arange(layer_count, dtype=jnp.int32) * slab)[None, 1:, None]
    later = history.reshape(layer_count * slab, width).at[(wanted[:, 1:] + shift).reshape(-1)].get(
        mode="promise_in_bounds"
    )
    later = exchange(later.reshape(parts, (layer_count - 1) * capacity, width), "dom")
    later = later.reshape(parts, layer_count - 1, capacity, width).transpose(1, 0, 2, 3)
    later = later.reshape(layer_count - 1, slot_count, width)
    pulled = [first.reshape(slot_count, width)] + [later[i] for i in range(layer_count - 1)]

    rank = jnp.arange(capacity, dtype=jnp.int32)
    live = rank[None, None, :] < halo_counts[:, :, None]
    slot_wt = jnp.where(live.reshape(layer_count, slot_count), halo_wt.astype(f32), 0.0)
    tiles_t = tiles.transpose(0, 2, 1)

    hidden = features
    supports, slopes, pieces = [], [], []
    for depth in range(layer_count):
        support_bf, slope, hidden = forward_layer(
            beta_table[depth],
            tile_cols,
            hidden,
            tiles,
            pulled[depth],
            halo_dst[depth][None, :],
            slot_wt[depth][None, :],
            features,
            weights[depth],
        )
        supports.append(support_bf)
        slopes.append(slope)
        if depth + 1 < layer_count:
            pieces.append(hidden)
            for k in range(1, replicas):
                pieces.append(lax.ppermute(hidden, "rep", [(i, (i + k) % replicas) for i in range(replicas)]))
    grads = backward(tile_cols, cotangent, tiles_t, weights, supports, slopes)
    chunk = layer_count * width // parts
    mine = exchange(grads.reshape(parts, chunk, width), "dom").astype(f32).sum(axis=0)
    mine = exchange(jnp.broadcast_to(mine[None], (replicas, chunk, width)), "rep").sum(axis=0)
    whole = exchange(jnp.broadcast_to(mine.astype(bf16)[None], (parts, chunk, width)), "dom")
    weight_grad = whole.astype(f32).reshape(layer_count, width, width)
    new_history = assemble(replicas, pieces)
    return (hidden, new_history, weight_grad)


def solution(mesh):
    in_specs = (
        P(("dom", "rep"), None),
        P(None, "dom", None),
        P(("dom", "rep"), None, None),
        P(("dom", "rep")),
        P(None, ("dom", "rep")),
        P(None, ("dom", "rep")),
        P(None, ("dom", "rep")),
        P(None, ("dom", "rep")),
        P(),
        P(("dom", "rep"), None),
    )
    out_specs = (P(("dom", "rep"), None), P(None, "dom", None), P())
    return jax.shard_map(body, mesh=mesh, in_specs=in_specs, out_specs=out_specs, check_vma=False)
```

time: 564 us -> 433 us (0.77); the launches traced: 554 us -> 432 us
  Pallas kernels: 0 us -> 210 us
  waiting for transfers between devices: 296 us -> 113 us
  matrix products: 60.1 us -> 0 us
  local copies, waits for them, and re-layouts: 92.4 us -> 38.9 us
  between operations: 16.5 us -> 1.05 us
  other arithmetic: 14.1 us -> 2.11 us
  starting transfers between devices: 55.8 us -> 44.7 us
    psum x1 -> x0, waiting for transfers between devices: 252 us -> none  [body(): weight_grad = lax.psum(local_grads, ('dom', 'rep'))]
    pallas_call x0 -> x6, Pallas kernels: none -> 210 us  [the longest x1 192 us: assemble(): pl.pallas_call(functools.partial(assemble_kernel, replicas), out_shape=ja...]
    dot_general x25 -> x0, matrix products: 60.1 us -> none  [the longest x4 12.8 us: block_sum(): jnp.einsum('tij,tjw->tiw', tiles, gathered, preferred_element_type=jnp.fl...]
    ppermute x0 -> x9, waiting for transfers between devices: none -> 55.1 us  [body(): lax.ppermute(hidden, 'rep', [(i, (i + k) % replicas) for i in range(repli...]
    all_to_all x7 -> x5, starting transfers between devices: 55.5 us -> 34 us  [exchange(): return lax.all_to_all(value, axis, split_axis=0, concat_axis=0, tiled=True)]
    dot_general x3 -> x0, local copies, waits for them, and re-layouts: 16.7 us -> none  [block_back(): jnp.einsum('tji,tjw->tiw', tiles, spread, preferred_element_type=jnp.floa...]
    gather x8 -> x2, local copies, waits for them, and re-layouts: 35.6 us -> 21.2 us  [the longest x1 15.9 us: body(): history.reshape(layer_count * slab, width)]
    all_to_all x7 -> x5, waiting for transfers between devices: 43.8 us -> 57.4 us  [exchange(): return lax.all_to_all(value, axis, split_axis=0, concat_axis=0, tiled=True)]
  transfers between devices with their start and end apart: 9 -> 14, of which waited for: 6 -> 9; matrix products, arithmetic and copies ran while one was open for 26% -> 6% of each run, Pallas kernels for 0% -> 45%
where the time goes in v1:
time: 433 us; the launch traced here: 432 us
  Pallas kernels  210 us (48%)
  waiting for transfers between devices  113 us (26%)
  starting transfers between devices  44.7 us (10%)
  local copies, waits for them, and re-layouts  38.9 us (9%)
  blocking collectives  22.9 us (5%)
    pallas_call x1, Pallas kernels, assemble(): pl.pallas_call(functools.partial(assemble_kernel, replicas), out_shape=ja...  192 us
    all_to_all x5, waiting for transfers between devices, exchange(): return lax.all_to_all(value, axis, split_axis=0, concat_axis=0, tiled=True)  57.4 us
    ppermute x9, waiting for transfers between devices, body(): lax.ppermute(hidden, 'rep', [(i, (i + k) % replicas) for i in range(repli...  55.1 us
    all_to_all x5, starting transfers between devices, exchange(): return lax.all_to_all(value, axis, split_axis=0, concat_axis=0, tiled=True)  34 us
    all_to_all x1, blocking collectives, exchange(): return lax.all_to_all(value, axis, split_axis=0, concat_axis=0, tiled=True)  22.9 us
    gather x1, local copies, waits for them, and re-layouts, body(): history.reshape(layer_count * slab, width)  15.9 us
    pallas_call x4, Pallas kernels, forward_layer(): pl.pallas_call(functools.partial(forward_kernel, beta), out_shape=(jax.Sh...  13.5 us
    ppermute x9, starting transfers between devices, body(): lax.ppermute(hidden, 'rep', [(i, (i + k) % replicas) for i in range(repli...  10.7 us
  transfers between devices with their start and end apart: 14, of which 9 were waited for; matrix products, arithmetic and copies ran while one was open for 6% of the time, Pallas kernels for 45%

profile of v1, /device:TPU:2, one launch (start us, length us, event | category | flops | bytes accessed | tf_op | source)
XLA Modules:
  0.0 432.4 jit_solution(11360831634944941001)
XLA Ops:
  0.6 0.8 reshape.116
  1.5 0.1 copy.24
  1.6 0.7 copy.25
  2.3 12.0 %all-to-all-start = ((s32[64,1,96]{2,1,0:T(1,128)}), s32[64,1,96]{2,1,0:T(1,128)S(1)}, u32[]{:S(2)}, u32[]{:S(2)}) async-start(s32[64,1,96]{2,1,0:T(1,128)} %copy.25), calls=%async_computation | async-start | bytes 65536 | tf_op jit(solution)/shard_map/all_to_all | solution.py:179
  14.3 1.7 slice_bitcast_fusion
  16.0 6.8 %all-to-all-done = s32[64,1,96]{2,1,0:T(1,128)S(1)} async-done(((s32[64,1,96]{2,1,0:T(1,128)}), s32[64,1,96]{2,1,0:T(1,128)S(1)}, u32[]{:S(2)}, u32[]{:S(2)}) %all-to-all-start) | async-done | bytes 24608 | tf_op jit(solution)/shard_map/all_to_all | solution.py:179
  22.8 0.1 copy.26
  22.9 0.1 copy.27
  23.0 0.1 reshape_squeeze.3
  23.2 5.4 %gather_fusion = bf16[1536,256]{1,0:T(8,128)(2,1)} fusion(bf16[4096,256]{1,0:T(8,128)(2,1)S(1)} %slice_bitcast_fusion, s32[2048]{0:T(1024)S(1)} %pad_clamp_fusion.1), kind=kCustom, calls=%fused_computation | custom fusion | bytes 1579008 | tf_op jit(solution)/shard_map/gather | solution.py:205
  28.5 5.5 %all-to-all-start.1 = ((bf16[64,24,256]{2,1,0:T(8,128)(2,1)}), bf16[64,24,256]{2,1,0:T(8,128)(2,1)S(1)}, u32[]{:S(2)}, u32[]{:S(2)}) async-start(bf16[64,24,256]{2,1,0:T(8,128)(2,1)} %bitcast.39), calls=%async_computation.1 | async-start | bytes 1572864 | tf_op jit(solution)/shard_map/all_to_all | solution.py:179
  34.1 0.1 slice.66
  34.1 0.1 slice_add_fusion
  34.2 0.1 copy.28
  34.3 0.2 reshape.121
  34.5 0.1 fusion
  34.6 15.9 %gather_fusion.1 = bf16[4608,256]{1,0:T(8,128)(2,1)} fusion(bf16[16384,256]{1,0:T(8,128)(2,1)} %bitcast.37, s32[5120]{0:T(1024)S(1)} %pad_clamp_fusion), kind=kCustom, calls=%fused_computation.1 | custom fusion | bytes 4737024 | tf_op jit(solution)/shard_map/gather | solution.py:208
  50.4 6.9 %all-to-all-done.1 = bf16[64,24,256]{2,1,0:T(8,128)(2,1)S(1)} async-done(((bf16[64,24,256]{2,1,0:T(8,128)(2,1)}), bf16[64,24,256]{2,1,0:T(8,128)(2,1)S(1)}, u32[]{:S(2)}, u32[]{:S(2)}) %all-to-all-start.1) | async-done | bytes 786464 | tf_op jit(solution)/shard_map/all_to_all | solution.py:179
  57.3 6.1 %all-to-all-start.2 = ((bf16[64,72,256]{2,1,0:T(8,128)(2,1)}), bf16[64,72,256]{2,1,0:T(8,128)(2,1)}, u32[]{:S(2)}, u32[]{:S(2)}) async-start(bf16[64,72,256]{2,1,0:T(8,128)(2,1)} %bitcast.38), calls=%async_computation.2 | async-start | bytes 4718592 | tf_op jit(solution)/shard_map/all_to_all | solution.py:179
  63.5 0.1 lt.51
  63.6 0.7 lt.52
  64.3 0.1 lt.49
  64.4 0.8 copy.29
  65.3 0.7 slice_bitcast_fusion.1
  66.0 0.8 convert_select_fusion
  66.8 0.6 fusion.3
  67.4 1.5 fusion.4
  68.9 1.2 copy-done.2
  70.1 0.7 copy-done.19
  70.8 1.0 copy-done.21
  71.8 3.2 shard_map.121
  75.0 0.8 copy-done.5
  75.8 0.8 copy-done.11
  76.6 43.7 %all-to-all-done.2 = bf16[64,72,256]{2,1,0:T(8,128)(2,1)} async-done(((bf16[64,72,256]{2,1,0:T(8,128)(2,1)}), bf16[64,72,256]{2,1,0:T(8,128)(2,1)}, u32[]{:S(2)}, u32[]{:S(2)}) %all-to-all-start.2) | async-done | bytes 2359328 | tf_op jit(solution)/shard_map/all_to_all | solution.py:179
  120.3 1.9 fusion.2
  122.3 0.1 copy-done.6
  122.4 0.0 copy-done.14
  122.4 0.2 copy-done.22
  122.6 3.2 shard_map.122
  125.9 3.2 shard_map.123
  129.1 4.0 shard_map.124
  133.1 4.9 %shard_map.126 = bf16[4,256,256]{2,1,0:T(8,128)(2,1)S(1)} custom-call(s32[32]{0:T(128)S(1)} %copy-done.20, bf16[1024,256]{1,0:T(8,128)(2,1)S(1)} %copy-done.4, bf16[32,128,128]{2,1,0:T(8,128)(2,1)S(1)} %bitcast.31, bf16[4,256,256]{2,1,0:T(8,128)(2,1)S(1)} %copy-done, bf16[1024,256]{1,0:T(8,128)(2,1)S(1)} %copy-done.12, ...), custom_call_target="tpu_custom_call" | custom-call | flops 2000000000 | bytes 9000000 | tf_op jit(solution)/shard_map/pallas_call | solution.py:132
  138.0 22.9 %all_to_all.34 = bf16[64,16,256]{2,1,0:T(8,128)(2,1)S(1)} all-to-all(bf16[64,16,256]{2,1,0:T(8,128)(2,1)S(1)} %bitcast.32), channel_id=1, replica_groups=mesh['dom'=64,'rep'=4] {'dom'}, dimensions={0} | all-to-all | bytes 1048576 | tf_op jit(solution)/shard_map/all_to_all | solution.py:179
  161.0 0.1 convert_reduce_fusion
  161.1 0.6 broadcast_in_dim.9
  161.7 4.5 %all-to-all-start.4 = ((f32[4,16,256]{2,1,0:T(8,128)}), f32[4,16,256]{2,1,0:T(8,128)S(1)}, u32[]{:S(2)}, u32[]{:S(2)}) async-start(f32[4,16,256]{2,1,0:T(8,128)} %broadcast_in_dim.9), calls=%async_computation.4 | async-start | bytes 131072 | tf_op jit(solution)/shard_map/all_to_all | solution.py:179
  166.2 2.0 collective-permute-start
  168.2 2.7 collective-permute-start.1
  170.9 1.5 collective-permute-start.2
  172.3 0.6 collective-permute-start.6
  172.9 0.8 broadcast_in_dim.10
  173.7 5.9 %all-to-all-start.5 = ((bf16[64,16,256]{2,1,0:T(8,128)(2,1)}), bf16[64,16,256]{2,1,0:T(8,128)(2,1)S(1)}, u32[]{:S(2)}, u32[]{:S(2)}) async-start(bf16[64,16,256]{2,1,0:T(8,128)(2,1)} %broadcast_in_dim.10), calls=%async_computation.5 | async-start | bytes 1048576 | tf_op jit(solution)/shard_map/all_to_all | solution.py:179
  179.6 1.0 collective-permute-start.7
  180.6 12.7 %collective-permute-done.rest_1_ = bf16[1024,256]{1,0:T(8,128)(2,1)S(1)} collective-permute-done((bf16[1024,256]{1,0:T(8,128)(2,1)S(1)}, bf16[1024,256]{1,0:T(8,128)(2,1)S(1)}, u32[]{:S(2)}, u32[]{:S(2)}) %collective-permute-start) | collective-permute-done | bytes 524320 | tf_op jit(solution)/shard_map/ppermute | solution.py:240
  193.4 1.6 collective-permute-done.1.rest_2_
  195.0 0.5 collective-permute-start.3
  195.5 2.5 collective-permute-start.4
  198.0 17.9 %collective-permute-done.6.rest_9_ = bf16[1024,256]{1,0:T(8,128)(2,1)} collective-permute-done((bf16[1024,256]{1,0:T(8,128)(2,1)}, bf16[1024,256]{1,0:T(8,128)(2,1)}, u32[]{:S(2)}, u32[]{:S(2)}) %collective-permute-start.6) | collective-permute-done | bytes 524320 | tf_op jit(solution)/shard_map/ppermute | solution.py:240
  215.9 1.6 collective-permute-done.7.rest_10_
  217.5 9.8 %collective-permute-done.3.rest_5_ = bf16[1024,256]{1,0:T(8,128)(2,1)S(1)} collective-permute-done((bf16[1024,256]{1,0:T(8,128)(2,1)S(1)}, bf16[1024,256]{1,0:T(8,128)(2,1)S(1)}, u32[]{:S(2)}, u32[]{:S(2)}) %collective-permute-start.3) | collective-permute-done | bytes 524320 | tf_op jit(solution)/shard_map/ppermute | solution.py:240
  227.3 11.4 %collective-permute-done.4.rest_6_ = bf16[1024,256]{1,0:T(8,128)(2,1)S(1)} collective-permute-done((bf16[1024,256]{1,0:T(8,128)(2,1)S(1)}, bf16[1024,256]{1,0:T(8,128)(2,1)S(1)}, u32[]{:S(2)}, u32[]{:S(2)}) %collective-permute-start.4) | collective-permute-done | bytes 524320 | tf_op jit(solution)/shard_map/ppermute | solution.py:240
  238.8 0.8 copy-done.28
  239.5 191.8 %shard_map.125 = bf16[3,4096,256]{2,1,0:T(8,128)(2,1)} custom-call(bf16[1024,256]{1,0:T(8,128)(2,1)} %copy-done.5, bf16[1024,256]{1,0:T(8,128)(2,1)} %copy-done.23, bf16[1024,256]{1,0:T(8,128)(2,1)} %copy-done.24, bf16[1024,256]{1,0:T(8,128)(2,1)} %collective-permute-done.2.rest_3_, bf16[1024,256]{1,0:T(8,128)(2,1)} %copy-done.7, ...), custom_call_target="tpu_custom_call" | custom-call | bytes 12600000 | tf_op jit(solution)/shard_map/pallas_call | solution.py:168
  431.4 1.1 bitcast_convert_fusion
  (65 shorter events, 0.2 us)
Async XLA Ops:
  2.3 20.5 %all-to-all-start = ((s32[64,1,96]{2,1,0:T(1,128)}), s32[64,1,96]{2,1,0:T(1,128)S(1)}, u32[]{:S(2)}, u32[]{:S(2)}) async-start(s32[64,1,96]{2,1,0:T(1,128)} %copy.25), calls=%async_computation | async-start | bytes 65536 | tf_op jit(solution)/shard_map/all_to_all | solution.py:179
  28.5 28.8 %all-to-all-start.1 = ((bf16[64,24,256]{2,1,0:T(8,128)(2,1)}), bf16[64,24,256]{2,1,0:T(8,128)(2,1)S(1)}, u32[]{:S(2)}, u32[]{:S(2)}) async-start(bf16[64,24,256]{2,1,0:T(8,128)(2,1)} %bitcast.39), calls=%async_computation.1 | async-start | bytes 1572864 | tf_op jit(solution)/shard_map/all_to_all | solution.py:179
  57.3 6.1 %copy-start.29 = (s32[4,64]{1,0:T(4,128)S(1)}, s32[4,64]{1,0:T(4,128)}, u32[]{:S(2)}) copy-start(s32[4,64]{1,0:T(4,128)} %param.15) | copy-start | bytes 3076
  57.3 7.1 %copy-start.1 = (bf16[32,128,128]{2,1,0:T(8,128)(2,1)S(1)}, bf16[32,128,128]{2,1,0:T(8,128)(2,1)}, u32[]{:S(2)}) copy-start(bf16[32,128,128]{2,1,0:T(8,128)(2,1)} %tiles.7) | copy-start | bytes 3145732
  57.3 62.9 %all-to-all-start.2 = ((bf16[64,72,256]{2,1,0:T(8,128)(2,1)}), bf16[64,72,256]{2,1,0:T(8,128)(2,1)}, u32[]{:S(2)}, u32[]{:S(2)}) async-start(bf16[64,72,256]{2,1,0:T(8,128)(2,1)} %bitcast.38), calls=%async_computation.2 | async-start | bytes 4718592 | tf_op jit(solution)/shard_map/all_to_all | solution.py:179
  63.5 1.8 copy-start
  68.9 1.2 copy-start.2
  70.1 0.7 copy-start.19
  70.8 1.0 copy-start.21
  75.0 0.8 copy-start.5
  75.8 0.8 copy-start.11
  120.3 2.0 copy-start.3
  120.3 2.1 copy-start.6
  120.3 2.1 copy-start.14
  120.3 2.1 copy-start.17
  120.3 2.1 copy-start.18
  120.3 2.1 copy-start.20
  120.3 2.3 copy-start.22
  122.6 3.2 copy-start.13
  122.6 3.2 copy-start.15
  122.6 3.2 copy-start.16
  125.8 3.2 copy-start.7
  129.1 4.0 copy-start.9
  129.1 4.0 copy-start.4
  129.1 4.0 copy-start.12
  138.0 41.6 %copy-start.10 = (bf16[1024,256]{1,0:T(8,128)(2,1)S(1)}, bf16[1024,256]{1,0:T(8,128)(2,1)}, u32[]{:S(2)}) copy-start(bf16[1024,256]{1,0:T(8,128)(2,1)} %copy-done.9) | copy-start | bytes 1572868
  138.0 57.0 %copy-start.8 = (bf16[1024,256]{1,0:T(8,128)(2,1)S(1)}, bf16[1024,256]{1,0:T(8,128)(2,1)}, u32[]{:S(2)}) copy-start(bf16[1024,256]{1,0:T(8,128)(2,1)} %copy-done.7) | copy-start | bytes 1572868
  161.7 11.2 %all-to-all-start.4 = ((f32[4,16,256]{2,1,0:T(8,128)}), f32[4,16,256]{2,1,0:T(8,128)S(1)}, u32[]{:S(2)}, u32[]{:S(2)}) async-start(f32[4,16,256]{2,1,0:T(8,128)} %broadcast_in_dim.9), calls=%async_computation.4 | async-start | bytes 131072 | tf_op jit(solution)/shard_map/all_to_all | solution.py:179
  166.2 27.2 %collective-permute-start = (bf16[1024,256]{1,0:T(8,128)(2,1)S(1)}, bf16[1024,256]{1,0:T(8,128)(2,1)S(1)}, u32[]{:S(2)}, u32[]{:S(2)}) collective-permute-start(bf16[1024,256]{1,0:T(8,128)(2,1)S(1)} %copy-done.6), channel_id=1, source_target_pairs={{0,1},{1,2},{2,3},{3,0},{4,5},{5,6},{6,7},{7,4},{8,9},{9,10},{10,1... | collective-permute-start | bytes 1572872 | tf_op jit(solution)/shard_map/ppermute | solution.py:240
  168.2 26.8 %collective-permute-start.1 = (bf16[1024,256]{1,0:T(8,128)(2,1)S(1)}, bf16[1024,256]{1,0:T(8,128)(2,1)S(1)}, u32[]{:S(2)}, u32[]{:S(2)}) collective-permute-start(bf16[1024,256]{1,0:T(8,128)(2,1)S(1)} %copy-done.6), channel_id=1, source_target_pairs={{0,2},{1,3},{2,0},{3,1},{4,6},{5,7},{6,4},{7,5},{8,10},{9,11},{10,... | collective-permute-start | bytes 1572872 | tf_op jit(solution)/shard_map/ppermute | solution.py:240
  170.9 24.6 %collective-permute-start.2 = (bf16[1024,256]{1,0:T(8,128)(2,1)S(1)}, bf16[1024,256]{1,0:T(8,128)(2,1)}, u32[]{:S(2)}, u32[]{:S(2)}) collective-permute-start(bf16[1024,256]{1,0:T(8,128)(2,1)S(1)} %copy-done.6), channel_id=1, source_target_pairs={{0,3},{1,0},{2,1},{3,2},{4,7},{5,4},{6,5},{7,6},{8,11},{9,8},{10,9... | collective-permute-start | bytes 1572872 | tf_op jit(solution)/shard_map/ppermute | solution.py:240
  172.3 43.6 %collective-permute-start.6 = (bf16[1024,256]{1,0:T(8,128)(2,1)}, bf16[1024,256]{1,0:T(8,128)(2,1)}, u32[]{:S(2)}, u32[]{:S(2)}) collective-permute-start(bf16[1024,256]{1,0:T(8,128)(2,1)} %copy-done.9), channel_id=1, source_target_pairs={{0,1},{1,2},{2,3},{3,0},{4,5},{5,6},{6,7},{7,4},{8,9},{9,10},{10,1... | collective-permute-start | bytes 1572872 | tf_op jit(solution)/shard_map/ppermute | solution.py:240
  173.7 257.6 %all-to-all-start.5 = ((bf16[64,16,256]{2,1,0:T(8,128)(2,1)}), bf16[64,16,256]{2,1,0:T(8,128)(2,1)S(1)}, u32[]{:S(2)}, u32[]{:S(2)}) async-start(bf16[64,16,256]{2,1,0:T(8,128)(2,1)} %broadcast_in_dim.10), calls=%async_computation.5 | async-start | bytes 1048576 | tf_op jit(solution)/shard_map/all_to_all | solution.py:179
  179.6 37.9 %collective-permute-start.7 = (bf16[1024,256]{1,0:T(8,128)(2,1)S(1)}, bf16[1024,256]{1,0:T(8,128)(2,1)S(1)}, u32[]{:S(2)}, u32[]{:S(2)}) collective-permute-start(bf16[1024,256]{1,0:T(8,128)(2,1)S(1)} %copy-done.10), channel_id=1, source_target_pairs={{0,2},{1,3},{2,0},{3,1},{4,6},{5,7},{6,4},{7,5},{8,10},{9,11},{10,... | collective-permute-start | bytes 1572872 | tf_op jit(solution)/shard_map/ppermute | solution.py:240
  193.4 45.4 %copy-start.23 = (bf16[1024,256]{1,0:T(8,128)(2,1)}, bf16[1024,256]{1,0:T(8,128)(2,1)S(1)}, u32[]{:S(2)}) copy-start(bf16[1024,256]{1,0:T(8,128)(2,1)S(1)} %collective-permute-done.rest_1_) | copy-start | bytes 1572868
  193.4 24.1 %collective-permute-start.8 = (bf16[1024,256]{1,0:T(8,128)(2,1)S(1)}, bf16[1024,256]{1,0:T(8,128)(2,1)S(1)}, u32[]{:S(2)}, u32[]{:S(2)}) collective-permute-start(bf16[1024,256]{1,0:T(8,128)(2,1)S(1)} %copy-done.10), channel_id=1, source_target_pairs={{0,3},{1,0},{2,1},{3,2},{4,7},{5,4},{6,5},{7,6},{8,11},{9,8},{10,9... | collective-permute-start | bytes 1572872 | tf_op jit(solution)/shard_map/ppermute | solution.py:240
  195.0 43.8 %copy-start.24 = (bf16[1024,256]{1,0:T(8,128)(2,1)}, bf16[1024,256]{1,0:T(8,128)(2,1)S(1)}, u32[]{:S(2)}) copy-start(bf16[1024,256]{1,0:T(8,128)(2,1)S(1)} %collective-permute-done.1.rest_2_) | copy-start | bytes 1572868
  195.0 32.3 %collective-permute-start.3 = (bf16[1024,256]{1,0:T(8,128)(2,1)S(1)}, bf16[1024,256]{1,0:T(8,128)(2,1)S(1)}, u32[]{:S(2)}, u32[]{:S(2)}) collective-permute-start(bf16[1024,256]{1,0:T(8,128)(2,1)S(1)} %copy-done.8), channel_id=1, source_target_pairs={{0,1},{1,2},{2,3},{3,0},{4,5},{5,6},{6,7},{7,4},{8,9},{9,10},{10,1... | collective-permute-start | bytes 1572872 | tf_op jit(solution)/shard_map/ppermute | solution.py:240
  195.5 43.3 %collective-permute-start.4 = (bf16[1024,256]{1,0:T(8,128)(2,1)S(1)}, bf16[1024,256]{1,0:T(8,128)(2,1)S(1)}, u32[]{:S(2)}, u32[]{:S(2)}) collective-permute-start(bf16[1024,256]{1,0:T(8,128)(2,1)S(1)} %copy-done.8), channel_id=1, source_target_pairs={{0,2},{1,3},{2,0},{3,1},{4,6},{5,7},{6,4},{7,5},{8,10},{9,11},{10,... | collective-permute-start | bytes 1572872 | tf_op jit(solution)/shard_map/ppermute | solution.py:240
  215.9 22.9 %collective-permute-start.5 = (bf16[1024,256]{1,0:T(8,128)(2,1)S(1)}, bf16[1024,256]{1,0:T(8,128)(2,1)}, u32[]{:S(2)}, u32[]{:S(2)}) collective-permute-start(bf16[1024,256]{1,0:T(8,128)(2,1)S(1)} %copy-done.8), channel_id=1, source_target_pairs={{0,3},{1,0},{2,1},{3,2},{4,7},{5,4},{6,5},{7,6},{8,11},{9,8},{10,9... | collective-permute-start | bytes 1572872 | tf_op jit(solution)/shard_map/ppermute | solution.py:240
  217.5 21.2 %copy-start.25 = (bf16[1024,256]{1,0:T(8,128)(2,1)}, bf16[1024,256]{1,0:T(8,128)(2,1)S(1)}, u32[]{:S(2)}) copy-start(bf16[1024,256]{1,0:T(8,128)(2,1)S(1)} %collective-permute-done.7.rest_10_) | copy-start | bytes 1572868
  217.5 21.2 %copy-start.26 = (bf16[1024,256]{1,0:T(8,128)(2,1)}, bf16[1024,256]{1,0:T(8,128)(2,1)S(1)}, u32[]{:S(2)}) copy-start(bf16[1024,256]{1,0:T(8,128)(2,1)S(1)} %collective-permute-done.8.rest_11_) | copy-start | bytes 1572868
  227.3 11.4 %copy-start.27 = (bf16[1024,256]{1,0:T(8,128)(2,1)}, bf16[1024,256]{1,0:T(8,128)(2,1)S(1)}, u32[]{:S(2)}) copy-start(bf16[1024,256]{1,0:T(8,128)(2,1)S(1)} %collective-permute-done.3.rest_5_) | copy-start | bytes 1572868
  238.8 0.8 copy-start.28

commit v2 on v1

v2 whole, which is shorter than its diff:
```python
import functools

import jax
import jax.numpy as jnp
from jax import lax
from jax.experimental import pallas as pl
from jax.experimental.pallas import tpu as pltpu
from jax.sharding import PartitionSpec as P

restart_rate = 0.1
beta_table = [
    0.4054651081081644,
    0.22314355131420976,
    0.15415067982725836,
    0.11778303565638346,
    0.09531017980432493,
    0.08004270767353637,
    0.06899287148695142,
    0.06062462181643484,
]
f32 = jnp.float32
bf16 = jnp.bfloat16
gelu_c = 0.7978845608028654
gelu_k = 0.044715
row_step = 256
vmem_limit = 58 * 1024 * 1024
VMEM = pl.BlockSpec(memory_space=pltpu.VMEM)
SMEM = pl.BlockSpec(memory_space=pltpu.SMEM)
ANY = pl.BlockSpec(memory_space=pl.ANY)


def pull_kernel(lo, capacity, wanted, history, rows_o, tables, folded, rows, sems):
    count, slab, width = tables.shape
    parts, slots, _ = rows_o.shape
    lanes = width // 2
    unroll = 4
    copies = [pltpu.make_async_copy(history.at[lo + i], tables.at[i], sems.at[i]) for i in range(count)]
    for copy in copies:
        copy.start()
    for layer in range(count):
        copies[layer].wait()
        folded[pl.ds(0, slab, stride=2), :] = tables[layer, :, :lanes].astype(f32)
        folded[pl.ds(1, slab, stride=2), :] = tables[layer, :, lanes:].astype(f32)

        def step(i, carry):
            for u in range(unroll):
                part = i * unroll + u
                base = pl.multiple_of(part * (2 * slots), 16)
                for c in range(capacity):
                    row = pl.multiple_of(2 * wanted[part, (lo + layer) * capacity + c], 2)
                    rows[pl.ds(base + 2 * (layer * capacity + c), 2), :] = folded[pl.ds(row, 2), :]
            return carry

        lax.fori_loop(0, parts // unroll, step, 0)
    for side in range(2):
        half = rows[pl.ds(side, parts * slots, stride=2), :]
        rows_o[:, :, side * lanes : (side + 1) * lanes] = half.reshape(parts, slots, lanes).astype(bf16)


def pull_rows(wanted, history, lo, count, capacity):
    _, slab, width = history.shape
    parts = wanted.shape[0]
    shape = (parts, count * capacity, width)
    return pl.pallas_call(
        functools.partial(pull_kernel, lo, capacity),
        out_shape=jax.ShapeDtypeStruct(shape, bf16),
        in_specs=[SMEM, ANY],
        out_specs=VMEM,
        scratch_shapes=[
            pltpu.VMEM((count, slab, width), bf16),
            pltpu.VMEM((2 * slab, width // 2), f32),
            pltpu.VMEM((2 * parts * count * capacity, width // 2), f32),
            pltpu.SemaphoreType.DMA((count,)),
        ],
        compiler_params=pltpu.CompilerParams(vmem_limit_bytes=vmem_limit),
        cost_estimate=pl.CostEstimate(flops=0, bytes_accessed=20_000_000, transcendentals=0),
    )(wanted, history)


def window(index, capacity):
    start = index * capacity // 16 * 16
    stop = -(-(index + 1) * capacity // 16) * 16
    return start, stop


def forward_math(depth, lo16, hi16, cols, hidden, tiles, pulled, dst, wt, features, weights, support_o, slope_o, hidden_o):
    beta = beta_table[depth]
    parts, _, width = pulled.shape
    slots = parts * (hi16 - lo16)
    row_count = features.shape[0]
    step = row_step
    per_block = tiles.shape[0] // (row_count // 128)
    dst_row = dst[depth : depth + 1, :]
    wt_row = wt[depth : depth + 1, :]
    for chunk in range(row_count // step):
        lo = chunk * step
        position = lax.broadcasted_iota(jnp.int32, (step, slots), 0) + lo
        scatter = jnp.where(dst_row == position, wt_row, 0.0).astype(bf16)
        acc = jnp.dot(
            scatter, pulled[:, lo16:hi16, :].reshape(slots, width), preferred_element_type=f32
        )
        parts_of = []
        for block in range(lo // 128, (lo + step) // 128):
            picked = jnp.concatenate(
                [
                    hidden[pl.ds(pl.multiple_of(cols[block * per_block + k] * 128, 128), 128), :]
                    for k in range(per_block)
                ],
                axis=0,
            )
            tile_row = jnp.concatenate([tiles[block * per_block + k] for k in range(per_block)], axis=1)
            parts_of.append(jnp.dot(tile_row, picked, preferred_element_type=f32))
        acc = acc + jnp.concatenate(parts_of, axis=0)
        support = (1.0 - restart_rate) * acc + restart_rate * features[lo : lo + step, :].astype(f32)
        support_bf = support.astype(bf16)
        support_o[lo : lo + step, :] = support_bf
        pre = (1.0 - beta) * support + beta * jnp.dot(
            support_bf, weights[depth], preferred_element_type=f32
        )
        square = pre * pre
        th = jnp.tanh(gelu_c * (pre + gelu_k * pre * square))
        half = 0.5 * (1.0 + th)
        hidden_o[lo : lo + step, :] = (pre * half).astype(bf16)
        slope_o[lo : lo + step, :] = half + 0.5 * pre * (1.0 - th * th) * (
            gelu_c * (1.0 + 3.0 * gelu_k * square)
        )


def forward_layer(depth, slots16, cols, hidden, tiles, pulled, dst, wt, features, weights):
    rows, width = features.shape
    return pl.pallas_call(
        functools.partial(forward_math, depth, *slots16),
        out_shape=(
            jax.ShapeDtypeStruct((rows, width), bf16),
            jax.ShapeDtypeStruct((rows, width), f32),
            jax.ShapeDtypeStruct((rows, width), bf16),
        ),
        in_specs=[SMEM] + [VMEM] * 7,
        out_specs=(VMEM, VMEM, VMEM),
        compiler_params=pltpu.CompilerParams(vmem_limit_bytes=vmem_limit),
        cost_estimate=pl.CostEstimate(flops=1_300_000_000, bytes_accessed=6_000_000, transcendentals=262144),
    )(cols, hidden, tiles, pulled, dst, wt, features, weights)


def finish_kernel(half, windows, *refs):
    cols, hidden, pulled, dst, wt, weights = refs[:6]
    count = 4 + 2 * half
    away, refs = refs[6 : 6 + count], refs[6 + count :]
    fresh, grads_o, refs = refs[:half], refs[half], refs[half + 1 :]
    held, refs = refs[:count], refs[count:]
    supports = held[4 : 4 + half] + refs[:half]
    slopes = held[4 + half :] + refs[half : 2 * half]
    total, grad_bf, gs_bf, sems = refs[2 * half :]
    tiles, features, cot, tiles_t = held[:4]
    copies = [pltpu.make_async_copy(a, b, sems.at[i]) for i, (a, b) in enumerate(zip(away, held))]
    for copy in copies:
        copy.start()
    copies[0].wait()
    copies[1].wait()
    for i in range(half):
        depth = half + i
        forward_math(
            depth, *windows[i], cols, hidden, tiles, pulled, dst, wt, features, weights,
            supports[depth], slopes[depth], fresh[i],
        )
        hidden = fresh[i]
    for copy in copies[2:]:
        copy.wait()
    backward_math(cols, cot, tiles_t, weights, supports, slopes, grads_o, total, grad_bf, gs_bf)


def backward_math(cols, cot, tiles_t, weights, supports, slopes, grads_o, total, grad_bf, gs_bf):
    layer_count = weights.shape[0]
    row_count, width = cot.shape
    step = row_step
    per_block = tiles_t.shape[0] // (row_count // 128)
    for depth in range(layer_count - 1, -1, -1):
        beta = beta_table[depth]
        weight = weights[depth]
        for chunk in range(row_count // step):
            lo = chunk * step
            if depth == layer_count - 1:
                grad_out = cot[lo : lo + step, :].astype(f32)
            else:
                grad_out = ((1.0 - restart_rate) * total[lo : lo + step, :]).astype(bf16).astype(f32)
            gp = grad_out * slopes[depth][lo : lo + step, :]
            gp_bf = gp.astype(bf16)
            grad_bf[lo : lo + step, :] = gp_bf
            if depth > 0:
                gs = (1.0 - beta) * gp + beta * lax.dot_general(
                    gp_bf, weight, (((1,), (1,)), ((), ())), preferred_element_type=f32
                )
                gs_bf[lo : lo + step, :] = gs.astype(bf16)
        grads_o[depth] = (
            beta
            * lax.dot_general(
                supports[depth][...], grad_bf[...], (((0,), (0,)), ((), ())), preferred_element_type=f32
            )
        ).astype(bf16)
        if depth > 0:
            total[...] = jnp.zeros_like(total)
            for block in range(row_count // 128):
                tile_col = jnp.concatenate(
                    [tiles_t[block * per_block + k] for k in range(per_block)], axis=0
                )
                product = jnp.dot(
                    tile_col, gs_bf[block * 128 : (block + 1) * 128, :], preferred_element_type=f32
                )
                for k in range(per_block):
                    at = pl.ds(pl.multiple_of(cols[block * per_block + k] * 128, 128), 128)
                    total[at, :] = total[at, :] + product[k * 128 : (k + 1) * 128, :]


def finish(half, windows, cols, hidden, pulled, dst, wt, weights, tiles, features, cot, tiles_t, supports, slopes):
    layer_count, width, _ = weights.shape
    away = [tiles, features, cot, tiles_t, *supports, *slopes]
    block = jax.ShapeDtypeStruct(features.shape, bf16)
    new = layer_count - half
    outs = pl.pallas_call(
        functools.partial(finish_kernel, half, windows),
        out_shape=(block,) * new + (jax.ShapeDtypeStruct((layer_count, width, width), bf16),),
        in_specs=[SMEM] + [VMEM] * 5 + [ANY] * len(away),
        out_specs=(VMEM,) * (new + 1),
        scratch_shapes=[pltpu.VMEM(a.shape, a.dtype) for a in away]
        + [pltpu.VMEM(features.shape, bf16)] * new
        + [pltpu.VMEM(features.shape, f32)] * new
        + [
            pltpu.VMEM(features.shape, f32),
            pltpu.VMEM(features.shape, bf16),
            pltpu.VMEM(features.shape, bf16),
            pltpu.SemaphoreType.DMA((len(away),)),
        ],
        compiler_params=pltpu.CompilerParams(vmem_limit_bytes=vmem_limit),
        cost_estimate=pl.CostEstimate(flops=5_000_000_000, bytes_accessed=12_000_000, transcendentals=524288),
    )(cols, hidden, pulled, dst, wt, weights, *away)
    return outs[:new], outs[new]


def assemble_kernel(places, replicas, rows, count, *refs):
    pieces = refs[:count]
    out, sems = refs[-2:]
    me = lax.axis_index("rep")
    copies = []
    for i, (layer, ahead, offset) in enumerate(places):
        at = lax.rem(me + ahead, replicas) * rows + offset
        size = pieces[i].shape[0]
        copies.append(
            pltpu.make_async_copy(
                pieces[i], out.at[layer, pl.ds(pl.multiple_of(at, 128), size), :], sems.at[i]
            )
        )
    for copy in copies:
        copy.start()
    for copy in copies:
        copy.wait()


def assemble(layers, replicas, rows, pieces, so_far):
    places = [piece[:3] for piece in pieces]
    blocks = [piece[3] for piece in pieces]
    width = blocks[0].shape[1]
    extra = [] if so_far is None else [so_far]
    return pl.pallas_call(
        functools.partial(assemble_kernel, places, replicas, rows, len(blocks)),
        out_shape=jax.ShapeDtypeStruct((layers, replicas * rows, width), bf16),
        in_specs=[VMEM] * len(blocks) + [ANY] * len(extra),
        out_specs=ANY,
        input_output_aliases={len(blocks): 0} if extra else {},
        scratch_shapes=[pltpu.SemaphoreType.DMA((len(blocks),))],
        cost_estimate=pl.CostEstimate(flops=0, bytes_accessed=4_200_000, transcendentals=0),
    )(*blocks, *extra)


def move(value, by):
    size = lax.axis_size("rep")
    return lax.ppermute(value, "rep", [(i, (i + by) % size) for i in range(size)])


def send_near(value):
    return [move(value, 1), move(value, -1)]


def send_far(near):
    half = near[0].shape[0] // 2
    return [move(near[0][:half], 1), move(near[1][half:], -1)]


def exchange(value, axis):
    return lax.all_to_all(value, axis, split_axis=0, concat_axis=0, tiled=True)


def body(
    features,
    history,
    tiles,
    tile_cols,
    halo_ids,
    halo_counts,
    halo_dst,
    halo_wt,
    weights,
    cotangent,
):
    row_count, width = features.shape
    layer_count = weights.shape[0]
    parts = lax.axis_size("dom")
    replicas = lax.axis_size("rep")
    slot_count = halo_ids.shape[1]
    capacity = slot_count // parts
    slab = history.shape[1]

    half = layer_count // 2

    wanted = halo_ids.reshape(layer_count, parts, capacity).transpose(1, 0, 2)
    wanted = exchange(wanted.reshape(parts, layer_count * capacity), "dom")
    early = exchange(pull_rows(wanted, history, 0, half, capacity), "dom")
    later = exchange(pull_rows(wanted, history, half, half, capacity), "dom")

    rank = jnp.arange(capacity, dtype=jnp.int32)
    live = rank[None, None, :] < halo_counts[:, :, None]
    slot_wt = jnp.where(live, halo_wt.reshape(layer_count, parts, capacity).astype(f32), 0.0)
    slot_dst = halo_dst.reshape(layer_count, parts, capacity)
    windows = [window(i, capacity) for i in range(half)]
    spread_dst, spread_wt = [], []
    for depth in range(layer_count):
        start, stop = windows[depth % half]
        before = depth % half * capacity - start
        pad = ((0, 0), (before, stop - start - capacity - before))
        spread_dst.append(jnp.pad(slot_dst[depth], pad).reshape(-1))
        spread_wt.append(jnp.pad(slot_wt[depth], pad).reshape(-1))
    dst = jnp.stack(spread_dst)
    wt = jnp.stack(spread_wt)
    tiles_t = tiles.transpose(0, 2, 1)

    hidden = features
    supports, slopes, fresh = [], [], []
    for depth in range(half):
        support_bf, slope, hidden = forward_layer(
            depth, windows[depth], tile_cols, hidden, tiles, early, dst, wt, features, weights
        )
        supports.append(support_bf)
        slopes.append(slope)
        fresh.append(hidden)
    near = [send_near(fresh[0]), send_near(hidden)]
    near[0], hidden = lax.optimization_barrier((near[0], hidden))
    far = [send_far(near[0])]
    later, near[1], far[0] = lax.optimization_barrier((later, near[1], far[0]))
    last, grads = finish(
        half, windows, tile_cols, hidden, later, dst, wt, weights,
        tiles, features, cotangent, tiles_t, supports, slopes,
    )
    fresh.append(last[0])
    hidden = last[1]
    near.append(send_near(fresh[2]))
    far.append(send_far(near[1]))
    chunk = layer_count * width // parts
    mine = exchange(grads.reshape(parts, chunk, width), "dom")
    mine, far[1], near[2] = lax.optimization_barrier((mine, far[1], near[2]))
    far.append(send_far(near[2]))
    mine = mine.astype(f32).sum(axis=0)
    mine = exchange(jnp.broadcast_to(mine[None], (replicas, chunk, width)), "rep")
    mine = mine.sum(axis=0)
    whole = exchange(jnp.broadcast_to(mine.astype(bf16)[None], (parts, chunk, width)), "dom")
    weight_grad = whole.astype(f32).reshape(layer_count, width, width)
    first, second = [], []
    for layer in range(layer_count - 1):
        first += [(layer, 0, 0, fresh[layer]), (layer, replicas - 1, 0, near[layer][0]), (layer, 1, 0, near[layer][1])]
        (second if layer + 2 == layer_count else first).extend(
            [(layer, 2, 0, far[layer][0]), (layer, 2, row_count // 2, far[layer][1])]
        )
    new_history = assemble(layer_count - 1, replicas, row_count, first, None)
    new_history = assemble(layer_count - 1, replicas, row_count, second, new_history)
    return (hidden, new_history, weight_grad)


def solution(mesh):
    in_specs = (
        P(("dom", "rep"), None),
        P(None, "dom", None),
        P(("dom", "rep"), None, None),
        P(("dom", "rep")),
        P(None, ("dom", "rep")),
        P(None, ("dom", "rep")),
        P(None, ("dom", "rep")),
        P(None, ("dom", "rep")),
        P(),
        P(("dom", "rep"), None),
    )
    out_specs = (P(("dom", "rep"), None), P(None, "dom", None), P())
    return jax.shard_map(body, mesh=mesh, in_specs=in_specs, out_specs=out_specs, check_vma=False)
```

time: 433 us -> 212 us (0.49)
  Pallas kernels: 210 us -> 51.8 us
  waiting for transfers between devices: 113 us -> 63.4 us
  local copies, waits for them, and re-layouts: 38.9 us -> 9.63 us
  blocking collectives: 22.9 us -> 30.4 us
  starting transfers between devices: 44.7 us -> 51.3 us
    pallas_call x6 -> x7, Pallas kernels: 210 us -> 51.8 us  [the longest x2 16.6 us: pull_rows(): pl.pallas_call(functools.partial(pull_kernel, lo, capacity), out_shape=ja...]
    ppermute x9 -> x12, waiting for transfers between devices: 55.1 us -> 20 us  [move(): lax.ppermute(value, 'rep', [(i, (i + by) % size) for i in range(size)])]
    gather x2 -> x0, local copies, waits for them, and re-layouts: 21.2 us -> none  [the longest x1 15.9 us: body(): history.reshape(layer_count * slab, width)]
    all_to_all x5 -> x4, waiting for transfers between devices: 57.4 us -> 43.4 us  [exchange(): return lax.all_to_all(value, axis, split_axis=0, concat_axis=0, tiled=True)]
    ppermute x9 -> x12, starting transfers between devices: 10.7 us -> 19.8 us  [move(): lax.ppermute(value, 'rep', [(i, (i + by) % size) for i in range(size)])]
    all_to_all x1 -> x2, blocking collectives: 22.9 us -> 30.4 us  [exchange(): return lax.all_to_all(value, axis, split_axis=0, concat_axis=0, tiled=True)]
    all_to_all x5 -> x4, starting transfers between devices: 34 us -> 31.5 us  [exchange(): return lax.all_to_all(value, axis, split_axis=0, concat_axis=0, tiled=True)]
  transfers between devices with their start and end apart: 14 -> 16, of which waited for: 9 -> 10; matrix products, arithmetic and copies ran while one was open for 6% -> 4% of each run, Pallas kernels for 45% -> 13%
where the time goes in v2:
time: 212 us; the launch traced here: 210 us
  waiting for transfers between devices  63.4 us (30%)
  Pallas kernels  51.8 us (24%)
  starting transfers between devices  51.3 us (24%)
  blocking collectives  30.4 us (14%)
  local copies, waits for them, and re-layouts  9.63 us (5%)
  other arithmetic  2.55 us (1%)
    all_to_all x4, waiting for transfers between devices, exchange(): return lax.all_to_all(value, axis, split_axis=0, concat_axis=0, tiled=True)  43.4 us
    all_to_all x4, starting transfers between devices, exchange(): return lax.all_to_all(value, axis, split_axis=0, concat_axis=0, tiled=True)  31.5 us
    all_to_all x2, blocking collectives, exchange(): return lax.all_to_all(value, axis, split_axis=0, concat_axis=0, tiled=True)  30.4 us
    ppermute x12, waiting for transfers between devices, move(): lax.ppermute(value, 'rep', [(i, (i + by) % size) for i in range(size)])  20 us
    ppermute x12, starting transfers between devices, move(): lax.ppermute(value, 'rep', [(i, (i + by) % size) for i in range(size)])  19.8 us
    pallas_call x2, Pallas kernels, pull_rows(): pl.pallas_call(functools.partial(pull_kernel, lo, capacity), out_shape=ja...  16.6 us
    pallas_call x1, Pallas kernels, finish(): pl.pallas_call(functools.partial(finish_kernel, half, windows), out_shape...  15.5 us
    pallas_call x2, Pallas kernels, forward_layer(): pl.pallas_call(functools.partial(forward_math, depth, *slots16), out_shap...  12.7 us
  transfers between devices with their start and end apart: 16, of which 10 were waited for; matrix products, arithmetic and copies ran while one was open for 4% of the time, Pallas kernels for 13%

profile of v2, /device:TPU:2, one launch (start us, length us, event | category | flops | bytes accessed | tf_op | source)
XLA Modules:
  0.0 210.1 jit_solution(12600817576949016953)
XLA Ops:
  0.6 0.8 reshape.39
  1.5 0.1 copy.22
  1.6 20.6 %all_to_all.36 = s32[64,1,96]{2,1,0:T(1,128)} all-to-all(s32[64,1,96]{2,1,0:T(1,128)S(1)} %copy.23), channel_id=1, replica_groups=mesh['dom'=64,'rep'=4] {'dom'}, dimensions={0} | all-to-all | bytes 49152 | tf_op jit(solution)/shard_map/all_to_all | solution.py:289
  22.2 8.3 %shard_map.121 = bf16[64,48,256]{2,1,0:T(8,128)(2,1)} custom-call(s32[64,96]{1,0:T(8,128)} %bitcast.21, bf16[4,4096,256]{2,1,0:T(8,128)(2,1)} %history.3), custom_call_target="tpu_custom_call" | custom-call | bytes 20000000 | tf_op jit(solution)/shard_map/pallas_call | solution.py:64
  30.5 5.4 %all-to-all-start.1 = ((bf16[64,48,256]{2,1,0:T(8,128)(2,1)}), bf16[64,48,256]{2,1,0:T(8,128)(2,1)S(1)}, u32[]{:S(2)}, u32[]{:S(2)}) async-start(bf16[64,48,256]{2,1,0:T(8,128)(2,1)} %shard_map.121), calls=%async_computation.1 | async-start | bytes 3145728 | tf_op jit(solution)/shard_map/all_to_all | solution.py:289
  35.9 8.3 %shard_map.124 = bf16[64,48,256]{2,1,0:T(8,128)(2,1)} custom-call(s32[64,96]{1,0:T(8,128)} %bitcast.22, bf16[4,4096,256]{2,1,0:T(8,128)(2,1)} %history.3), custom_call_target="tpu_custom_call" | custom-call | bytes 20000000 | tf_op jit(solution)/shard_map/pallas_call | solution.py:64
  44.3 31.8 %all-to-all-done.1.pulled = bf16[64,48,256]{2,1,0:T(8,128)(2,1)S(1)} async-done(((bf16[64,48,256]{2,1,0:T(8,128)(2,1)}), bf16[64,48,256]{2,1,0:T(8,128)(2,1)S(1)}, u32[]{:S(2)}, u32[]{:S(2)}) %all-to-all-start.1) | async-done | bytes 1572896 | tf_op jit(solution)/shard_map/all_to_all | solution.py:289
  76.1 5.4 %all-to-all-start.2 = ((bf16[64,48,256]{2,1,0:T(8,128)(2,1)}), bf16[64,48,256]{2,1,0:T(8,128)(2,1)S(1)}, u32[]{:S(2)}, u32[]{:S(2)}) async-start(bf16[64,48,256]{2,1,0:T(8,128)(2,1)} %shard_map.124), calls=%async_computation.2 | async-start | bytes 3145728 | tf_op jit(solution)/shard_map/all_to_all | solution.py:289
  81.6 0.1 squeeze.27
  81.7 0.1 pad.31
  81.8 0.1 stack_reshape.27
  81.9 0.1 squeeze.26
  82.0 0.1 stack_reshape.26
  82.0 0.1 squeeze.25
  82.1 0.1 pad.29
  82.2 0.1 stack_reshape.25
  82.3 0.1 squeeze.24
  82.4 0.1 stack_reshape.24
  82.5 0.1 reshape.43
  82.6 0.1 fusion
  82.8 0.1 stack_reshape.31
  82.9 0.1 stack_reshape.30
  83.1 0.1 stack_reshape.29
  83.2 0.1 stack_reshape.28
  83.3 0.7 pad_add_fusion.dst.refs_3_
  83.9 0.6 pad_maximum_fusion.wt.refs_4_
  84.6 6.4 %shard_map.122 = (bf16[1024,256]{1,0:T(8,128)(2,1)}, f32[1024,256]{1,0:T(8,128)}, bf16[1024,256]{1,0:T(8,128)(2,1)}) custom-call(s32[32]{0:T(128)} %refs_0_.1, bf16[1024,256]{1,0:T(8,128)(2,1)} %refs_7_.1, bf16[32,128,128]{2,1,0:T(8,128)(2,1)} %refs_6_.1, bf16[64,48,256]{2,1,0:T(8,128)(2,1)} %copy-done.1, s32[4,2048]{1,0:T(4,128)} %pad_add_fusion.dst.refs_3_, ...), custom_call_target="tpu_custom_call" | custom-call | flops 1300000000 | bytes 6000000 | tf_op jit(solution)/shard_map/pallas_call | solution.py:131
  90.9 1.6 collective-permute-start
  92.5 1.7 collective-permute-start.1
  94.2 6.4 %shard_map.123 = (bf16[1024,256]{1,0:T(8,128)(2,1)}, f32[1024,256]{1,0:T(8,128)}, bf16[1024,256]{1,0:T(8,128)(2,1)}) custom-call(s32[32]{0:T(128)} %refs_0_.1, bf16[1024,256]{1,0:T(8,128)(2,1)} %get-tuple-element.25.hidden.refs_0_, bf16[32,128,128]{2,1,0:T(8,128)(2,1)} %refs_6_.1, bf16[64,48,256]{2,1,0:T(8,128)(2,1)} %copy-done.1, ...), custom_call_target="tpu_custom_call" | custom-call | flops 1300000000 | bytes 6000000 | tf_op jit(solution)/shard_map/pallas_call | solution.py:131
  100.5 0.4 collective-permute-start.2
  100.9 2.9 %collective-permute-start.3 = (bf16[1024,256]{1,0:T(8,128)(2,1)}, bf16[1024,256]{1,0:T(8,128)(2,1)}, u32[]{:S(2)}, u32[]{:S(2)}) collective-permute-start(bf16[1024,256]{1,0:T(8,128)(2,1)} %get-tuple-element.27.refs_1_.refs_5_), channel_id=1, source_target_pairs={{0,3},{1,0},{2,1},{3,2},{4,7},{5,4},{6,5},{7,6},{8,11},{9,8},{10,9... | collective-permute-start | bytes 1572872 | tf_op jit(solution)/shard_map/ppermute | solution.py:276
  103.8 3.3 %collective-permute-done.refs_1_ = bf16[1024,256]{1,0:T(8,128)(2,1)S(1)} collective-permute-done((bf16[1024,256]{1,0:T(8,128)(2,1)}, bf16[1024,256]{1,0:T(8,128)(2,1)S(1)}, u32[]{:S(2)}, u32[]{:S(2)}) %collective-permute-start) | collective-permute-done | bytes 524320 | tf_op jit(solution)/shard_map/ppermute | solution.py:276
  107.1 0.4 collective-permute-done.1.refs_2_
  107.5 0.8 slice.54
  108.3 1.6 collective-permute-start.4
  109.9 0.8 slice.55
  110.6 1.7 collective-permute-start.5
  112.3 2.3 %copy.24 = bf16[32,128,128]{1,2,0:T(8,128)(2,1)} copy(bf16[32,128,128]{2,1,0:T(8,128)(2,1)} %refs_6_.1) | data formatting | bytes 2097152 | tf_op args[2]
  114.6 7.0 %all-to-all-done.2.refs_2_ = bf16[64,48,256]{2,1,0:T(8,128)(2,1)S(1)} async-done(((bf16[64,48,256]{2,1,0:T(8,128)(2,1)}), bf16[64,48,256]{2,1,0:T(8,128)(2,1)S(1)}, u32[]{:S(2)}, u32[]{:S(2)}) %all-to-all-start.2) | async-done | bytes 1572896 | tf_op jit(solution)/shard_map/all_to_all | solution.py:289
  121.5 1.7 collective-permute-done.4.refs_3_
  123.3 0.1 collective-permute-done.5.refs_4_
  123.4 15.5 %shard_map.125 = (bf16[1024,256]{1,0:T(8,128)(2,1)}, bf16[1024,256]{1,0:T(8,128)(2,1)}, bf16[4,256,256]{2,1,0:T(8,128)(2,1)}) custom-call(s32[32]{0:T(128)} %refs_0_.1, bf16[1024,256]{1,0:T(8,128)(2,1)} %get-tuple-element.27.refs_1_.refs_5_, bf16[64,48,256]{2,1,0:T(8,128)(2,1)} %copy-done, s32[4,2048]{1,0:T(4,128)} %pad_add_fusion.dst.refs_3_, ...), custom_call_target="tpu_custom_call" | custom-call | flops 5000000000 | bytes 12000000 | tf_op jit(solution)/shard_map/pallas_call | solution.py:219
  138.9 10.3 %all-to-all-start.3 = ((bf16[64,16,256]{2,1,0:T(8,128)(2,1)}), bf16[64,16,256]{2,1,0:T(8,128)(2,1)S(1)}, u32[]{:S(2)}, u32[]{:S(2)}) async-start(bf16[64,16,256]{2,1,0:T(8,128)(2,1)} %bitcast.19), calls=%async_computation.3 | async-start | bytes 1048576 | tf_op jit(solution)/shard_map/all_to_all | solution.py:289
  149.2 1.7 collective-permute-start.8
  150.8 1.7 collective-permute-start.9
  152.5 0.4 collective-permute-start.6
  153.0 1.0 slice.57
  153.9 3.0 %collective-permute-start.7 = (bf16[512,256]{1,0:T(8,128)(2,1)S(1)}, bf16[512,256]{1,0:T(8,128)(2,1)S(1)}, u32[]{:S(2)}, u32[]{:S(2)}) collective-permute-start(bf16[512,256]{1,0:T(8,128)(2,1)S(1)} %slice.57), channel_id=1, source_target_pairs={{0,3},{1,0},{2,1},{3,2},{4,7},{5,4},{6,5},{7,6},{8,11},{9,8},{10,9... | collective-permute-start | bytes 786440 | tf_op jit(solution)/shard_map/ppermute | solution.py:276
  156.9 13.4 %collective-permute-done.6.refs_8_ = bf16[512,256]{1,0:T(8,128)(2,1)S(1)} collective-permute-done((bf16[512,256]{1,0:T(8,128)(2,1)S(1)}, bf16[512,256]{1,0:T(8,128)(2,1)S(1)}, u32[]{:S(2)}, u32[]{:S(2)}) %collective-permute-start.6) | collective-permute-done | bytes 262176 | tf_op jit(solution)/shard_map/ppermute | solution.py:276
  170.3 0.1 collective-permute-done.7.refs_9_
  170.4 0.1 convert_reduce_fusion
  170.5 9.8 %all_to_all.37 = f32[4,16,256]{2,1,0:T(8,128)S(1)} all-to-all(f32[4,16,256]{2,1,0:T(8,128)S(1)} %broadcast_in_dim.9), channel_id=1, replica_groups=mesh['dom'=64,'rep'=4] {'rep'}, dimensions={0} | all-to-all | bytes 131072 | tf_op jit(solution)/shard_map/all_to_all | solution.py:289
  180.4 0.8 broadcast_in_dim.10
  181.2 10.3 %all-to-all-start.5 = ((bf16[64,16,256]{2,1,0:T(8,128)(2,1)}), bf16[64,16,256]{2,1,0:T(8,128)(2,1)S(1)}, u32[]{:S(2)}, u32[]{:S(2)}) async-start(bf16[64,16,256]{2,1,0:T(8,128)(2,1)} %broadcast_in_dim.10), calls=%async_computation.5 | async-start | bytes 1048576 | tf_op jit(solution)/shard_map/all_to_all | solution.py:289
  191.5 0.6 collective-permute-start.10
  192.2 2.7 %collective-permute-start.11 = (bf16[512,256]{1,0:T(8,128)(2,1)S(1)}, bf16[512,256]{1,0:T(8,128)(2,1)S(1)}, u32[]{:S(2)}, u32[]{:S(2)}) collective-permute-start(bf16[512,256]{1,0:T(8,128)(2,1)S(1)} %slice.59), channel_id=1, source_target_pairs={{0,3},{1,0},{2,1},{3,2},{4,7},{5,4},{6,5},{7,6},{8,11},{9,8},{10,9... | collective-permute-start | bytes 786440 | tf_op jit(solution)/shard_map/ppermute | solution.py:276
  195.0 5.2 %shard_map.126.refs_2_ = bf16[3,4096,256]{2,1,0:T(8,128)(2,1)} custom-call(bf16[1024,256]{1,0:T(8,128)(2,1)} %get-tuple-element.25.hidden.refs_0_, bf16[1024,256]{1,0:T(8,128)(2,1)} %copy-done.2, bf16[1024,256]{1,0:T(8,128)(2,1)} %copy-done.3, bf16[512,256]{1,0:T(8,128)(2,1)} %copy-done.7, bf16[512,256]{1,0:T(8,128)(2,1)} %collective-permute-done.5.refs_4_, ...), custom_call_target="tpu_custom_call" | custom-call | bytes 4200000 | tf_op jit(solution)/shard_map/pallas_call | solution.py:263
  200.2 1.0 collective-permute-done.10.refs_0_
  201.2 0.7 copy-done.10
  201.9 0.7 copy-done.11
  202.6 1.8 shard_map.127
  204.4 4.6 %all-to-all-done.5 = bf16[64,16,256]{2,1,0:T(8,128)(2,1)S(1)} async-done(((bf16[64,16,256]{2,1,0:T(8,128)(2,1)}), bf16[64,16,256]{2,1,0:T(8,128)(2,1)S(1)}, u32[]{:S(2)}, u32[]{:S(2)}) %all-to-all-start.5) | async-done | bytes 524320 | tf_op jit(solution)/shard_map/all_to_all | solution.py:289
  209.1 1.1 bitcast_convert_fusion
  (48 shorter events, 0.5 us)
Async XLA Ops:
  30.5 45.6 %all-to-all-start.1 = ((bf16[64,48,256]{2,1,0:T(8,128)(2,1)}), bf16[64,48,256]{2,1,0:T(8,128)(2,1)S(1)}, u32[]{:S(2)}, u32[]{:S(2)}) async-start(bf16[64,48,256]{2,1,0:T(8,128)(2,1)} %shard_map.121), calls=%async_computation.1 | async-start | bytes 3145728 | tf_op jit(solution)/shard_map/all_to_all | solution.py:289
  44.3 37.3 %copy-start.12 = (s32[4,1536]{1,0:T(4,128)S(1)}, s32[4,1536]{1,0:T(4,128)}, u32[]{:S(2)}) copy-start(s32[4,1536]{1,0:T(4,128)} %param.16) | copy-start | bytes 73732
  44.3 38.2 %copy-start.13 = (bf16[4,1536]{1,0:T(4,128)(2,1)S(1)}, bf16[4,1536]{1,0:T(4,128)(2,1)}, u32[]{:S(2)}) copy-start(bf16[4,1536]{1,0:T(4,128)(2,1)} %param.17) | copy-start | bytes 36868
  44.3 38.3 %copy-start.14 = (s32[4,64]{1,0:T(4,128)S(1)}, s32[4,64]{1,0:T(4,128)}, u32[]{:S(2)}) copy-start(s32[4,64]{1,0:T(4,128)} %param.15) | copy-start | bytes 3076
  76.1 5.5 %copy-start.1 = (bf16[64,48,256]{2,1,0:T(8,128)(2,1)}, bf16[64,48,256]{2,1,0:T(8,128)(2,1)S(1)}, u32[]{:S(2)}) copy-start(bf16[64,48,256]{2,1,0:T(8,128)(2,1)S(1)} %all-to-all-done.1.pulled) | copy-start | bytes 4718596
  76.1 45.5 %all-to-all-start.2 = ((bf16[64,48,256]{2,1,0:T(8,128)(2,1)}), bf16[64,48,256]{2,1,0:T(8,128)(2,1)S(1)}, u32[]{:S(2)}, u32[]{:S(2)}) async-start(bf16[64,48,256]{2,1,0:T(8,128)(2,1)} %shard_map.124), calls=%async_computation.2 | async-start | bytes 3145728 | tf_op jit(solution)/shard_map/all_to_all | solution.py:289
  90.9 16.2 %collective-permute-start = (bf16[1024,256]{1,0:T(8,128)(2,1)}, bf16[1024,256]{1,0:T(8,128)(2,1)S(1)}, u32[]{:S(2)}, u32[]{:S(2)}) collective-permute-start(bf16[1024,256]{1,0:T(8,128)(2,1)} %get-tuple-element.25.hidden.refs_0_), channel_id=1, source_target_pairs={{0,1},{1,2},{2,3},{3,0},{4,5},{5,6},{6,7},{7,4},{8,9},{9,10},{10,1... | collective-permute-start | bytes 1572872 | tf_op jit(solution)/shard_map/ppermute | solution.py:276
  92.5 15.0 %collective-permute-start.1 = (bf16[1024,256]{1,0:T(8,128)(2,1)}, bf16[1024,256]{1,0:T(8,128)(2,1)S(1)}, u32[]{:S(2)}, u32[]{:S(2)}) collective-permute-start(bf16[1024,256]{1,0:T(8,128)(2,1)} %get-tuple-element.25.hidden.refs_0_), channel_id=1, source_target_pairs={{0,3},{1,0},{2,1},{3,2},{4,7},{5,4},{6,5},{7,6},{8,11},{9,8},{10,9... | collective-permute-start | bytes 1572872 | tf_op jit(solution)/shard_map/ppermute | solution.py:276
  100.5 21.0 %collective-permute-start.2 = (bf16[1024,256]{1,0:T(8,128)(2,1)}, bf16[1024,256]{1,0:T(8,128)(2,1)S(1)}, u32[]{:S(2)}, u32[]{:S(2)}) collective-permute-start(bf16[1024,256]{1,0:T(8,128)(2,1)} %get-tuple-element.27.refs_1_.refs_5_), channel_id=1, source_target_pairs={{0,1},{1,2},{2,3},{3,0},{4,5},{5,6},{6,7},{7,4},{8,9},{9,10},{10,1... | collective-permute-start | bytes 1572872 | tf_op jit(solution)/shard_map/ppermute | solution.py:276
  100.9 20.6 %collective-permute-start.3 = (bf16[1024,256]{1,0:T(8,128)(2,1)}, bf16[1024,256]{1,0:T(8,128)(2,1)}, u32[]{:S(2)}, u32[]{:S(2)}) collective-permute-start(bf16[1024,256]{1,0:T(8,128)(2,1)} %get-tuple-element.27.refs_1_.refs_5_), channel_id=1, source_target_pairs={{0,3},{1,0},{2,1},{3,2},{4,7},{5,4},{6,5},{7,6},{8,11},{9,8},{10,9... | collective-permute-start | bytes 1572872 | tf_op jit(solution)/shard_map/ppermute | solution.py:276
  107.1 7.5 %copy-start.2 = (bf16[1024,256]{1,0:T(8,128)(2,1)}, bf16[1024,256]{1,0:T(8,128)(2,1)S(1)}, u32[]{:S(2)}) copy-start(bf16[1024,256]{1,0:T(8,128)(2,1)S(1)} %collective-permute-done.refs_1_) | copy-start | bytes 1572868
  107.5 7.0 %copy-start.3 = (bf16[1024,256]{1,0:T(8,128)(2,1)}, bf16[1024,256]{1,0:T(8,128)(2,1)S(1)}, u32[]{:S(2)}) copy-start(bf16[1024,256]{1,0:T(8,128)(2,1)S(1)} %collective-permute-done.1.refs_2_) | copy-start | bytes 1572868
  108.3 14.9 %collective-permute-start.4 = (bf16[512,256]{1,0:T(8,128)(2,1)}, bf16[512,256]{1,0:T(8,128)(2,1)S(1)}, u32[]{:S(2)}, u32[]{:S(2)}) collective-permute-start(bf16[512,256]{1,0:T(8,128)(2,1)} %slice.54), channel_id=1, source_target_pairs={{0,1},{1,2},{2,3},{3,0},{4,5},{5,6},{6,7},{7,4},{8,9},{9,10},{10,1... | collective-permute-start | bytes 786440 | tf_op jit(solution)/shard_map/ppermute | solution.py:276
  110.6 12.7 %collective-permute-start.5 = (bf16[512,256]{1,0:T(8,128)(2,1)}, bf16[512,256]{1,0:T(8,128)(2,1)}, u32[]{:S(2)}, u32[]{:S(2)}) collective-permute-start(bf16[512,256]{1,0:T(8,128)(2,1)} %slice.55), channel_id=1, source_target_pairs={{0,3},{1,0},{2,1},{3,2},{4,7},{5,4},{6,5},{7,6},{8,11},{9,8},{10,9... | collective-permute-start | bytes 786440 | tf_op jit(solution)/shard_map/ppermute | solution.py:276
  121.5 1.8 copy-start
  121.5 31.0 %copy-start.4 = (bf16[1024,256]{1,0:T(8,128)(2,1)}, bf16[1024,256]{1,0:T(8,128)(2,1)S(1)}, u32[]{:S(2)}) copy-start(bf16[1024,256]{1,0:T(8,128)(2,1)S(1)} %collective-permute-done.2.refs_6_) | copy-start | bytes 1572868
  123.3 15.6 %copy-start.7 = (bf16[512,256]{1,0:T(8,128)(2,1)}, bf16[512,256]{1,0:T(8,128)(2,1)S(1)}, u32[]{:S(2)}) copy-start(bf16[512,256]{1,0:T(8,128)(2,1)S(1)} %collective-permute-done.4.refs_3_) | copy-start | bytes 786436
  138.9 31.5 %all-to-all-start.3 = ((bf16[64,16,256]{2,1,0:T(8,128)(2,1)}), bf16[64,16,256]{2,1,0:T(8,128)(2,1)S(1)}, u32[]{:S(2)}, u32[]{:S(2)}) async-start(bf16[64,16,256]{2,1,0:T(8,128)(2,1)} %bitcast.19), calls=%async_computation.3 | async-start | bytes 1048576 | tf_op jit(solution)/shard_map/all_to_all | solution.py:289
  149.2 21.2 %collective-permute-start.8 = (bf16[1024,256]{1,0:T(8,128)(2,1)}, bf16[1024,256]{1,0:T(8,128)(2,1)S(1)}, u32[]{:S(2)}, u32[]{:S(2)}) collective-permute-start(bf16[1024,256]{1,0:T(8,128)(2,1)} %get-tuple-element.39.refs_10_), channel_id=1, source_target_pairs={{0,1},{1,2},{2,3},{3,0},{4,5},{5,6},{6,7},{7,4},{8,9},{9,10},{10,1... | collective-permute-start | bytes 1572872 | tf_op jit(solution)/shard_map/ppermute | solution.py:276
  150.8 19.5 %collective-permute-start.9 = (bf16[1024,256]{1,0:T(8,128)(2,1)}, bf16[1024,256]{1,0:T(8,128)(2,1)S(1)}, u32[]{:S(2)}, u32[]{:S(2)}) collective-permute-start(bf16[1024,256]{1,0:T(8,128)(2,1)} %get-tuple-element.39.refs_10_), channel_id=1, source_target_pairs={{0,3},{1,0},{2,1},{3,2},{4,7},{5,4},{6,5},{7,6},{8,11},{9,8},{10,9... | collective-permute-start | bytes 1572872 | tf_op jit(solution)/shard_map/ppermute | solution.py:276
  152.5 17.7 %collective-permute-start.6 = (bf16[512,256]{1,0:T(8,128)(2,1)S(1)}, bf16[512,256]{1,0:T(8,128)(2,1)S(1)}, u32[]{:S(2)}, u32[]{:S(2)}) collective-permute-start(bf16[512,256]{1,0:T(8,128)(2,1)S(1)} %slice.56), channel_id=1, source_target_pairs={{0,1},{1,2},{2,3},{3,0},{4,5},{5,6},{6,7},{7,4},{8,9},{9,10},{10,1... | collective-permute-start | bytes 786440 | tf_op jit(solution)/shard_map/ppermute | solution.py:276
  153.9 16.4 %collective-permute-start.7 = (bf16[512,256]{1,0:T(8,128)(2,1)S(1)}, bf16[512,256]{1,0:T(8,128)(2,1)S(1)}, u32[]{:S(2)}, u32[]{:S(2)}) collective-permute-start(bf16[512,256]{1,0:T(8,128)(2,1)S(1)} %slice.57), channel_id=1, source_target_pairs={{0,3},{1,0},{2,1},{3,2},{4,7},{5,4},{6,5},{7,6},{8,11},{9,8},{10,9... | collective-permute-start | bytes 786440 | tf_op jit(solution)/shard_map/ppermute | solution.py:276
  170.3 21.9 %copy-start.8 = (bf16[512,256]{1,0:T(8,128)(2,1)}, bf16[512,256]{1,0:T(8,128)(2,1)S(1)}, u32[]{:S(2)}) copy-start(bf16[512,256]{1,0:T(8,128)(2,1)S(1)} %collective-permute-done.6.refs_8_) | copy-start | bytes 786436
  170.4 21.8 %copy-start.9 = (bf16[512,256]{1,0:T(8,128)(2,1)}, bf16[512,256]{1,0:T(8,128)(2,1)S(1)}, u32[]{:S(2)}) copy-start(bf16[512,256]{1,0:T(8,128)(2,1)S(1)} %collective-permute-done.7.refs_9_) | copy-start | bytes 786436
  170.4 21.8 %copy-start.5 = (bf16[1024,256]{1,0:T(8,128)(2,1)}, bf16[1024,256]{1,0:T(8,128)(2,1)S(1)}, u32[]{:S(2)}) copy-start(bf16[1024,256]{1,0:T(8,128)(2,1)S(1)} %collective-permute-done.8.refs_11_) | copy-start | bytes 1572868
  170.4 21.8 %copy-start.6 = (bf16[1024,256]{1,0:T(8,128)(2,1)}, bf16[1024,256]{1,0:T(8,128)(2,1)S(1)}, u32[]{:S(2)}) copy-start(bf16[1024,256]{1,0:T(8,128)(2,1)S(1)} %collective-permute-done.9.refs_12_) | copy-start | bytes 1572868
  181.2 27.9 %all-to-all-start.5 = ((bf16[64,16,256]{2,1,0:T(8,128)(2,1)}), bf16[64,16,256]{2,1,0:T(8,128)(2,1)S(1)}, u32[]{:S(2)}, u32[]{:S(2)}) async-start(bf16[64,16,256]{2,1,0:T(8,128)(2,1)} %broadcast_in_dim.10), calls=%async_computation.5 | async-start | bytes 1048576 | tf_op jit(solution)/shard_map/all_to_all | solution.py:289
  191.5 9.6 %collective-permute-start.10 = (bf16[512,256]{1,0:T(8,128)(2,1)S(1)}, bf16[512,256]{1,0:T(8,128)(2,1)S(1)}, u32[]{:S(2)}, u32[]{:S(2)}) collective-permute-start(bf16[512,256]{1,0:T(8,128)(2,1)S(1)} %slice.58), channel_id=1, source_target_pairs={{0,1},{1,2},{2,3},{3,0},{4,5},{5,6},{6,7},{7,4},{8,9},{9,10},{10,1... | collective-permute-start | bytes 786440 | tf_op jit(solution)/shard_map/ppermute | solution.py:276
  192.2 8.9 %collective-permute-start.11 = (bf16[512,256]{1,0:T(8,128)(2,1)S(1)}, bf16[512,256]{1,0:T(8,128)(2,1)S(1)}, u32[]{:S(2)}, u32[]{:S(2)}) collective-permute-start(bf16[512,256]{1,0:T(8,128)(2,1)S(1)} %slice.59), channel_id=1, source_target_pairs={{0,3},{1,0},{2,1},{3,2},{4,7},{5,4},{6,5},{7,6},{8,11},{9,8},{10,9... | collective-permute-start | bytes 786440 | tf_op jit(solution)/shard_map/ppermute | solution.py:276
  201.2 0.7 copy-start.10
  201.9 0.7 copy-start.11

commit v3 on v2

--- a/solution.py
+++ b/solution.py
@@ -22,7 +22,7 @@
 bf16 = jnp.bfloat16
 gelu_c = 0.7978845608028654
 gelu_k = 0.044715
-row_step = 256
+row_step = 512
 vmem_limit = 58 * 1024 * 1024
 VMEM = pl.BlockSpec(memory_space=pltpu.VMEM)
 SMEM = pl.BlockSpec(memory_space=pltpu.SMEM)
@@ -77,16 +77,11 @@
     )(wanted, history)
 
 
-def window(index, capacity):
-    start = index * capacity // 16 * 16
-    stop = -(-(index + 1) * capacity // 16) * 16
-    return start, stop
-
-
-def forward_math(depth, lo16, hi16, cols, hidden, tiles, pulled, dst, wt, features, weights, support_o, slope_o, hidden_o):
+def forward_math(depth, at, cols, hidden, tiles, pulled, dst, wt, features, weights, support_o, slope_o, hidden_o):
     beta = beta_table[depth]
     parts, _, width = pulled.shape
-    slots = parts * (hi16 - lo16)
+    slots = dst.shape[1]
+    capacity = slots // parts
     row_count = features.shape[0]
     step = row_step
     per_block = tiles.shape[0] // (row_count // 128)
@@ -97,7 +92,9 @@
         position = lax.broadcasted_iota(jnp.int32, (step, slots), 0) + lo
         scatter = jnp.where(dst_row == position, wt_row, 0.0).astype(bf16)
         acc = jnp.dot(
-            scatter, pulled[:, lo16:hi16, :].reshape(slots, width), preferred_element_type=f32
+            scatter,
+            pulled[:, at * capacity : (at + 1) * capacity, :].reshape(slots, width),
+            preferred_element_type=f32,
         )
         parts_of = []
         for block in range(lo // 128, (lo + step) // 128):
@@ -126,10 +123,10 @@
         )
 
 
-def forward_layer(depth, slots16, cols, hidden, tiles, pulled, dst, wt, features, weights):
+def forward_layer(depth, at, cols, hidden, tiles, pulled, dst, wt, features, weights):
     rows, width = features.shape
     return pl.pallas_call(
-        functools.partial(forward_math, depth, *slots16),
+        functools.partial(forward_math, depth, at),
         out_shape=(
             jax.ShapeDtypeStruct((rows, width), bf16),
             jax.ShapeDtypeStruct((rows, width), f32),
@@ -142,7 +139,7 @@
     )(cols, hidden, tiles, pulled, dst, wt, features, weights)
 
 
-def finish_kernel(half, windows, *refs):
+def finish_kernel(half, *refs):
     cols, hidden, pulled, dst, wt, weights = refs[:6]
     count = 4 + 2 * half
     away, refs = refs[6 : 6 + count], refs[6 + count :]
@@ -160,7 +157,7 @@
     for i in range(half):
         depth = half + i
         forward_math(
-            depth, *windows[i], cols, hidden, tiles, pulled, dst, wt, features, weights,
+            depth, i, cols, hidden, tiles, pulled, dst, wt, features, weights,
             supports[depth], slopes[depth], fresh[i],
         )
         hidden = fresh[i]
@@ -211,13 +208,13 @@
                     total[at, :] = total[at, :] + product[k * 128 : (k + 1) * 128, :]
 
 
-def finish(half, windows, cols, hidden, pulled, dst, wt, weights, tiles, features, cot, tiles_t, supports, slopes):
+def finish(half, cols, hidden, pulled, dst, wt, weights, tiles, features, cot, tiles_t, supports, slopes):
     layer_count, width, _ = weights.shape
     away = [tiles, features, cot, tiles_t, *supports, *slopes]
     block = jax.ShapeDtypeStruct(features.shape, bf16)
     new = layer_count - half
     outs = pl.pallas_call(
-        functools.partial(finish_kernel, half, windows),
+        functools.partial(finish_kernel, half),
         out_shape=(block,) * new + (jax.ShapeDtypeStruct((layer_count, width, width), bf16),),
         in_specs=[SMEM] + [VMEM] * 5 + [ANY] * len(away),
         out_specs=(VMEM,) * (new + 1),
@@ -318,25 +315,14 @@
 
     rank = jnp.arange(capacity, dtype=jnp.int32)
     live = rank[None, None, :] < halo_counts[:, :, None]
-    slot_wt = jnp.where(live, halo_wt.reshape(layer_count, parts, capacity).astype(f32), 0.0)
-    slot_dst = halo_dst.reshape(layer_count, parts, capacity)
-    windows = [window(i, capacity) for i in range(half)]
-    spread_dst, spread_wt = [], []
-    for depth in range(layer_count):
-        start, stop = windows[depth % half]
-        before = depth % half * capacity - start
-        pad = ((0, 0), (before, stop - start - capacity - before))
-        spread_dst.append(jnp.pad(slot_dst[depth], pad).reshape(-1))
-        spread_wt.append(jnp.pad(slot_wt[depth], pad).reshape(-1))
-    dst = jnp.stack(spread_dst)
-    wt = jnp.stack(spread_wt)
+    wt = jnp.where(live.reshape(layer_count, slot_count), halo_wt.astype(f32), 0.0)
     tiles_t = tiles.transpose(0, 2, 1)
 
     hidden = features
     supports, slopes, fresh = [], [], []
     for depth in range(half):
         support_bf, slope, hidden = forward_layer(
-            depth, windows[depth], tile_cols, hidden, tiles, early, dst, wt, features, weights
+            depth, depth, tile_cols, hidden, tiles, early, halo_dst, wt, features, weights
         )
         supports.append(support_bf)
         slopes.append(slope)
@@ -346,7 +332,7 @@
     far = [send_far(near[0])]
     later, near[1], far[0] = lax.optimization_barrier((later, near[1], far[0]))
     last, grads = finish(
-        half, windows, tile_cols, hidden, later, dst, wt, weights,
+        half, tile_cols, hidden, later, halo_dst, wt, weights,
         tiles, features, cotangent, tiles_t, supports, slopes,
     )
     fresh.append(last[0])
@@ -355,7 +341,7 @@
     far.append(send_far(near[1]))
     chunk = layer_count * width // parts
     mine = exchange(grads.reshape(parts, chunk, width), "dom")
-    mine, far[1], near[2] = lax.optimization_barrier((mine, far[1], near[2]))
+    mine, near[2] = lax.optimization_barrier((mine, near[2]))
     far.append(send_far(near[2]))
     mine = mine.astype(f32).sum(axis=0)
     mine = exchange(jnp.broadcast_to(mine[None], (replicas, chunk, width)), "rep")
@@ -365,7 +351,7 @@
     first, second = [], []
     for layer in range(layer_count - 1):
         first += [(layer, 0, 0, fresh[layer]), (layer, replicas - 1, 0, near[layer][0]), (layer, 1, 0, near[layer][1])]
-        (second if layer + 2 == layer_count else first).extend(
+        (second if layer > 0 else first).extend(
             [(layer, 2, 0, far[layer][0]), (layer, 2, row_count // 2, far[layer][1])]
         )
     new_history = assemble(layer_count - 1, replicas, row_count, first, None)

time: 212 us -> 203 us (0.958)
  Pallas kernels: 51.8 us -> 47.4 us
  starting transfers between devices: 51.3 us -> 47.5 us
    pallas_call x3, Pallas kernels: 28.2 us -> 23.7 us  [the longest x1 13 us: finish(): pl.pallas_call(functools.partial(finish_kernel, half), out_shape=(block,)...]
    all_to_all x4, starting transfers between devices: 31.5 us -> 27.5 us  [exchange(): return lax.all_to_all(value, axis, split_axis=0, concat_axis=0, tiled=True)]
    unnamed x31 -> x29, local copies, waits for them, and re-layouts: 3.71 us -> 5.77 us
  transfers between devices with their start and end apart: 16 -> 16, of which waited for: 10 -> 9; matrix products, arithmetic and copies ran while one was open for 4% -> 3% of each run, Pallas kernels for 13% -> 13%
where the time goes in v3:
time: 203 us; the launch traced here: 202 us
  waiting for transfers between devices  63.5 us (31%)
  starting transfers between devices  47.5 us (23%)
  Pallas kernels  47.4 us (23%)
  blocking collectives  30.1 us (15%)
  local copies, waits for them, and re-layouts  10.4 us (5%)
    all_to_all x4, waiting for transfers between devices, exchange(): return lax.all_to_all(value, axis, split_axis=0, concat_axis=0, tiled=True)  43.6 us
    all_to_all x2, blocking collectives, exchange(): return lax.all_to_all(value, axis, split_axis=0, concat_axis=0, tiled=True)  30.1 us
    all_to_all x4, starting transfers between devices, exchange(): return lax.all_to_all(value, axis, split_axis=0, concat_axis=0, tiled=True)  27.5 us
    ppermute x12, starting transfers between devices, move(): lax.ppermute(value, 'rep', [(i, (i + by) % size) for i in range(size)])  20 us
    ppermute x12, waiting for transfers between devices, move(): lax.ppermute(value, 'rep', [(i, (i + by) % size) for i in range(size)])  19.8 us
    pallas_call x2, Pallas kernels, pull_rows(): pl.pallas_call(functools.partial(pull_kernel, lo, capacity), out_shape=ja...  16.6 us
    pallas_call x1, Pallas kernels, finish(): pl.pallas_call(functools.partial(finish_kernel, half), out_shape=(block,)...  13 us
    pallas_call x2, Pallas kernels, forward_layer(): pl.pallas_call(functools.partial(forward_math, depth, at), out_shape=(jax...  10.7 us
  transfers between devices with their start and end apart: 16, of which 9 were waited for; matrix products, arithmetic and copies ran while one was open for 3% of the time, Pallas kernels for 13%

profile of v3, /device:TPU:2, one launch (start us, length us, event | category | flops | bytes accessed | tf_op | source)
XLA Modules:
  0.0 201.6 jit_solution(5911019062573104533)
XLA Ops:
  0.6 0.8 reshape.30
  1.5 0.1 copy.22
  1.6 0.1 copy.23
  1.6 20.4 %all_to_all.36 = s32[64,1,96]{2,1,0:T(1,128)} all-to-all(s32[64,1,96]{2,1,0:T(1,128)S(1)} %copy.23), channel_id=1, replica_groups=mesh['dom'=64,'rep'=4] {'dom'}, dimensions={0} | all-to-all | bytes 49152 | tf_op jit(solution)/shard_map/all_to_all | solution.py:286
  22.1 8.3 %shard_map.121 = bf16[64,48,256]{2,1,0:T(8,128)(2,1)} custom-call(s32[64,96]{1,0:T(8,128)} %bitcast.13, bf16[4,4096,256]{2,1,0:T(8,128)(2,1)} %history.3), custom_call_target="tpu_custom_call" | custom-call | bytes 20000000 | tf_op jit(solution)/shard_map/pallas_call | solution.py:64
  30.3 5.7 %all-to-all-start.1 = ((bf16[64,48,256]{2,1,0:T(8,128)(2,1)}), bf16[64,48,256]{2,1,0:T(8,128)(2,1)S(1)}, u32[]{:S(2)}, u32[]{:S(2)}) async-start(bf16[64,48,256]{2,1,0:T(8,128)(2,1)} %shard_map.121), calls=%async_computation.1 | async-start | bytes 3145728 | tf_op jit(solution)/shard_map/all_to_all | solution.py:286
  36.1 8.3 %shard_map.124 = bf16[64,48,256]{2,1,0:T(8,128)(2,1)} custom-call(s32[64,96]{1,0:T(8,128)} %bitcast.14, bf16[4,4096,256]{2,1,0:T(8,128)(2,1)} %history.3), custom_call_target="tpu_custom_call" | custom-call | bytes 20000000 | tf_op jit(solution)/shard_map/pallas_call | solution.py:64
  44.4 0.0 copy-start.13
  44.4 0.0 copy-start.12
  44.5 31.8 %all-to-all-done.1.pulled = bf16[64,48,256]{2,1,0:T(8,128)(2,1)S(1)} async-done(((bf16[64,48,256]{2,1,0:T(8,128)(2,1)}), bf16[64,48,256]{2,1,0:T(8,128)(2,1)S(1)}, u32[]{:S(2)}, u32[]{:S(2)}) %all-to-all-start.1) | async-done | bytes 1572896 | tf_op jit(solution)/shard_map/all_to_all | solution.py:286
  76.2 1.1 copy-done.1
  77.4 5.4 %all-to-all-start.2 = ((bf16[64,48,256]{2,1,0:T(8,128)(2,1)}), bf16[64,48,256]{2,1,0:T(8,128)(2,1)S(1)}, u32[]{:S(2)}, u32[]{:S(2)}) async-start(bf16[64,48,256]{2,1,0:T(8,128)(2,1)} %shard_map.124), calls=%async_computation.2 | async-start | bytes 3145728 | tf_op jit(solution)/shard_map/all_to_all | solution.py:286
  82.8 0.1 lt.23
  82.9 0.1 lt.24
  83.0 0.1 lt.21
  83.1 0.6 convert_select_fusion.wt.refs_4_
  83.8 5.3 %shard_map.122 = (bf16[1024,256]{1,0:T(8,128)(2,1)}, f32[1024,256]{1,0:T(8,128)}, bf16[1024,256]{1,0:T(8,128)(2,1)}) custom-call(s32[32]{0:T(128)} %refs_0_.1, bf16[1024,256]{1,0:T(8,128)(2,1)} %refs_7_.1, bf16[32,128,128]{2,1,0:T(8,128)(2,1)} %refs_6_.1, bf16[64,48,256]{2,1,0:T(8,128)(2,1)} %copy-done.1, s32[4,1536]{1,0:T(4,128)} %refs_3_.1, ...), custom_call_target="tpu_custom_call" | custom-call | flops 1300000000 | bytes 6000000 | tf_op jit(solution)/shard_map/pallas_call | solution.py:128
  89.1 1.6 collective-permute-start
  90.7 1.7 collective-permute-start.1
  92.3 5.4 %shard_map.123 = (bf16[1024,256]{1,0:T(8,128)(2,1)}, f32[1024,256]{1,0:T(8,128)}, bf16[1024,256]{1,0:T(8,128)(2,1)}) custom-call(s32[32]{0:T(128)} %refs_0_.1, bf16[1024,256]{1,0:T(8,128)(2,1)} %get-tuple-element.23.hidden.refs_0_, bf16[32,128,128]{2,1,0:T(8,128)(2,1)} %refs_6_.1, bf16[64,48,256]{2,1,0:T(8,128)(2,1)} %copy-done.1, s32[4,1536]{1,0:T(4,128)} %refs_3_.1, ...), custom_call_target="tpu_custom_call" | custom-call | flops 1300000000 | bytes 6000000 | tf_op jit(solution)/shard_map/pallas_call | solution.py:128
  97.7 0.4 collective-permute-start.2
  98.1 2.9 %collective-permute-start.3 = (bf16[1024,256]{1,0:T(8,128)(2,1)}, bf16[1024,256]{1,0:T(8,128)(2,1)}, u32[]{:S(2)}, u32[]{:S(2)}) collective-permute-start(bf16[1024,256]{1,0:T(8,128)(2,1)} %get-tuple-element.25.refs_1_.refs_5_), channel_id=1, source_target_pairs={{0,3},{1,0},{2,1},{3,2},{4,7},{5,4},{6,5},{7,6},{8,11},{9,8},{10,9... | collective-permute-start | bytes 1572872 | tf_op jit(solution)/shard_map/ppermute | solution.py:273
  101.0 4.3 %collective-permute-done.refs_1_ = bf16[1024,256]{1,0:T(8,128)(2,1)S(1)} collective-permute-done((bf16[1024,256]{1,0:T(8,128)(2,1)}, bf16[1024,256]{1,0:T(8,128)(2,1)S(1)}, u32[]{:S(2)}, u32[]{:S(2)}) %collective-permute-start) | collective-permute-done | bytes 524320 | tf_op jit(solution)/shard_map/ppermute | solution.py:273
  105.3 0.4 collective-permute-done.1.refs_2_
  105.7 0.8 slice.18
  106.5 1.6 collective-permute-start.4
  108.0 0.7 slice.19
  108.8 1.7 collective-permute-start.5
  110.4 2.3 %copy.24 = bf16[32,128,128]{1,2,0:T(8,128)(2,1)} copy(bf16[32,128,128]{2,1,0:T(8,128)(2,1)} %refs_6_.1) | data formatting | bytes 2097152 | tf_op args[2]
  112.7 10.1 %all-to-all-done.2.refs_2_ = bf16[64,48,256]{2,1,0:T(8,128)(2,1)S(1)} async-done(((bf16[64,48,256]{2,1,0:T(8,128)(2,1)}), bf16[64,48,256]{2,1,0:T(8,128)(2,1)S(1)}, u32[]{:S(2)}, u32[]{:S(2)}) %all-to-all-start.2) | async-done | bytes 1572896 | tf_op jit(solution)/shard_map/all_to_all | solution.py:286
  122.8 0.0 collective-permute-done.2.refs_6_
  122.8 0.0 collective-permute-done.3.refs_7_
  122.8 0.0 collective-permute-done.4.refs_3_
  122.9 0.0 collective-permute-done.5.refs_4_
  122.9 1.2 copy-done
  124.1 13.0 %shard_map.125 = (bf16[1024,256]{1,0:T(8,128)(2,1)}, bf16[1024,256]{1,0:T(8,128)(2,1)}, bf16[4,256,256]{2,1,0:T(8,128)(2,1)}) custom-call(s32[32]{0:T(128)} %refs_0_.1, bf16[1024,256]{1,0:T(8,128)(2,1)} %get-tuple-element.25.refs_1_.refs_5_, bf16[64,48,256]{2,1,0:T(8,128)(2,1)} %copy-done, s32[4,1536]{1,0:T(4,128)} %refs_3_.1, ...), custom_call_target="tpu_custom_call" | custom-call | flops 5000000000 | bytes 12000000 | tf_op jit(solution)/shard_map/pallas_call | solution.py:216
  137.1 7.8 %all-to-all-start.3 = ((bf16[64,16,256]{2,1,0:T(8,128)(2,1)}), bf16[64,16,256]{2,1,0:T(8,128)(2,1)S(1)}, u32[]{:S(2)}, u32[]{:S(2)}) async-start(bf16[64,16,256]{2,1,0:T(8,128)(2,1)} %bitcast.11), calls=%async_computation.3 | async-start | bytes 1048576 | tf_op jit(solution)/shard_map/all_to_all | solution.py:286
  144.9 1.9 collective-permute-start.8
  146.8 1.7 collective-permute-start.9
  148.4 12.2 %collective-permute-done.8.refs_9_ = bf16[1024,256]{1,0:T(8,128)(2,1)S(1)} collective-permute-done((bf16[1024,256]{1,0:T(8,128)(2,1)}, bf16[1024,256]{1,0:T(8,128)(2,1)S(1)}, u32[]{:S(2)}, u32[]{:S(2)}) %collective-permute-start.8) | collective-permute-done | bytes 524320 | tf_op jit(solution)/shard_map/ppermute | solution.py:273
  160.6 0.1 collective-permute-done.9.refs_10_
  160.7 1.8 all-to-all-done.3
  162.4 0.1 convert_reduce_fusion
  162.5 9.6 %all_to_all.37 = f32[4,16,256]{2,1,0:T(8,128)S(1)} all-to-all(f32[4,16,256]{2,1,0:T(8,128)S(1)} %broadcast_in_dim.9), channel_id=1, replica_groups=mesh['dom'=64,'rep'=4] {'rep'}, dimensions={0} | all-to-all | bytes 131072 | tf_op jit(solution)/shard_map/all_to_all | solution.py:286
  172.2 0.8 broadcast_in_dim.10
  173.0 8.5 %all-to-all-start.5 = ((bf16[64,16,256]{2,1,0:T(8,128)(2,1)}), bf16[64,16,256]{2,1,0:T(8,128)(2,1)S(1)}, u32[]{:S(2)}, u32[]{:S(2)}) async-start(bf16[64,16,256]{2,1,0:T(8,128)(2,1)} %broadcast_in_dim.10), calls=%async_computation.5 | async-start | bytes 1048576 | tf_op jit(solution)/shard_map/all_to_all | solution.py:286
  181.6 0.6 collective-permute-start.6
  182.3 1.0 slice.21
  183.2 2.7 %collective-permute-start.7 = (bf16[512,256]{1,0:T(8,128)(2,1)S(1)}, bf16[512,256]{1,0:T(8,128)(2,1)S(1)}, u32[]{:S(2)}, u32[]{:S(2)}) collective-permute-start(bf16[512,256]{1,0:T(8,128)(2,1)S(1)} %slice.21), channel_id=1, source_target_pairs={{0,3},{1,0},{2,1},{3,2},{4,7},{5,4},{6,5},{7,6},{8,11},{9,8},{10,9... | collective-permute-start | bytes 786440 | tf_op jit(solution)/shard_map/ppermute | solution.py:273
  186.0 0.0 copy-done.5
  186.0 0.1 collective-permute-start.10
  186.1 0.0 copy-done.6
  186.1 3.3 %collective-permute-start.11 = (bf16[512,256]{1,0:T(8,128)(2,1)S(1)}, bf16[512,256]{1,0:T(8,128)(2,1)S(1)}, u32[]{:S(2)}, u32[]{:S(2)}) collective-permute-start(bf16[512,256]{1,0:T(8,128)(2,1)S(1)} %slice.23), channel_id=1, source_target_pairs={{0,3},{1,0},{2,1},{3,2},{4,7},{5,4},{6,5},{7,6},{8,11},{9,8},{10,9... | collective-permute-start | bytes 786440 | tf_op jit(solution)/shard_map/ppermute | solution.py:273
  189.4 4.9 %shard_map.126.refs_4_ = bf16[3,4096,256]{2,1,0:T(8,128)(2,1)} custom-call(bf16[1024,256]{1,0:T(8,128)(2,1)} %get-tuple-element.23.hidden.refs_0_, bf16[1024,256]{1,0:T(8,128)(2,1)} %copy-done.2, bf16[1024,256]{1,0:T(8,128)(2,1)} %copy-done.3, bf16[512,256]{1,0:T(8,128)(2,1)} %copy-done.7, bf16[512,256]{1,0:T(8,128)(2,1)} %collective-permute-done.5.refs_4_, ...), custom_call_target="tpu_custom_call" | custom-call | bytes 4200000 | tf_op jit(solution)/shard_map/pallas_call | solution.py:260
  194.3 0.0 collective-permute-done.6.refs_0_
  194.3 0.0 copy-start.8
  194.3 0.0 collective-permute-done.7.refs_1_
  194.3 2.5 %collective-permute-done.10.refs_2_ = bf16[512,256]{1,0:T(8,128)(2,1)S(1)} collective-permute-done((bf16[512,256]{1,0:T(8,128)(2,1)S(1)}, bf16[512,256]{1,0:T(8,128)(2,1)S(1)}, u32[]{:S(2)}, u32[]{:S(2)}) %collective-permute-start.10) | collective-permute-done | bytes 262176 | tf_op jit(solution)/shard_map/ppermute | solution.py:273
  196.9 0.3 collective-permute-done.11.refs_3_
  197.2 0.4 copy-done.10
  197.6 0.7 copy-done.11
  198.3 2.2 %shard_map.127 = bf16[3,4096,256]{2,1,0:T(8,128)(2,1)} custom-call(bf16[512,256]{1,0:T(8,128)(2,1)} %copy-done.8, bf16[512,256]{1,0:T(8,128)(2,1)} %copy-done.9, bf16[512,256]{1,0:T(8,128)(2,1)} %copy-done.10, bf16[512,256]{1,0:T(8,128)(2,1)} %copy-done.11, bf16[3,4096,256]{2,1,0:T(8,128)(2,1)} %shard_map.126.refs_4_), custom_call_target="tpu_custom_call", output_to_operand_aliasing={{}: (4, {})} | custom-call | bytes 4200000 | tf_op jit(solution)/shard_map/pallas_call | solution.py:260
  200.5 0.0 all-to-all-done.5
  200.5 1.1 bitcast_convert_fusion
  (25 shorter events, 0.1 us)
Async XLA Ops:
  30.3 45.9 %all-to-all-start.1 = ((bf16[64,48,256]{2,1,0:T(8,128)(2,1)}), bf16[64,48,256]{2,1,0:T(8,128)(2,1)S(1)}, u32[]{:S(2)}, u32[]{:S(2)}) async-start(bf16[64,48,256]{2,1,0:T(8,128)(2,1)} %shard_map.121), calls=%async_computation.1 | async-start | bytes 3145728 | tf_op jit(solution)/shard_map/all_to_all | solution.py:286
  44.4 38.4 %copy-start.13 = (s32[4,64]{1,0:T(4,128)S(1)}, s32[4,64]{1,0:T(4,128)}, u32[]{:S(2)}) copy-start(s32[4,64]{1,0:T(4,128)} %param.15) | copy-start | bytes 3076
  44.4 38.7 %copy-start.12 = (bf16[4,1536]{1,0:T(4,128)(2,1)S(1)}, bf16[4,1536]{1,0:T(4,128)(2,1)}, u32[]{:S(2)}) copy-start(bf16[4,1536]{1,0:T(4,128)(2,1)} %param.17) | copy-start | bytes 36868
  76.2 1.1 copy-start.1
  77.4 45.5 %all-to-all-start.2 = ((bf16[64,48,256]{2,1,0:T(8,128)(2,1)}), bf16[64,48,256]{2,1,0:T(8,128)(2,1)S(1)}, u32[]{:S(2)}, u32[]{:S(2)}) async-start(bf16[64,48,256]{2,1,0:T(8,128)(2,1)} %shard_map.124), calls=%async_computation.2 | async-start | bytes 3145728 | tf_op jit(solution)/shard_map/all_to_all | solution.py:286
  89.1 16.2 %collective-permute-start = (bf16[1024,256]{1,0:T(8,128)(2,1)}, bf16[1024,256]{1,0:T(8,128)(2,1)S(1)}, u32[]{:S(2)}, u32[]{:S(2)}) collective-permute-start(bf16[1024,256]{1,0:T(8,128)(2,1)} %get-tuple-element.23.hidden.refs_0_), channel_id=1, source_target_pairs={{0,1},{1,2},{2,3},{3,0},{4,5},{5,6},{6,7},{7,4},{8,9},{9,10},{10,1... | collective-permute-start | bytes 1572872 | tf_op jit(solution)/shard_map/ppermute | solution.py:273
  90.7 15.0 %collective-permute-start.1 = (bf16[1024,256]{1,0:T(8,128)(2,1)}, bf16[1024,256]{1,0:T(8,128)(2,1)S(1)}, u32[]{:S(2)}, u32[]{:S(2)}) collective-permute-start(bf16[1024,256]{1,0:T(8,128)(2,1)} %get-tuple-element.23.hidden.refs_0_), channel_id=1, source_target_pairs={{0,3},{1,0},{2,1},{3,2},{4,7},{5,4},{6,5},{7,6},{8,11},{9,8},{10,9... | collective-permute-start | bytes 1572872 | tf_op jit(solution)/shard_map/ppermute | solution.py:273
  97.7 25.1 %collective-permute-start.2 = (bf16[1024,256]{1,0:T(8,128)(2,1)}, bf16[1024,256]{1,0:T(8,128)(2,1)S(1)}, u32[]{:S(2)}, u32[]{:S(2)}) collective-permute-start(bf16[1024,256]{1,0:T(8,128)(2,1)} %get-tuple-element.25.refs_1_.refs_5_), channel_id=1, source_target_pairs={{0,1},{1,2},{2,3},{3,0},{4,5},{5,6},{6,7},{7,4},{8,9},{9,10},{10,1... | collective-permute-start | bytes 1572872 | tf_op jit(solution)/shard_map/ppermute | solution.py:273
  98.1 24.7 %collective-permute-start.3 = (bf16[1024,256]{1,0:T(8,128)(2,1)}, bf16[1024,256]{1,0:T(8,128)(2,1)}, u32[]{:S(2)}, u32[]{:S(2)}) collective-permute-start(bf16[1024,256]{1,0:T(8,128)(2,1)} %get-tuple-element.25.refs_1_.refs_5_), channel_id=1, source_target_pairs={{0,3},{1,0},{2,1},{3,2},{4,7},{5,4},{6,5},{7,6},{8,11},{9,8},{10,9... | collective-permute-start | bytes 1572872 | tf_op jit(solution)/shard_map/ppermute | solution.py:273
  105.3 7.4 %copy-start.2 = (bf16[1024,256]{1,0:T(8,128)(2,1)}, bf16[1024,256]{1,0:T(8,128)(2,1)S(1)}, u32[]{:S(2)}) copy-start(bf16[1024,256]{1,0:T(8,128)(2,1)S(1)} %collective-permute-done.refs_1_) | copy-start | bytes 1572868
  105.7 7.0 %copy-start.3 = (bf16[1024,256]{1,0:T(8,128)(2,1)}, bf16[1024,256]{1,0:T(8,128)(2,1)S(1)}, u32[]{:S(2)}) copy-start(bf16[1024,256]{1,0:T(8,128)(2,1)S(1)} %collective-permute-done.1.refs_2_) | copy-start | bytes 1572868
  106.5 16.4 %collective-permute-start.4 = (bf16[512,256]{1,0:T(8,128)(2,1)}, bf16[512,256]{1,0:T(8,128)(2,1)S(1)}, u32[]{:S(2)}, u32[]{:S(2)}) collective-permute-start(bf16[512,256]{1,0:T(8,128)(2,1)} %slice.18), channel_id=1, source_target_pairs={{0,1},{1,2},{2,3},{3,0},{4,5},{5,6},{6,7},{7,4},{8,9},{9,10},{10,1... | collective-permute-start | bytes 786440 | tf_op jit(solution)/shard_map/ppermute | solution.py:273
  108.8 14.1 %collective-permute-start.5 = (bf16[512,256]{1,0:T(8,128)(2,1)}, bf16[512,256]{1,0:T(8,128)(2,1)}, u32[]{:S(2)}, u32[]{:S(2)}) collective-permute-start(bf16[512,256]{1,0:T(8,128)(2,1)} %slice.19), channel_id=1, source_target_pairs={{0,3},{1,0},{2,1},{3,2},{4,7},{5,4},{6,5},{7,6},{8,11},{9,8},{10,9... | collective-permute-start | bytes 786440 | tf_op jit(solution)/shard_map/ppermute | solution.py:273
  122.8 1.2 copy-start
  122.8 58.7 %copy-start.4 = (bf16[1024,256]{1,0:T(8,128)(2,1)}, bf16[1024,256]{1,0:T(8,128)(2,1)S(1)}, u32[]{:S(2)}) copy-start(bf16[1024,256]{1,0:T(8,128)(2,1)S(1)} %collective-permute-done.2.refs_6_) | copy-start | bytes 1572868
  122.9 14.2 %copy-start.7 = (bf16[512,256]{1,0:T(8,128)(2,1)}, bf16[512,256]{1,0:T(8,128)(2,1)S(1)}, u32[]{:S(2)}) copy-start(bf16[512,256]{1,0:T(8,128)(2,1)S(1)} %collective-permute-done.4.refs_3_) | copy-start | bytes 786436
  137.1 25.4 %all-to-all-start.3 = ((bf16[64,16,256]{2,1,0:T(8,128)(2,1)}), bf16[64,16,256]{2,1,0:T(8,128)(2,1)S(1)}, u32[]{:S(2)}, u32[]{:S(2)}) async-start(bf16[64,16,256]{2,1,0:T(8,128)(2,1)} %bitcast.11), calls=%async_computation.3 | async-start | bytes 1048576 | tf_op jit(solution)/shard_map/all_to_all | solution.py:286
  144.9 15.7 %collective-permute-start.8 = (bf16[1024,256]{1,0:T(8,128)(2,1)}, bf16[1024,256]{1,0:T(8,128)(2,1)S(1)}, u32[]{:S(2)}, u32[]{:S(2)}) collective-permute-start(bf16[1024,256]{1,0:T(8,128)(2,1)} %get-tuple-element.37.refs_8_), channel_id=1, source_target_pairs={{0,1},{1,2},{2,3},{3,0},{4,5},{5,6},{6,7},{7,4},{8,9},{9,10},{10,1... | collective-permute-start | bytes 1572872 | tf_op jit(solution)/shard_map/ppermute | solution.py:273
  146.8 13.9 %collective-permute-start.9 = (bf16[1024,256]{1,0:T(8,128)(2,1)}, bf16[1024,256]{1,0:T(8,128)(2,1)S(1)}, u32[]{:S(2)}, u32[]{:S(2)}) collective-permute-start(bf16[1024,256]{1,0:T(8,128)(2,1)} %get-tuple-element.37.refs_8_), channel_id=1, source_target_pairs={{0,3},{1,0},{2,1},{3,2},{4,7},{5,4},{6,5},{7,6},{8,11},{9,8},{10,9... | collective-permute-start | bytes 1572872 | tf_op jit(solution)/shard_map/ppermute | solution.py:273
  160.6 25.4 %copy-start.5 = (bf16[1024,256]{1,0:T(8,128)(2,1)}, bf16[1024,256]{1,0:T(8,128)(2,1)S(1)}, u32[]{:S(2)}) copy-start(bf16[1024,256]{1,0:T(8,128)(2,1)S(1)} %collective-permute-done.8.refs_9_) | copy-start | bytes 1572868
  160.7 25.4 %copy-start.6 = (bf16[1024,256]{1,0:T(8,128)(2,1)}, bf16[1024,256]{1,0:T(8,128)(2,1)S(1)}, u32[]{:S(2)}) copy-start(bf16[1024,256]{1,0:T(8,128)(2,1)S(1)} %collective-permute-done.9.refs_10_) | copy-start | bytes 1572868
  173.0 27.5 %all-to-all-start.5 = ((bf16[64,16,256]{2,1,0:T(8,128)(2,1)}), bf16[64,16,256]{2,1,0:T(8,128)(2,1)S(1)}, u32[]{:S(2)}, u32[]{:S(2)}) async-start(bf16[64,16,256]{2,1,0:T(8,128)(2,1)} %broadcast_in_dim.10), calls=%async_computation.5 | async-start | bytes 1048576 | tf_op jit(solution)/shard_map/all_to_all | solution.py:286
  181.6 12.7 %collective-permute-start.6 = (bf16[512,256]{1,0:T(8,128)(2,1)S(1)}, bf16[512,256]{1,0:T(8,128)(2,1)S(1)}, u32[]{:S(2)}, u32[]{:S(2)}) collective-permute-start(bf16[512,256]{1,0:T(8,128)(2,1)S(1)} %slice.20), channel_id=1, source_target_pairs={{0,1},{1,2},{2,3},{3,0},{4,5},{5,6},{6,7},{7,4},{8,9},{9,10},{10,1... | collective-permute-start | bytes 786440 | tf_op jit(solution)/shard_map/ppermute | solution.py:273
  183.2 11.1 %collective-permute-start.7 = (bf16[512,256]{1,0:T(8,128)(2,1)S(1)}, bf16[512,256]{1,0:T(8,128)(2,1)S(1)}, u32[]{:S(2)}, u32[]{:S(2)}) collective-permute-start(bf16[512,256]{1,0:T(8,128)(2,1)S(1)} %slice.21), channel_id=1, source_target_pairs={{0,3},{1,0},{2,1},{3,2},{4,7},{5,4},{6,5},{7,6},{8,11},{9,8},{10,9... | collective-permute-start | bytes 786440 | tf_op jit(solution)/shard_map/ppermute | solution.py:273
  186.0 10.9 %collective-permute-start.10 = (bf16[512,256]{1,0:T(8,128)(2,1)S(1)}, bf16[512,256]{1,0:T(8,128)(2,1)S(1)}, u32[]{:S(2)}, u32[]{:S(2)}) collective-permute-start(bf16[512,256]{1,0:T(8,128)(2,1)S(1)} %slice.22), channel_id=1, source_target_pairs={{0,1},{1,2},{2,3},{3,0},{4,5},{5,6},{6,7},{7,4},{8,9},{9,10},{10,1... | collective-permute-start | bytes 786440 | tf_op jit(solution)/shard_map/ppermute | solution.py:273
  186.1 11.1 %collective-permute-start.11 = (bf16[512,256]{1,0:T(8,128)(2,1)S(1)}, bf16[512,256]{1,0:T(8,128)(2,1)S(1)}, u32[]{:S(2)}, u32[]{:S(2)}) collective-permute-start(bf16[512,256]{1,0:T(8,128)(2,1)S(1)} %slice.23), channel_id=1, source_target_pairs={{0,3},{1,0},{2,1},{3,2},{4,7},{5,4},{6,5},{7,6},{8,11},{9,8},{10,9... | collective-permute-start | bytes 786440 | tf_op jit(solution)/shard_map/ppermute | solution.py:273
  194.3 2.9 %copy-start.8 = (bf16[512,256]{1,0:T(8,128)(2,1)}, bf16[512,256]{1,0:T(8,128)(2,1)S(1)}, u32[]{:S(2)}) copy-start(bf16[512,256]{1,0:T(8,128)(2,1)S(1)} %collective-permute-done.6.refs_0_) | copy-start | bytes 786436
  194.3 2.9 %copy-start.9 = (bf16[512,256]{1,0:T(8,128)(2,1)}, bf16[512,256]{1,0:T(8,128)(2,1)S(1)}, u32[]{:S(2)}) copy-start(bf16[512,256]{1,0:T(8,128)(2,1)S(1)} %collective-permute-done.7.refs_1_) | copy-start | bytes 786436
  196.9 0.7 copy-start.10
  197.6 0.7 copy-start.11

commit v4 on v3

--- a/solution.py
+++ b/solution.py
@@ -24,6 +24,7 @@
 gelu_k = 0.044715
 row_step = 512
 vmem_limit = 58 * 1024 * 1024
+layer_vmem_limit = 46 * 1024 * 1024
 VMEM = pl.BlockSpec(memory_space=pltpu.VMEM)
 SMEM = pl.BlockSpec(memory_space=pltpu.SMEM)
 ANY = pl.BlockSpec(memory_space=pl.ANY)
@@ -134,7 +135,7 @@
         ),
         in_specs=[SMEM] + [VMEM] * 7,
         out_specs=(VMEM, VMEM, VMEM),
-        compiler_params=pltpu.CompilerParams(vmem_limit_bytes=vmem_limit),
+        compiler_params=pltpu.CompilerParams(vmem_limit_bytes=layer_vmem_limit),
         cost_estimate=pl.CostEstimate(flops=1_300_000_000, bytes_accessed=6_000_000, transcendentals=262144),
     )(cols, hidden, tiles, pulled, dst, wt, features, weights)
 
@@ -340,22 +341,27 @@
     near.append(send_near(fresh[2]))
     far.append(send_far(near[1]))
     chunk = layer_count * width // parts
+    def own(layer):
+        return (layer, 0, 0, fresh[layer])
+
+    def beside(layer):
+        return [(layer, replicas - 1, 0, near[layer][0]), (layer, 1, 0, near[layer][1])]
+
+    def across(layer):
+        return [(layer, 2, 0, far[layer][0]), (layer, 2, row_count // 2, far[layer][1])]
+
+    place = functools.partial(assemble, layer_count - 1, replicas, row_count)
     mine = exchange(grads.reshape(parts, chunk, width), "dom")
-    mine, near[2] = lax.optimization_barrier((mine, near[2]))
+    new_history = place([own(0), own(1), own(2)] + beside(0) + across(0) + beside(1), None)
+    mine, near[2], new_history = lax.optimization_barrier((mine, near[2], new_history))
     far.append(send_far(near[2]))
     mine = mine.astype(f32).sum(axis=0)
     mine = exchange(jnp.broadcast_to(mine[None], (replicas, chunk, width)), "rep")
     mine = mine.sum(axis=0)
     whole = exchange(jnp.broadcast_to(mine.astype(bf16)[None], (parts, chunk, width)), "dom")
     weight_grad = whole.astype(f32).reshape(layer_count, width, width)
-    first, second = [], []
-    for layer in range(layer_count - 1):
-        first += [(layer, 0, 0, fresh[layer]), (layer, replicas - 1, 0, near[layer][0]), (layer, 1, 0, near[layer][1])]
-        (second if layer > 0 else first).extend(
-            [(layer, 2, 0, far[layer][0]), (layer, 2, row_count // 2, far[layer][1])]
-        )
-    new_history = assemble(layer_count - 1, replicas, row_count, first, None)
-    new_history = assemble(layer_count - 1, replicas, row_count, second, new_history)
+    new_history = place(beside(2), new_history)
+    new_history = place(across(1) + across(2), new_history)
     return (hidden, new_history, weight_grad)
 
 

time: 203 us -> 201 us (level)
  waiting for transfers between devices: 63.5 us -> 71.1 us
  Pallas kernels: 47.4 us -> 44.8 us
  local copies, waits for them, and re-layouts: 10.4 us -> 8.2 us
  starting transfers between devices: 47.5 us -> 45.4 us
    ppermute x12, waiting for transfers between devices: 19.8 us -> 26.2 us  [move(): lax.ppermute(value, 'rep', [(i, (i + by) % size) for i in range(size)])]
    pallas_call x2, Pallas kernels: 10.7 us -> 5.93 us  [forward_layer(): pl.pallas_call(functools.partial(forward_math, depth, at), out_shape=(jax...]
    ppermute x12, starting transfers between devices: 20 us -> 16.1 us  [move(): lax.ppermute(value, 'rep', [(i, (i + by) % size) for i in range(size)])]
    pallas_call x2 -> x3, Pallas kernels: 7.07 us -> 8.59 us  [assemble(): pl.pallas_call(functools.partial(assemble_kernel, places, replicas, rows,...]
    unnamed x29 -> x53, local copies, waits for them, and re-layouts: 5.77 us -> 5.18 us
  transfers between devices with their start and end apart: 16 -> 16, of which waited for: 9 -> 10; matrix products, arithmetic and copies ran while one was open for 3% -> 1% of each run, Pallas kernels for 13% -> 11%
where the time goes in v4:
time: 201 us; the launch traced here: 200 us
  waiting for transfers between devices  71.1 us (35%)
  starting transfers between devices  45.4 us (23%)
  Pallas kernels  44.8 us (22%)
  blocking collectives  28.6 us (14%)
  local copies, waits for them, and re-layouts  8.2 us (4%)
    all_to_all x4, waiting for transfers between devices, exchange(): return lax.all_to_all(value, axis, split_axis=0, concat_axis=0, tiled=True)  45 us
    all_to_all x4, starting transfers between devices, exchange(): return lax.all_to_all(value, axis, split_axis=0, concat_axis=0, tiled=True)  29.4 us
    all_to_all x2, blocking collectives, exchange(): return lax.all_to_all(value, axis, split_axis=0, concat_axis=0, tiled=True)  28.6 us
    ppermute x12, waiting for transfers between devices, move(): lax.ppermute(value, 'rep', [(i, (i + by) % size) for i in range(size)])  26.2 us
    pallas_call x2, Pallas kernels, pull_rows(): pl.pallas_call(functools.partial(pull_kernel, lo, capacity), out_shape=ja...  16.7 us
    ppermute x12, starting transfers between devices, move(): lax.ppermute(value, 'rep', [(i, (i + by) % size) for i in range(size)])  16.1 us
    pallas_call x1, Pallas kernels, finish(): pl.pallas_call(functools.partial(finish_kernel, half), out_shape=(block,)...  13.6 us
    pallas_call x3, Pallas kernels, assemble(): pl.pallas_call(functools.partial(assemble_kernel, places, replicas, rows,...  8.59 us
  transfers between devices with their start and end apart: 16, of which 10 were waited for; matrix products, arithmetic and copies ran while one was open for 1% of the time, Pallas kernels for 11%

profile of v4, /device:TPU:2, one launch (start us, length us, event | category | flops | bytes accessed | tf_op | source)
XLA Modules:
  0.0 200.4 jit_solution(8111499038031551641)
XLA Ops:
  0.6 0.8 reshape.30
  1.5 0.1 copy.23
  1.6 0.1 copy.24
  1.6 20.6 %all_to_all.36 = s32[64,1,96]{2,1,0:T(1,128)} all-to-all(s32[64,1,96]{2,1,0:T(1,128)S(1)} %copy.24), channel_id=1, replica_groups=mesh['dom'=64,'rep'=4] {'dom'}, dimensions={0} | all-to-all | bytes 49152 | tf_op jit(solution)/shard_map/all_to_all | solution.py:287
  22.2 8.3 %shard_map.121 = bf16[64,48,256]{2,1,0:T(8,128)(2,1)} custom-call(s32[64,96]{1,0:T(8,128)} %bitcast.13, bf16[4,4096,256]{2,1,0:T(8,128)(2,1)} %history.3), custom_call_target="tpu_custom_call" | custom-call | bytes 20000000 | tf_op jit(solution)/shard_map/pallas_call | solution.py:65
  30.5 5.4 %all-to-all-start.1 = ((bf16[64,48,256]{2,1,0:T(8,128)(2,1)}), bf16[64,48,256]{2,1,0:T(8,128)(2,1)S(1)}, u32[]{:S(2)}, u32[]{:S(2)}) async-start(bf16[64,48,256]{2,1,0:T(8,128)(2,1)} %shard_map.121), calls=%async_computation.1 | async-start | bytes 3145728 | tf_op jit(solution)/shard_map/all_to_all | solution.py:287
  35.9 0.0 copy-start.25
  35.9 0.0 copy-start.24
  36.0 0.0 copy-start
  36.0 0.0 copy-start.5
  36.0 0.0 copy-start.6
  36.0 8.4 %shard_map.124 = bf16[64,48,256]{2,1,0:T(8,128)(2,1)} custom-call(s32[64,96]{1,0:T(8,128)} %bitcast.14, bf16[4,4096,256]{2,1,0:T(8,128)(2,1)} %history.3), custom_call_target="tpu_custom_call" | custom-call | bytes 20000000 | tf_op jit(solution)/shard_map/pallas_call | solution.py:65
  44.4 31.6 %all-to-all-done.1.pulled = bf16[64,48,256]{2,1,0:T(8,128)(2,1)S(1)} async-done(((bf16[64,48,256]{2,1,0:T(8,128)(2,1)}), bf16[64,48,256]{2,1,0:T(8,128)(2,1)S(1)}, u32[]{:S(2)}, u32[]{:S(2)}) %all-to-all-start.1) | async-done | bytes 1572896 | tf_op jit(solution)/shard_map/all_to_all | solution.py:287
  76.1 5.6 %all-to-all-start.2 = ((bf16[64,48,256]{2,1,0:T(8,128)(2,1)}), bf16[64,48,256]{2,1,0:T(8,128)(2,1)}, u32[]{:S(2)}, u32[]{:S(2)}) async-start(bf16[64,48,256]{2,1,0:T(8,128)(2,1)} %shard_map.124), calls=%async_computation.2 | async-start | bytes 3145728 | tf_op jit(solution)/shard_map/all_to_all | solution.py:287
  81.7 0.1 lt.21
  81.8 0.1 lt.23
  81.9 0.1 lt.24
  82.1 0.0 copy-start.3
  82.1 1.0 copy-done.3
  83.1 1.0 copy-done.4
  84.2 2.6 %shard_map.122 = (bf16[1024,256]{1,0:T(8,128)(2,1)S(1)}, f32[1024,256]{1,0:T(8,128)S(1)}, bf16[1024,256]{1,0:T(8,128)(2,1)S(1)}) custom-call(s32[32]{0:T(128)S(1)} %copy-done.6, bf16[1024,256]{1,0:T(8,128)(2,1)S(1)} %copy-done.3, bf16[32,128,128]{2,1,0:T(8,128)(2,1)S(1)} %copy-done, bf16[64,48,256]{2,1,0:T(8,128)(2,1)S(1)} %all-to-all-done.1.pulled, ...), custom_call_target="tpu_custom_call" | custom-call | flops 1300000000 | bytes 6000000 | tf_op jit(solution)/shard_map/pallas_call | solution.py:129
  86.7 0.0 copy-start.7
  86.8 3.1 %collective-permute-start.1 = (bf16[1024,256]{1,0:T(8,128)(2,1)S(1)}, bf16[1024,256]{1,0:T(8,128)(2,1)S(1)}, u32[]{:S(2)}, u32[]{:S(2)}) collective-permute-start(bf16[1024,256]{1,0:T(8,128)(2,1)S(1)} %get-tuple-element.24.hidden.refs_0_), channel_id=1, source_target_pairs={{0,3},{1,0},{2,1},{3,2},{4,7},{5,4},{6,5},{7,6},{8,11},{9,8},{10,9... | collective-permute-start | bytes 1572872 | tf_op jit(solution)/shard_map/ppermute | solution.py:274
  89.9 0.0 collective-permute-start
  89.9 3.4 %shard_map.123 = (bf16[1024,256]{1,0:T(8,128)(2,1)S(1)}, f32[1024,256]{1,0:T(8,128)S(1)}, bf16[1024,256]{1,0:T(8,128)(2,1)}) custom-call(s32[32]{0:T(128)S(1)} %copy-done.6, bf16[1024,256]{1,0:T(8,128)(2,1)S(1)} %get-tuple-element.24.hidden.refs_0_, bf16[32,128,128]{2,1,0:T(8,128)(2,1)S(1)} %copy-done, bf16[64,48,256]{2,1,0:T(8,128)(2,1)S(1)} %all-to-all-done.1.pulled, ...), custom_call_target="tpu_custom_call" | custom-call | flops 1300000000 | bytes 6000000 | tf_op jit(solution)/shard_map/pallas_call | solution.py:129
  93.2 1.0 copy-done.8
  94.2 3.2 %collective-permute-start.3 = (bf16[1024,256]{1,0:T(8,128)(2,1)}, bf16[1024,256]{1,0:T(8,128)(2,1)S(1)}, u32[]{:S(2)}, u32[]{:S(2)}) collective-permute-start(bf16[1024,256]{1,0:T(8,128)(2,1)} %get-tuple-element.26.refs_1_), channel_id=1, source_target_pairs={{0,3},{1,0},{2,1},{3,2},{4,7},{5,4},{6,5},{7,6},{8,11},{9,8},{10,9... | collective-permute-start | bytes 1572872 | tf_op jit(solution)/shard_map/ppermute | solution.py:274
  97.4 0.0 collective-permute-start.2
  97.5 4.7 %collective-permute-done.1.refs_4_ = bf16[1024,256]{1,0:T(8,128)(2,1)S(1)} collective-permute-done((bf16[1024,256]{1,0:T(8,128)(2,1)S(1)}, bf16[1024,256]{1,0:T(8,128)(2,1)S(1)}, u32[]{:S(2)}, u32[]{:S(2)}) %collective-permute-start.1) | collective-permute-done | bytes 524320 | tf_op jit(solution)/shard_map/ppermute | solution.py:274
  102.1 3.7 %collective-permute-done.refs_3_ = bf16[1024,256]{1,0:T(8,128)(2,1)S(1)} collective-permute-done((bf16[1024,256]{1,0:T(8,128)(2,1)S(1)}, bf16[1024,256]{1,0:T(8,128)(2,1)S(1)}, u32[]{:S(2)}, u32[]{:S(2)}) %collective-permute-start) | collective-permute-done | bytes 524320 | tf_op jit(solution)/shard_map/ppermute | solution.py:274
  105.9 0.8 slice.19
  106.7 0.0 collective-permute-start.5
  106.7 0.0 copy-done.16
  106.8 2.0 collective-permute-start.4
  108.7 1.3 copy.25
  110.0 11.6 %all-to-all-done.2.refs_2_ = bf16[64,48,256]{2,1,0:T(8,128)(2,1)} async-done(((bf16[64,48,256]{2,1,0:T(8,128)(2,1)}), bf16[64,48,256]{2,1,0:T(8,128)(2,1)}, u32[]{:S(2)}, u32[]{:S(2)}) %all-to-all-start.2) | async-done | bytes 1572896 | tf_op jit(solution)/shard_map/all_to_all | solution.py:287
  121.6 0.0 collective-permute-done.3.refs_8_
  121.6 0.0 collective-permute-done.2.refs_7_
  121.7 0.0 collective-permute-done.5.refs_6_
  121.7 13.6 %shard_map.125 = (bf16[1024,256]{1,0:T(8,128)(2,1)}, bf16[1024,256]{1,0:T(8,128)(2,1)}, bf16[4,256,256]{2,1,0:T(8,128)(2,1)}) custom-call(s32[32]{0:T(128)} %refs_0_.1, bf16[1024,256]{1,0:T(8,128)(2,1)} %get-tuple-element.26.refs_1_, bf16[64,48,256]{2,1,0:T(8,128)(2,1)} %all-to-all-done.2.refs_2_, s32[4,1536]{1,0:T(4,128)} %refs_3_.1, f32[4,1536]{1,0:T(4,128)} %copy-done.2, ...), custom_call_target="tpu_custom_call" | custom-call | flops 5000000000 | bytes 12000000 | tf_op jit(solution)/shard_map/pallas_call | solution.py:217
  135.3 9.8 %all-to-all-start.3 = ((bf16[64,16,256]{2,1,0:T(8,128)(2,1)}), bf16[64,16,256]{2,1,0:T(8,128)(2,1)S(1)}, u32[]{:S(2)}, u32[]{:S(2)}) async-start(bf16[64,16,256]{2,1,0:T(8,128)(2,1)} %bitcast.11), calls=%async_computation.3 | async-start | bytes 1048576 | tf_op jit(solution)/shard_map/all_to_all | solution.py:287
  145.2 0.7 collective-permute-start.9
  145.8 1.6 collective-permute-start.8
  147.5 4.2 %shard_map.126.refs_2_ = bf16[3,4096,256]{2,1,0:T(8,128)(2,1)} custom-call(bf16[1024,256]{1,0:T(8,128)(2,1)} %copy-done.1, bf16[1024,256]{1,0:T(8,128)(2,1)} %get-tuple-element.26.refs_1_, bf16[1024,256]{1,0:T(8,128)(2,1)} %get-tuple-element.38.refs_2_, bf16[1024,256]{1,0:T(8,128)(2,1)} %copy-done.16, bf16[1024,256]{1,0:T(8,128)(2,1)} %copy-done.15, ...), custom_call_target="tpu_custom_call" | custom-call | bytes 4200000 | tf_op jit(solution)/shard_map/pallas_call | solution.py:261
  151.7 7.9 %collective-permute-done.9.refs_1_ = bf16[1024,256]{1,0:T(8,128)(2,1)S(1)} collective-permute-done((bf16[1024,256]{1,0:T(8,128)(2,1)}, bf16[1024,256]{1,0:T(8,128)(2,1)S(1)}, u32[]{:S(2)}, u32[]{:S(2)}) %collective-permute-start.9) | collective-permute-done | bytes 524320 | tf_op jit(solution)/shard_map/ppermute | solution.py:274
  159.6 1.3 collective-permute-done.8.refs_0_
  161.0 1.7 all-to-all-done.3
  162.7 0.1 convert_reduce_fusion
  162.8 8.0 %all_to_all.37 = f32[4,16,256]{2,1,0:T(8,128)S(1)} all-to-all(f32[4,16,256]{2,1,0:T(8,128)S(1)} %broadcast_in_dim.9), channel_id=1, replica_groups=mesh['dom'=64,'rep'=4] {'rep'}, dimensions={0} | all-to-all | bytes 131072 | tf_op jit(solution)/shard_map/all_to_all | solution.py:287
  170.8 0.8 broadcast_in_dim.10
  171.6 8.6 %all-to-all-start.5 = ((bf16[64,16,256]{2,1,0:T(8,128)(2,1)}), bf16[64,16,256]{2,1,0:T(8,128)(2,1)S(1)}, u32[]{:S(2)}, u32[]{:S(2)}) async-start(bf16[64,16,256]{2,1,0:T(8,128)(2,1)} %broadcast_in_dim.10), calls=%async_computation.5 | async-start | bytes 1048576 | tf_op jit(solution)/shard_map/all_to_all | solution.py:287
  180.3 1.2 collective-permute-start.7
  181.5 0.9 collective-permute-start.6
  182.4 0.6 collective-permute-start.10
  183.1 2.7 %collective-permute-start.11 = (bf16[512,256]{1,0:T(8,128)(2,1)S(1)}, bf16[512,256]{1,0:T(8,128)(2,1)}, u32[]{:S(2)}, u32[]{:S(2)}) collective-permute-start(bf16[512,256]{1,0:T(8,128)(2,1)S(1)} %slice.23), channel_id=1, source_target_pairs={{0,3},{1,0},{2,1},{3,2},{4,7},{5,4},{6,5},{7,6},{8,11},{9,8},{10,9... | collective-permute-start | bytes 786440 | tf_op jit(solution)/shard_map/ppermute | solution.py:274
  185.7 2.2 %shard_map.127.refs_4_ = bf16[3,4096,256]{2,1,0:T(8,128)(2,1)} custom-call(bf16[1024,256]{1,0:T(8,128)(2,1)} %copy-done.18, bf16[1024,256]{1,0:T(8,128)(2,1)} %copy-done.17, bf16[3,4096,256]{2,1,0:T(8,128)(2,1)} %shard_map.126.refs_2_), custom_call_target="tpu_custom_call", output_to_operand_aliasing={{}: (2, {})} | custom-call | bytes 4200000 | tf_op jit(solution)/shard_map/pallas_call | solution.py:261
  187.9 1.6 collective-permute-done.7.refs_1_
  189.5 2.4 %collective-permute-done.6.refs_0_ = bf16[512,256]{1,0:T(8,128)(2,1)S(1)} collective-permute-done((bf16[512,256]{1,0:T(8,128)(2,1)S(1)}, bf16[512,256]{1,0:T(8,128)(2,1)S(1)}, u32[]{:S(2)}, u32[]{:S(2)}) %collective-permute-start.6) | collective-permute-done | bytes 262176 | tf_op jit(solution)/shard_map/ppermute | solution.py:274
  191.9 4.5 %collective-permute-done.10.refs_2_ = bf16[512,256]{1,0:T(8,128)(2,1)S(1)} collective-permute-done((bf16[512,256]{1,0:T(8,128)(2,1)S(1)}, bf16[512,256]{1,0:T(8,128)(2,1)S(1)}, u32[]{:S(2)}, u32[]{:S(2)}) %collective-permute-start.10) | collective-permute-done | bytes 262176 | tf_op jit(solution)/shard_map/ppermute | solution.py:274
  196.4 0.0 collective-permute-done.11.refs_3_
  196.4 0.7 copy-done.23
  197.1 2.2 %shard_map.128 = bf16[3,4096,256]{2,1,0:T(8,128)(2,1)} custom-call(bf16[512,256]{1,0:T(8,128)(2,1)} %copy-done.22, bf16[512,256]{1,0:T(8,128)(2,1)} %copy-done.21, bf16[512,256]{1,0:T(8,128)(2,1)} %copy-done.23, bf16[512,256]{1,0:T(8,128)(2,1)} %collective-permute-done.11.refs_3_, ...), custom_call_target="tpu_custom_call", output_to_operand_aliasing={{}: (4, {})} | custom-call | bytes 4200000 | tf_op jit(solution)/shard_map/pallas_call | solution.py:261
  199.3 0.0 all-to-all-done.5
  199.3 1.1 bitcast_convert_fusion
  (50 shorter events, 0.2 us)
Async XLA Ops:
  30.5 45.6 %all-to-all-start.1 = ((bf16[64,48,256]{2,1,0:T(8,128)(2,1)}), bf16[64,48,256]{2,1,0:T(8,128)(2,1)S(1)}, u32[]{:S(2)}, u32[]{:S(2)}) async-start(bf16[64,48,256]{2,1,0:T(8,128)(2,1)} %shard_map.121), calls=%async_computation.1 | async-start | bytes 3145728 | tf_op jit(solution)/shard_map/all_to_all | solution.py:287
  35.9 45.8 %copy-start.25 = (s32[4,64]{1,0:T(4,128)S(1)}, s32[4,64]{1,0:T(4,128)}, u32[]{:S(2)}) copy-start(s32[4,64]{1,0:T(4,128)} %param.15) | copy-start | bytes 3076
  35.9 46.1 %copy-start.24 = (bf16[4,1536]{1,0:T(4,128)(2,1)S(1)}, bf16[4,1536]{1,0:T(4,128)(2,1)}, u32[]{:S(2)}) copy-start(bf16[4,1536]{1,0:T(4,128)(2,1)} %param.17) | copy-start | bytes 36868
  36.0 46.1 %copy-start = (bf16[32,128,128]{2,1,0:T(8,128)(2,1)S(1)}, bf16[32,128,128]{2,1,0:T(8,128)(2,1)}, u32[]{:S(2)}) copy-start(bf16[32,128,128]{2,1,0:T(8,128)(2,1)} %refs_6_.1) | copy-start | bytes 3145732
  36.0 46.1 %copy-start.5 = (s32[4,1536]{1,0:T(4,128)S(1)}, s32[4,1536]{1,0:T(4,128)}, u32[]{:S(2)}) copy-start(s32[4,1536]{1,0:T(4,128)} %refs_3_.1) | copy-start | bytes 73732
  36.0 46.1 %copy-start.6 = (s32[32]{0:T(128)S(1)}, s32[32]{0:T(128)}, u32[]{:S(2)}) copy-start(s32[32]{0:T(128)} %refs_0_.1) | copy-start | bytes 388
  76.1 45.6 %all-to-all-start.2 = ((bf16[64,48,256]{2,1,0:T(8,128)(2,1)}), bf16[64,48,256]{2,1,0:T(8,128)(2,1)}, u32[]{:S(2)}, u32[]{:S(2)}) async-start(bf16[64,48,256]{2,1,0:T(8,128)(2,1)} %shard_map.124), calls=%async_computation.2 | async-start | bytes 3145728 | tf_op jit(solution)/shard_map/all_to_all | solution.py:287
  82.1 1.0 copy-start.3
  83.1 1.0 copy-start.4
  84.2 25.9 %copy-start.2 = (f32[4,1536]{1,0:T(4,128)}, f32[4,1536]{1,0:T(4,128)S(1)}, u32[]{:S(2)}) copy-start(f32[4,1536]{1,0:T(4,128)S(1)} %convert_select_fusion.wt.refs_4_) | copy-start | bytes 73732
  86.7 19.1 %copy-start.7 = (f32[1024,256]{1,0:T(8,128)}, f32[1024,256]{1,0:T(8,128)S(1)}, u32[]{:S(2)}) copy-start(f32[1024,256]{1,0:T(8,128)S(1)} %get-tuple-element.32.refs_12_) | copy-start | bytes 3145732
  86.7 19.2 %copy-start.9 = (bf16[1024,256]{1,0:T(8,128)(2,1)}, bf16[1024,256]{1,0:T(8,128)(2,1)S(1)}, u32[]{:S(2)}) copy-start(bf16[1024,256]{1,0:T(8,128)(2,1)S(1)} %get-tuple-element.30.refs_10_) | copy-start | bytes 1572868
  86.8 48.5 %copy-start.1 = (bf16[1024,256]{1,0:T(8,128)(2,1)}, bf16[1024,256]{1,0:T(8,128)(2,1)S(1)}, u32[]{:S(2)}) copy-start(bf16[1024,256]{1,0:T(8,128)(2,1)S(1)} %get-tuple-element.24.hidden.refs_0_) | copy-start | bytes 1572868
  86.8 15.4 %collective-permute-start.1 = (bf16[1024,256]{1,0:T(8,128)(2,1)S(1)}, bf16[1024,256]{1,0:T(8,128)(2,1)S(1)}, u32[]{:S(2)}, u32[]{:S(2)}) collective-permute-start(bf16[1024,256]{1,0:T(8,128)(2,1)S(1)} %get-tuple-element.24.hidden.refs_0_), channel_id=1, source_target_pairs={{0,3},{1,0},{2,1},{3,2},{4,7},{5,4},{6,5},{7,6},{8,11},{9,8},{10,9... | collective-permute-start | bytes 1572872 | tf_op jit(solution)/shard_map/ppermute | solution.py:274
  89.9 16.0 %collective-permute-start = (bf16[1024,256]{1,0:T(8,128)(2,1)S(1)}, bf16[1024,256]{1,0:T(8,128)(2,1)S(1)}, u32[]{:S(2)}, u32[]{:S(2)}) collective-permute-start(bf16[1024,256]{1,0:T(8,128)(2,1)S(1)} %get-tuple-element.24.hidden.refs_0_), channel_id=1, source_target_pairs={{0,1},{1,2},{2,3},{3,0},{4,5},{5,6},{6,7},{7,4},{8,9},{9,10},{10,1... | collective-permute-start | bytes 1572872 | tf_op jit(solution)/shard_map/ppermute | solution.py:274
  93.2 1.0 copy-start.8
  94.2 12.5 %copy-start.10 = (bf16[1024,256]{1,0:T(8,128)(2,1)}, bf16[1024,256]{1,0:T(8,128)(2,1)S(1)}, u32[]{:S(2)}) copy-start(bf16[1024,256]{1,0:T(8,128)(2,1)S(1)} %get-tuple-element.31.refs_11_) | copy-start | bytes 1572868
  94.2 27.4 %collective-permute-start.3 = (bf16[1024,256]{1,0:T(8,128)(2,1)}, bf16[1024,256]{1,0:T(8,128)(2,1)S(1)}, u32[]{:S(2)}, u32[]{:S(2)}) collective-permute-start(bf16[1024,256]{1,0:T(8,128)(2,1)} %get-tuple-element.26.refs_1_), channel_id=1, source_target_pairs={{0,3},{1,0},{2,1},{3,2},{4,7},{5,4},{6,5},{7,6},{8,11},{9,8},{10,9... | collective-permute-start | bytes 1572872 | tf_op jit(solution)/shard_map/ppermute | solution.py:274
  97.4 24.2 %collective-permute-start.2 = (bf16[1024,256]{1,0:T(8,128)(2,1)}, bf16[1024,256]{1,0:T(8,128)(2,1)S(1)}, u32[]{:S(2)}, u32[]{:S(2)}) collective-permute-start(bf16[1024,256]{1,0:T(8,128)(2,1)} %get-tuple-element.26.refs_1_), channel_id=1, source_target_pairs={{0,1},{1,2},{2,3},{3,0},{4,5},{5,6},{6,7},{7,4},{8,9},{9,10},{10,1... | collective-permute-start | bytes 1572872 | tf_op jit(solution)/shard_map/ppermute | solution.py:274
  102.1 4.6 %copy-start.15 = (bf16[1024,256]{1,0:T(8,128)(2,1)}, bf16[1024,256]{1,0:T(8,128)(2,1)S(1)}, u32[]{:S(2)}) copy-start(bf16[1024,256]{1,0:T(8,128)(2,1)S(1)} %collective-permute-done.1.refs_4_) | copy-start | bytes 1572868
  105.9 0.9 copy-start.16
  106.7 15.0 %collective-permute-start.5 = (bf16[512,256]{1,0:T(8,128)(2,1)}, bf16[512,256]{1,0:T(8,128)(2,1)S(1)}, u32[]{:S(2)}, u32[]{:S(2)}) collective-permute-start(bf16[512,256]{1,0:T(8,128)(2,1)} %slice.19), channel_id=1, source_target_pairs={{0,3},{1,0},{2,1},{3,2},{4,7},{5,4},{6,5},{7,6},{8,11},{9,8},{10,9... | collective-permute-start | bytes 786440 | tf_op jit(solution)/shard_map/ppermute | solution.py:274
  106.8 14.9 %collective-permute-start.4 = (bf16[512,256]{1,0:T(8,128)(2,1)S(1)}, bf16[512,256]{1,0:T(8,128)(2,1)S(1)}, u32[]{:S(2)}, u32[]{:S(2)}) collective-permute-start(bf16[512,256]{1,0:T(8,128)(2,1)S(1)} %slice.18), channel_id=1, source_target_pairs={{0,1},{1,2},{2,3},{3,0},{4,5},{5,6},{6,7},{7,4},{8,9},{9,10},{10,1... | collective-permute-start | bytes 786440 | tf_op jit(solution)/shard_map/ppermute | solution.py:274
  121.6 13.6 %copy-start.11 = (bf16[1024,256]{1,0:T(8,128)(2,1)}, bf16[1024,256]{1,0:T(8,128)(2,1)S(1)}, u32[]{:S(2)}) copy-start(bf16[1024,256]{1,0:T(8,128)(2,1)S(1)} %collective-permute-done.3.refs_8_) | copy-start | bytes 1572868
  121.7 13.6 %copy-start.13 = (bf16[1024,256]{1,0:T(8,128)(2,1)}, bf16[1024,256]{1,0:T(8,128)(2,1)S(1)}, u32[]{:S(2)}) copy-start(bf16[1024,256]{1,0:T(8,128)(2,1)S(1)} %collective-permute-done.2.refs_7_) | copy-start | bytes 1572868
  121.7 13.6 %copy-start.19 = (bf16[512,256]{1,0:T(8,128)(2,1)}, bf16[512,256]{1,0:T(8,128)(2,1)S(1)}, u32[]{:S(2)}) copy-start(bf16[512,256]{1,0:T(8,128)(2,1)S(1)} %collective-permute-done.5.refs_6_) | copy-start | bytes 786436
  121.7 13.6 %copy-start.20 = (bf16[512,256]{1,0:T(8,128)(2,1)}, bf16[512,256]{1,0:T(8,128)(2,1)S(1)}, u32[]{:S(2)}) copy-start(bf16[512,256]{1,0:T(8,128)(2,1)S(1)} %collective-permute-done.4.refs_5_) | copy-start | bytes 786436
  135.3 27.4 %all-to-all-start.3 = ((bf16[64,16,256]{2,1,0:T(8,128)(2,1)}), bf16[64,16,256]{2,1,0:T(8,128)(2,1)S(1)}, u32[]{:S(2)}, u32[]{:S(2)}) async-start(bf16[64,16,256]{2,1,0:T(8,128)(2,1)} %bitcast.11), calls=%async_computation.3 | async-start | bytes 1048576 | tf_op jit(solution)/shard_map/all_to_all | solution.py:287
  145.1 35.1 %copy-start.14 = (bf16[1024,256]{1,0:T(8,128)(2,1)S(1)}, bf16[1024,256]{1,0:T(8,128)(2,1)}, u32[]{:S(2)}) copy-start(bf16[1024,256]{1,0:T(8,128)(2,1)} %copy-done.13) | copy-start | bytes 1572868
  145.1 35.1 %copy-start.12 = (bf16[1024,256]{1,0:T(8,128)(2,1)S(1)}, bf16[1024,256]{1,0:T(8,128)(2,1)}, u32[]{:S(2)}) copy-start(bf16[1024,256]{1,0:T(8,128)(2,1)} %copy-done.11) | copy-start | bytes 1572868
  145.2 14.5 %collective-permute-start.9 = (bf16[1024,256]{1,0:T(8,128)(2,1)}, bf16[1024,256]{1,0:T(8,128)(2,1)S(1)}, u32[]{:S(2)}, u32[]{:S(2)}) collective-permute-start(bf16[1024,256]{1,0:T(8,128)(2,1)} %get-tuple-element.38.refs_2_), channel_id=1, source_target_pairs={{0,3},{1,0},{2,1},{3,2},{4,7},{5,4},{6,5},{7,6},{8,11},{9,8},{10,9... | collective-permute-start | bytes 1572872 | tf_op jit(solution)/shard_map/ppermute | solution.py:274
  145.8 15.1 %collective-permute-start.8 = (bf16[1024,256]{1,0:T(8,128)(2,1)}, bf16[1024,256]{1,0:T(8,128)(2,1)S(1)}, u32[]{:S(2)}, u32[]{:S(2)}) collective-permute-start(bf16[1024,256]{1,0:T(8,128)(2,1)} %get-tuple-element.38.refs_2_), channel_id=1, source_target_pairs={{0,1},{1,2},{2,3},{3,0},{4,5},{5,6},{6,7},{7,4},{8,9},{9,10},{10,1... | collective-permute-start | bytes 1572872 | tf_op jit(solution)/shard_map/ppermute | solution.py:274
  159.6 26.1 %copy-start.17 = (bf16[1024,256]{1,0:T(8,128)(2,1)}, bf16[1024,256]{1,0:T(8,128)(2,1)S(1)}, u32[]{:S(2)}) copy-start(bf16[1024,256]{1,0:T(8,128)(2,1)S(1)} %collective-permute-done.9.refs_1_) | copy-start | bytes 1572868
  161.0 24.8 %copy-start.18 = (bf16[1024,256]{1,0:T(8,128)(2,1)}, bf16[1024,256]{1,0:T(8,128)(2,1)S(1)}, u32[]{:S(2)}) copy-start(bf16[1024,256]{1,0:T(8,128)(2,1)S(1)} %collective-permute-done.8.refs_0_) | copy-start | bytes 1572868
  171.6 27.7 %all-to-all-start.5 = ((bf16[64,16,256]{2,1,0:T(8,128)(2,1)}), bf16[64,16,256]{2,1,0:T(8,128)(2,1)S(1)}, u32[]{:S(2)}, u32[]{:S(2)}) async-start(bf16[64,16,256]{2,1,0:T(8,128)(2,1)} %broadcast_in_dim.10), calls=%async_computation.5 | async-start | bytes 1048576 | tf_op jit(solution)/shard_map/all_to_all | solution.py:287
  180.3 9.2 %collective-permute-start.7 = (bf16[512,256]{1,0:T(8,128)(2,1)S(1)}, bf16[512,256]{1,0:T(8,128)(2,1)S(1)}, u32[]{:S(2)}, u32[]{:S(2)}) collective-permute-start(bf16[512,256]{1,0:T(8,128)(2,1)S(1)} %slice.21), channel_id=1, source_target_pairs={{0,3},{1,0},{2,1},{3,2},{4,7},{5,4},{6,5},{7,6},{8,11},{9,8},{10,9... | collective-permute-start | bytes 786440 | tf_op jit(solution)/shard_map/ppermute | solution.py:274
  181.5 10.4 %collective-permute-start.6 = (bf16[512,256]{1,0:T(8,128)(2,1)S(1)}, bf16[512,256]{1,0:T(8,128)(2,1)S(1)}, u32[]{:S(2)}, u32[]{:S(2)}) collective-permute-start(bf16[512,256]{1,0:T(8,128)(2,1)S(1)} %slice.20), channel_id=1, source_target_pairs={{0,1},{1,2},{2,3},{3,0},{4,5},{5,6},{6,7},{7,4},{8,9},{9,10},{10,1... | collective-permute-start | bytes 786440 | tf_op jit(solution)/shard_map/ppermute | solution.py:274
  182.4 14.0 %collective-permute-start.10 = (bf16[512,256]{1,0:T(8,128)(2,1)S(1)}, bf16[512,256]{1,0:T(8,128)(2,1)S(1)}, u32[]{:S(2)}, u32[]{:S(2)}) collective-permute-start(bf16[512,256]{1,0:T(8,128)(2,1)S(1)} %slice.22), channel_id=1, source_target_pairs={{0,1},{1,2},{2,3},{3,0},{4,5},{5,6},{6,7},{7,4},{8,9},{9,10},{10,1... | collective-permute-start | bytes 786440 | tf_op jit(solution)/shard_map/ppermute | solution.py:274
  183.1 13.4 %collective-permute-start.11 = (bf16[512,256]{1,0:T(8,128)(2,1)S(1)}, bf16[512,256]{1,0:T(8,128)(2,1)}, u32[]{:S(2)}, u32[]{:S(2)}) collective-permute-start(bf16[512,256]{1,0:T(8,128)(2,1)S(1)} %slice.23), channel_id=1, source_target_pairs={{0,3},{1,0},{2,1},{3,2},{4,7},{5,4},{6,5},{7,6},{8,11},{9,8},{10,9... | collective-permute-start | bytes 786440 | tf_op jit(solution)/shard_map/ppermute | solution.py:274
  189.5 6.9 %copy-start.21 = (bf16[512,256]{1,0:T(8,128)(2,1)}, bf16[512,256]{1,0:T(8,128)(2,1)S(1)}, u32[]{:S(2)}) copy-start(bf16[512,256]{1,0:T(8,128)(2,1)S(1)} %collective-permute-done.7.refs_1_) | copy-start | bytes 786436
  191.9 4.5 %copy-start.22 = (bf16[512,256]{1,0:T(8,128)(2,1)}, bf16[512,256]{1,0:T(8,128)(2,1)S(1)}, u32[]{:S(2)}) copy-start(bf16[512,256]{1,0:T(8,128)(2,1)S(1)} %collective-permute-done.6.refs_0_) | copy-start | bytes 786436
  196.4 0.7 copy-start.23

commit v5 on v4

--- a/solution.py
+++ b/solution.py
@@ -30,18 +30,35 @@
 ANY = pl.BlockSpec(memory_space=pl.ANY)
 
 
-def pull_kernel(lo, capacity, wanted, history, rows_o, tables, folded, rows, sems):
+def pull_kernel(lo, capacity, wanted, history, rows_o, tables, folded, rows, packed, sems, out_sems):
     count, slab, width = tables.shape
-    parts, slots, _ = rows_o.shape
+    parts, slots, _ = packed.shape
     lanes = width // 2
     unroll = 4
-    copies = [pltpu.make_async_copy(history.at[lo + i], tables.at[i], sems.at[i]) for i in range(count)]
-    for copy in copies:
-        copy.start()
+    cuts = out_sems.shape[0]
+    size, share = slab // cuts, parts // cuts
+    copies = [
+        [
+            pltpu.make_async_copy(
+                history.at[lo + i, pl.ds(j * size, size), :],
+                tables.at[i, pl.ds(j * size, size), :],
+                sems.at[i, j],
+            )
+            for j in range(cuts)
+        ]
+        for i in range(count)
+    ]
+    for layer in copies:
+        for copy in layer:
+            copy.start()
+    sent = []
     for layer in range(count):
-        copies[layer].wait()
-        folded[pl.ds(0, slab, stride=2), :] = tables[layer, :, :lanes].astype(f32)
-        folded[pl.ds(1, slab, stride=2), :] = tables[layer, :, lanes:].astype(f32)
+        for j in range(cuts):
+            copies[layer][j].wait()
+            for side in range(2):
+                folded[pl.ds(2 * j * size + side, size, stride=2), :] = tables[
+                    layer, j * size : (j + 1) * size, side * lanes : (side + 1) * lanes
+                ].astype(f32)
 
         def step(i, carry):
             for u in range(unroll):
@@ -52,26 +69,43 @@
                     rows[pl.ds(base + 2 * (layer * capacity + c), 2), :] = folded[pl.ds(row, 2), :]
             return carry
 
-        lax.fori_loop(0, parts // unroll, step, 0)
-    for side in range(2):
-        half = rows[pl.ds(side, parts * slots, stride=2), :]
-        rows_o[:, :, side * lanes : (side + 1) * lanes] = half.reshape(parts, slots, lanes).astype(bf16)
+        if layer + 1 < count:
+            lax.fori_loop(0, parts // unroll, step, 0)
+            continue
+        for j in range(cuts):
+            lax.fori_loop(j * share // unroll, (j + 1) * share // unroll, step, 0)
+            for side in range(2):
+                half = rows[pl.ds(2 * j * share * slots + side, share * slots, stride=2), :]
+                packed[j * share : (j + 1) * share, :, side * lanes : (side + 1) * lanes] = half.reshape(
+                    share, slots, lanes
+                ).astype(bf16)
+            sent.append(
+                pltpu.make_async_copy(
+                    packed.at[pl.ds(j * share, share)], rows_o.at[pl.ds(j * share, share)], out_sems.at[j]
+                )
+            )
+            sent[j].start()
+    for copy in sent:
+        copy.wait()
 
 
 def pull_rows(wanted, history, lo, count, capacity):
     _, slab, width = history.shape
     parts = wanted.shape[0]
     shape = (parts, count * capacity, width)
+    cuts = 4
     return pl.pallas_call(
         functools.partial(pull_kernel, lo, capacity),
         out_shape=jax.ShapeDtypeStruct(shape, bf16),
         in_specs=[SMEM, ANY],
-        out_specs=VMEM,
+        out_specs=ANY,
         scratch_shapes=[
             pltpu.VMEM((count, slab, width), bf16),
             pltpu.VMEM((2 * slab, width // 2), f32),
             pltpu.VMEM((2 * parts * count * capacity, width // 2), f32),
-            pltpu.SemaphoreType.DMA((count,)),
+            pltpu.VMEM(shape, bf16),
+            pltpu.SemaphoreType.DMA((count, cuts)),
+            pltpu.SemaphoreType.DMA((cuts,)),
         ],
         compiler_params=pltpu.CompilerParams(vmem_limit_bytes=vmem_limit),
         cost_estimate=pl.CostEstimate(flops=0, bytes_accessed=20_000_000, transcendentals=0),
@@ -361,7 +395,8 @@
     whole = exchange(jnp.broadcast_to(mine.astype(bf16)[None], (parts, chunk, width)), "dom")
     weight_grad = whole.astype(f32).reshape(layer_count, width, width)
     new_history = place(beside(2), new_history)
-    new_history = place(across(1) + across(2), new_history)
+    new_history = place(across(1), new_history)
+    new_history = place(across(2), new_history)
     return (hidden, new_history, weight_grad)
 
 

time: 201 us -> 202 us (level)
  local copies, waits for them, and re-layouts: 8.2 us -> 10.4 us
    ppermute x12, waiting for transfers between devices: 26.2 us -> 23.6 us  [move(): lax.ppermute(value, 'rep', [(i, (i + by) % size) for i in range(size)])]
    pallas_call x3 -> x4, Pallas kernels: 8.59 us -> 10.1 us  [assemble(): pl.pallas_call(functools.partial(assemble_kernel, places, replicas, rows,...]
    unnamed x53 -> x55, local copies, waits for them, and re-layouts: 5.18 us -> 6.6 us
  transfers between devices with their start and end apart: 16 -> 16, of which waited for: 10 -> 10; matrix products, arithmetic and copies ran while one was open for 1% -> 2% of each run, Pallas kernels for 11% -> 12%
where the time goes in v5:
time: 202 us; the launch traced here: 201 us
  waiting for transfers between devices  69.4 us (34%)
  starting transfers between devices  45.2 us (22%)
  Pallas kernels  45 us (22%)
  blocking collectives  28.4 us (14%)
  local copies, waits for them, and re-layouts  10.4 us (5%)
    all_to_all x4, waiting for transfers between devices, exchange(): return lax.all_to_all(value, axis, split_axis=0, concat_axis=0, tiled=True)  45.8 us
    all_to_all x4, starting transfers between devices, exchange(): return lax.all_to_all(value, axis, split_axis=0, concat_axis=0, tiled=True)  29.5 us
    all_to_all x2, blocking collectives, exchange(): return lax.all_to_all(value, axis, split_axis=0, concat_axis=0, tiled=True)  28.4 us
    ppermute x12, waiting for transfers between devices, move(): lax.ppermute(value, 'rep', [(i, (i + by) % size) for i in range(size)])  23.6 us
    ppermute x12, starting transfers between devices, move(): lax.ppermute(value, 'rep', [(i, (i + by) % size) for i in range(size)])  15.8 us
    pallas_call x2, Pallas kernels, pull_rows(): pl.pallas_call(functools.partial(pull_kernel, lo, capacity), out_shape=ja...  15.4 us
    pallas_call x1, Pallas kernels, finish(): pl.pallas_call(functools.partial(finish_kernel, half), out_shape=(block,)...  13.6 us
    pallas_call x4, Pallas kernels, assemble(): pl.pallas_call(functools.partial(assemble_kernel, places, replicas, rows,...  10.1 us
  transfers between devices with their start and end apart: 16, of which 10 were waited for; matrix products, arithmetic and copies ran while one was open for 2% of the time, Pallas kernels for 12%

profile of v5, /device:TPU:2, one launch (start us, length us, event | category | flops | bytes accessed | tf_op | source)
XLA Modules:
  0.0 200.7 jit_solution(3324062896641152798)
XLA Ops:
  0.6 0.8 reshape.30
  1.5 0.1 copy.24
  1.6 0.1 copy.25
  1.6 20.4 %all_to_all.36 = s32[64,1,96]{2,1,0:T(1,128)} all-to-all(s32[64,1,96]{2,1,0:T(1,128)S(1)} %copy.25), channel_id=1, replica_groups=mesh['dom'=64,'rep'=4] {'dom'}, dimensions={0} | all-to-all | bytes 49152 | tf_op jit(solution)/shard_map/all_to_all | solution.py:321
  22.1 7.6 %shard_map.121 = bf16[64,48,256]{2,1,0:T(8,128)(2,1)} custom-call(s32[64,96]{1,0:T(8,128)} %bitcast.13, bf16[4,4096,256]{2,1,0:T(8,128)(2,1)} %history.3), custom_call_target="tpu_custom_call" | custom-call | bytes 20000000 | tf_op jit(solution)/shard_map/pallas_call | solution.py:97
  29.7 5.7 %all-to-all-start.1 = ((bf16[64,48,256]{2,1,0:T(8,128)(2,1)}), bf16[64,48,256]{2,1,0:T(8,128)(2,1)S(1)}, u32[]{:S(2)}, u32[]{:S(2)}) async-start(bf16[64,48,256]{2,1,0:T(8,128)(2,1)} %shard_map.121), calls=%async_computation.1 | async-start | bytes 3145728 | tf_op jit(solution)/shard_map/all_to_all | solution.py:321
  35.4 0.0 copy-start.26
  35.4 0.0 copy-start.25
  35.5 0.0 copy-start
  35.5 0.0 copy-start.5
  35.5 0.0 copy-start.6
  35.5 7.8 %shard_map.124 = bf16[64,48,256]{2,1,0:T(8,128)(2,1)} custom-call(s32[64,96]{1,0:T(8,128)} %bitcast.14, bf16[4,4096,256]{2,1,0:T(8,128)(2,1)} %history.3), custom_call_target="tpu_custom_call" | custom-call | bytes 20000000 | tf_op jit(solution)/shard_map/pallas_call | solution.py:97
  43.3 32.3 %all-to-all-done.1.pulled = bf16[64,48,256]{2,1,0:T(8,128)(2,1)S(1)} async-done(((bf16[64,48,256]{2,1,0:T(8,128)(2,1)}), bf16[64,48,256]{2,1,0:T(8,128)(2,1)S(1)}, u32[]{:S(2)}, u32[]{:S(2)}) %all-to-all-start.1) | async-done | bytes 1572896 | tf_op jit(solution)/shard_map/all_to_all | solution.py:321
  75.6 5.6 %all-to-all-start.2 = ((bf16[64,48,256]{2,1,0:T(8,128)(2,1)}), bf16[64,48,256]{2,1,0:T(8,128)(2,1)}, u32[]{:S(2)}, u32[]{:S(2)}) async-start(bf16[64,48,256]{2,1,0:T(8,128)(2,1)} %shard_map.124), calls=%async_computation.2 | async-start | bytes 3145728 | tf_op jit(solution)/shard_map/all_to_all | solution.py:321
  81.2 0.1 lt.21
  81.3 0.1 lt.23
  81.4 0.1 lt.24
  81.6 0.0 copy-start.3
  81.6 1.0 copy-done.3
  82.6 1.0 copy-done.4
  83.7 2.6 %shard_map.122 = (bf16[1024,256]{1,0:T(8,128)(2,1)S(1)}, f32[1024,256]{1,0:T(8,128)S(1)}, bf16[1024,256]{1,0:T(8,128)(2,1)S(1)}) custom-call(s32[32]{0:T(128)S(1)} %copy-done.6, bf16[1024,256]{1,0:T(8,128)(2,1)S(1)} %copy-done.3, bf16[32,128,128]{2,1,0:T(8,128)(2,1)S(1)} %copy-done, bf16[64,48,256]{2,1,0:T(8,128)(2,1)S(1)} %all-to-all-done.1.pulled, ...), custom_call_target="tpu_custom_call" | custom-call | flops 1300000000 | bytes 6000000 | tf_op jit(solution)/shard_map/pallas_call | solution.py:163
  86.2 0.0 copy-start.7
  86.3 3.1 %collective-permute-start.1 = (bf16[1024,256]{1,0:T(8,128)(2,1)S(1)}, bf16[1024,256]{1,0:T(8,128)(2,1)S(1)}, u32[]{:S(2)}, u32[]{:S(2)}) collective-permute-start(bf16[1024,256]{1,0:T(8,128)(2,1)S(1)} %get-tuple-element.24.hidden.refs_0_), channel_id=1, source_target_pairs={{0,3},{1,0},{2,1},{3,2},{4,7},{5,4},{6,5},{7,6},{8,11},{9,8},{10,9... | collective-permute-start | bytes 1572872 | tf_op jit(solution)/shard_map/ppermute | solution.py:308
  89.4 3.4 %shard_map.123 = (bf16[1024,256]{1,0:T(8,128)(2,1)S(1)}, f32[1024,256]{1,0:T(8,128)S(1)}, bf16[1024,256]{1,0:T(8,128)(2,1)}) custom-call(s32[32]{0:T(128)S(1)} %copy-done.6, bf16[1024,256]{1,0:T(8,128)(2,1)S(1)} %get-tuple-element.24.hidden.refs_0_, bf16[32,128,128]{2,1,0:T(8,128)(2,1)S(1)} %copy-done, bf16[64,48,256]{2,1,0:T(8,128)(2,1)S(1)} %all-to-all-done.1.pulled, ...), custom_call_target="tpu_custom_call" | custom-call | flops 1300000000 | bytes 6000000 | tf_op jit(solution)/shard_map/pallas_call | solution.py:163
  92.7 1.0 copy-done.8
  93.7 3.2 %collective-permute-start.3 = (bf16[1024,256]{1,0:T(8,128)(2,1)}, bf16[1024,256]{1,0:T(8,128)(2,1)S(1)}, u32[]{:S(2)}, u32[]{:S(2)}) collective-permute-start(bf16[1024,256]{1,0:T(8,128)(2,1)} %get-tuple-element.26.refs_1_), channel_id=1, source_target_pairs={{0,3},{1,0},{2,1},{3,2},{4,7},{5,4},{6,5},{7,6},{8,11},{9,8},{10,9... | collective-permute-start | bytes 1572872 | tf_op jit(solution)/shard_map/ppermute | solution.py:308
  96.9 4.7 %collective-permute-done.1.refs_4_ = bf16[1024,256]{1,0:T(8,128)(2,1)S(1)} collective-permute-done((bf16[1024,256]{1,0:T(8,128)(2,1)S(1)}, bf16[1024,256]{1,0:T(8,128)(2,1)S(1)}, u32[]{:S(2)}, u32[]{:S(2)}) %collective-permute-start.1) | collective-permute-done | bytes 524320 | tf_op jit(solution)/shard_map/ppermute | solution.py:308
  101.7 3.7 %collective-permute-done.refs_3_ = bf16[1024,256]{1,0:T(8,128)(2,1)S(1)} collective-permute-done((bf16[1024,256]{1,0:T(8,128)(2,1)S(1)}, bf16[1024,256]{1,0:T(8,128)(2,1)S(1)}, u32[]{:S(2)}, u32[]{:S(2)}) %collective-permute-start) | collective-permute-done | bytes 524320 | tf_op jit(solution)/shard_map/ppermute | solution.py:308
  105.4 0.8 slice.19
  106.2 0.0 collective-permute-start.5
  106.3 0.0 copy-done.16
  106.3 2.0 collective-permute-start.4
  108.2 1.3 copy.26
  109.6 11.6 %all-to-all-done.2.refs_2_ = bf16[64,48,256]{2,1,0:T(8,128)(2,1)} async-done(((bf16[64,48,256]{2,1,0:T(8,128)(2,1)}), bf16[64,48,256]{2,1,0:T(8,128)(2,1)}, u32[]{:S(2)}, u32[]{:S(2)}) %all-to-all-start.2) | async-done | bytes 1572896 | tf_op jit(solution)/shard_map/all_to_all | solution.py:321
  121.1 0.0 collective-permute-done.3.refs_8_
  121.2 0.0 collective-permute-done.2.refs_7_
  121.2 13.6 %shard_map.125 = (bf16[1024,256]{1,0:T(8,128)(2,1)}, bf16[1024,256]{1,0:T(8,128)(2,1)}, bf16[4,256,256]{2,1,0:T(8,128)(2,1)}) custom-call(s32[32]{0:T(128)} %refs_0_.1, bf16[1024,256]{1,0:T(8,128)(2,1)} %get-tuple-element.26.refs_1_, bf16[64,48,256]{2,1,0:T(8,128)(2,1)} %all-to-all-done.2.refs_2_, s32[4,1536]{1,0:T(4,128)} %refs_3_.1, f32[4,1536]{1,0:T(4,128)} %copy-done.2, ...), custom_call_target="tpu_custom_call" | custom-call | flops 5000000000 | bytes 12000000 | tf_op jit(solution)/shard_map/pallas_call | solution.py:251
  134.8 9.8 %all-to-all-start.3 = ((bf16[64,16,256]{2,1,0:T(8,128)(2,1)}), bf16[64,16,256]{2,1,0:T(8,128)(2,1)S(1)}, u32[]{:S(2)}, u32[]{:S(2)}) async-start(bf16[64,16,256]{2,1,0:T(8,128)(2,1)} %bitcast.11), calls=%async_computation.3 | async-start | bytes 1048576 | tf_op jit(solution)/shard_map/all_to_all | solution.py:321
  144.7 0.5 collective-permute-start.7
  145.1 1.6 collective-permute-start.6
  146.8 4.2 %shard_map.126.refs_2_ = bf16[3,4096,256]{2,1,0:T(8,128)(2,1)} custom-call(bf16[1024,256]{1,0:T(8,128)(2,1)} %copy-done.1, bf16[1024,256]{1,0:T(8,128)(2,1)} %get-tuple-element.26.refs_1_, bf16[1024,256]{1,0:T(8,128)(2,1)} %get-tuple-element.36.refs_2_, bf16[1024,256]{1,0:T(8,128)(2,1)} %copy-done.16, bf16[1024,256]{1,0:T(8,128)(2,1)} %copy-done.15, ...), custom_call_target="tpu_custom_call" | custom-call | bytes 4200000 | tf_op jit(solution)/shard_map/pallas_call | solution.py:295
  151.0 7.9 %collective-permute-done.7.refs_1_ = bf16[1024,256]{1,0:T(8,128)(2,1)S(1)} collective-permute-done((bf16[1024,256]{1,0:T(8,128)(2,1)}, bf16[1024,256]{1,0:T(8,128)(2,1)S(1)}, u32[]{:S(2)}, u32[]{:S(2)}) %collective-permute-start.7) | collective-permute-done | bytes 524320 | tf_op jit(solution)/shard_map/ppermute | solution.py:308
  158.9 1.3 collective-permute-done.6.refs_0_
  160.2 2.0 all-to-all-done.3
  162.2 0.1 convert_reduce_fusion
  162.3 8.0 %all_to_all.37 = f32[4,16,256]{2,1,0:T(8,128)S(1)} all-to-all(f32[4,16,256]{2,1,0:T(8,128)S(1)} %broadcast_in_dim.9), channel_id=1, replica_groups=mesh['dom'=64,'rep'=4] {'rep'}, dimensions={0} | all-to-all | bytes 131072 | tf_op jit(solution)/shard_map/all_to_all | solution.py:321
  170.3 0.8 broadcast_in_dim.10
  171.1 8.3 %all-to-all-start.5 = ((bf16[64,16,256]{2,1,0:T(8,128)(2,1)}), bf16[64,16,256]{2,1,0:T(8,128)(2,1)S(1)}, u32[]{:S(2)}, u32[]{:S(2)}) async-start(bf16[64,16,256]{2,1,0:T(8,128)(2,1)} %broadcast_in_dim.10), calls=%async_computation.5 | async-start | bytes 1048576 | tf_op jit(solution)/shard_map/all_to_all | solution.py:321
  179.5 0.7 slice.23
  180.3 1.2 collective-permute-start.11
  181.4 0.9 collective-permute-start.10
  182.3 0.6 collective-permute-start.8
  183.0 2.7 %collective-permute-start.9 = (bf16[512,256]{1,0:T(8,128)(2,1)S(1)}, bf16[512,256]{1,0:T(8,128)(2,1)S(1)}, u32[]{:S(2)}, u32[]{:S(2)}) collective-permute-start(bf16[512,256]{1,0:T(8,128)(2,1)S(1)} %slice.21), channel_id=1, source_target_pairs={{0,3},{1,0},{2,1},{3,2},{4,7},{5,4},{6,5},{7,6},{8,11},{9,8},{10,9... | collective-permute-start | bytes 786440 | tf_op jit(solution)/shard_map/ppermute | solution.py:308
  185.7 2.2 %shard_map.127.refs_2_ = bf16[3,4096,256]{2,1,0:T(8,128)(2,1)} custom-call(bf16[1024,256]{1,0:T(8,128)(2,1)} %copy-done.18, bf16[1024,256]{1,0:T(8,128)(2,1)} %copy-done.17, bf16[3,4096,256]{2,1,0:T(8,128)(2,1)} %shard_map.126.refs_2_), custom_call_target="tpu_custom_call", output_to_operand_aliasing={{}: (2, {})} | custom-call | bytes 4200000 | tf_op jit(solution)/shard_map/pallas_call | solution.py:295
  187.8 1.8 collective-permute-done.11.refs_1_
  189.6 2.2 %collective-permute-done.10.refs_0_ = bf16[512,256]{1,0:T(8,128)(2,1)S(1)} collective-permute-done((bf16[512,256]{1,0:T(8,128)(2,1)S(1)}, bf16[512,256]{1,0:T(8,128)(2,1)S(1)}, u32[]{:S(2)}, u32[]{:S(2)}) %collective-permute-start.10) | collective-permute-done | bytes 262176 | tf_op jit(solution)/shard_map/ppermute | solution.py:308
  191.8 0.7 copy-done.24
  192.5 1.8 shard_map.128.refs_2_
  194.4 2.0 collective-permute-done.8.refs_0_
  196.3 0.7 copy-done.21
  197.0 0.7 copy-done.23
  197.8 1.8 shard_map.129
  199.6 0.0 all-to-all-done.5
  199.6 1.1 bitcast_convert_fusion
  (53 shorter events, 0.2 us)
Async XLA Ops:
  29.7 45.9 %all-to-all-start.1 = ((bf16[64,48,256]{2,1,0:T(8,128)(2,1)}), bf16[64,48,256]{2,1,0:T(8,128)(2,1)S(1)}, u32[]{:S(2)}, u32[]{:S(2)}) async-start(bf16[64,48,256]{2,1,0:T(8,128)(2,1)} %shard_map.121), calls=%async_computation.1 | async-start | bytes 3145728 | tf_op jit(solution)/shard_map/all_to_all | solution.py:321
  35.4 45.8 %copy-start.26 = (s32[4,64]{1,0:T(4,128)S(1)}, s32[4,64]{1,0:T(4,128)}, u32[]{:S(2)}) copy-start(s32[4,64]{1,0:T(4,128)} %param.15) | copy-start | bytes 3076
  35.4 46.1 %copy-start.25 = (bf16[4,1536]{1,0:T(4,128)(2,1)S(1)}, bf16[4,1536]{1,0:T(4,128)(2,1)}, u32[]{:S(2)}) copy-start(bf16[4,1536]{1,0:T(4,128)(2,1)} %param.17) | copy-start | bytes 36868
  35.5 46.1 %copy-start = (bf16[32,128,128]{2,1,0:T(8,128)(2,1)S(1)}, bf16[32,128,128]{2,1,0:T(8,128)(2,1)}, u32[]{:S(2)}) copy-start(bf16[32,128,128]{2,1,0:T(8,128)(2,1)} %refs_6_.1) | copy-start | bytes 3145732
  35.5 46.1 %copy-start.5 = (s32[4,1536]{1,0:T(4,128)S(1)}, s32[4,1536]{1,0:T(4,128)}, u32[]{:S(2)}) copy-start(s32[4,1536]{1,0:T(4,128)} %refs_3_.1) | copy-start | bytes 73732
  35.5 46.1 %copy-start.6 = (s32[32]{0:T(128)S(1)}, s32[32]{0:T(128)}, u32[]{:S(2)}) copy-start(s32[32]{0:T(128)} %refs_0_.1) | copy-start | bytes 388
  75.6 45.6 %all-to-all-start.2 = ((bf16[64,48,256]{2,1,0:T(8,128)(2,1)}), bf16[64,48,256]{2,1,0:T(8,128)(2,1)}, u32[]{:S(2)}, u32[]{:S(2)}) async-start(bf16[64,48,256]{2,1,0:T(8,128)(2,1)} %shard_map.124), calls=%async_computation.2 | async-start | bytes 3145728 | tf_op jit(solution)/shard_map/all_to_all | solution.py:321
  81.6 1.0 copy-start.3
  82.6 1.0 copy-start.4
  83.7 25.9 %copy-start.2 = (f32[4,1536]{1,0:T(4,128)}, f32[4,1536]{1,0:T(4,128)S(1)}, u32[]{:S(2)}) copy-start(f32[4,1536]{1,0:T(4,128)S(1)} %convert_select_fusion.wt.refs_4_) | copy-start | bytes 73732
  86.2 19.1 %copy-start.7 = (f32[1024,256]{1,0:T(8,128)}, f32[1024,256]{1,0:T(8,128)S(1)}, u32[]{:S(2)}) copy-start(f32[1024,256]{1,0:T(8,128)S(1)} %get-tuple-element.32.refs_12_) | copy-start | bytes 3145732
  86.3 19.2 %copy-start.9 = (bf16[1024,256]{1,0:T(8,128)(2,1)}, bf16[1024,256]{1,0:T(8,128)(2,1)S(1)}, u32[]{:S(2)}) copy-start(bf16[1024,256]{1,0:T(8,128)(2,1)S(1)} %get-tuple-element.30.refs_10_) | copy-start | bytes 1572868
  86.3 48.5 %copy-start.1 = (bf16[1024,256]{1,0:T(8,128)(2,1)}, bf16[1024,256]{1,0:T(8,128)(2,1)S(1)}, u32[]{:S(2)}) copy-start(bf16[1024,256]{1,0:T(8,128)(2,1)S(1)} %get-tuple-element.24.hidden.refs_0_) | copy-start | bytes 1572868
  86.3 15.4 %collective-permute-start.1 = (bf16[1024,256]{1,0:T(8,128)(2,1)S(1)}, bf16[1024,256]{1,0:T(8,128)(2,1)S(1)}, u32[]{:S(2)}, u32[]{:S(2)}) collective-permute-start(bf16[1024,256]{1,0:T(8,128)(2,1)S(1)} %get-tuple-element.24.hidden.refs_0_), channel_id=1, source_target_pairs={{0,3},{1,0},{2,1},{3,2},{4,7},{5,4},{6,5},{7,6},{8,11},{9,8},{10,9... | collective-permute-start | bytes 1572872 | tf_op jit(solution)/shard_map/ppermute | solution.py:308
  89.4 16.0 %collective-permute-start = (bf16[1024,256]{1,0:T(8,128)(2,1)S(1)}, bf16[1024,256]{1,0:T(8,128)(2,1)S(1)}, u32[]{:S(2)}, u32[]{:S(2)}) collective-permute-start(bf16[1024,256]{1,0:T(8,128)(2,1)S(1)} %get-tuple-element.24.hidden.refs_0_), channel_id=1, source_target_pairs={{0,1},{1,2},{2,3},{3,0},{4,5},{5,6},{6,7},{7,4},{8,9},{9,10},{10,1... | collective-permute-start | bytes 1572872 | tf_op jit(solution)/shard_map/ppermute | solution.py:308
  92.7 1.0 copy-start.8
  93.7 12.5 %copy-start.10 = (bf16[1024,256]{1,0:T(8,128)(2,1)}, bf16[1024,256]{1,0:T(8,128)(2,1)S(1)}, u32[]{:S(2)}) copy-start(bf16[1024,256]{1,0:T(8,128)(2,1)S(1)} %get-tuple-element.31.refs_11_) | copy-start | bytes 1572868
  93.7 27.4 %collective-permute-start.3 = (bf16[1024,256]{1,0:T(8,128)(2,1)}, bf16[1024,256]{1,0:T(8,128)(2,1)S(1)}, u32[]{:S(2)}, u32[]{:S(2)}) collective-permute-start(bf16[1024,256]{1,0:T(8,128)(2,1)} %get-tuple-element.26.refs_1_), channel_id=1, source_target_pairs={{0,3},{1,0},{2,1},{3,2},{4,7},{5,4},{6,5},{7,6},{8,11},{9,8},{10,9... | collective-permute-start | bytes 1572872 | tf_op jit(solution)/shard_map/ppermute | solution.py:308
  96.9 24.2 %collective-permute-start.2 = (bf16[1024,256]{1,0:T(8,128)(2,1)}, bf16[1024,256]{1,0:T(8,128)(2,1)S(1)}, u32[]{:S(2)}, u32[]{:S(2)}) collective-permute-start(bf16[1024,256]{1,0:T(8,128)(2,1)} %get-tuple-element.26.refs_1_), channel_id=1, source_target_pairs={{0,1},{1,2},{2,3},{3,0},{4,5},{5,6},{6,7},{7,4},{8,9},{9,10},{10,1... | collective-permute-start | bytes 1572872 | tf_op jit(solution)/shard_map/ppermute | solution.py:308
  101.6 4.6 %copy-start.15 = (bf16[1024,256]{1,0:T(8,128)(2,1)}, bf16[1024,256]{1,0:T(8,128)(2,1)S(1)}, u32[]{:S(2)}) copy-start(bf16[1024,256]{1,0:T(8,128)(2,1)S(1)} %collective-permute-done.1.refs_4_) | copy-start | bytes 1572868
  105.4 0.9 copy-start.16
  106.2 15.0 %collective-permute-start.5 = (bf16[512,256]{1,0:T(8,128)(2,1)}, bf16[512,256]{1,0:T(8,128)(2,1)S(1)}, u32[]{:S(2)}, u32[]{:S(2)}) collective-permute-start(bf16[512,256]{1,0:T(8,128)(2,1)} %slice.19), channel_id=1, source_target_pairs={{0,3},{1,0},{2,1},{3,2},{4,7},{5,4},{6,5},{7,6},{8,11},{9,8},{10,9... | collective-permute-start | bytes 786440 | tf_op jit(solution)/shard_map/ppermute | solution.py:308
  106.3 14.9 %collective-permute-start.4 = (bf16[512,256]{1,0:T(8,128)(2,1)S(1)}, bf16[512,256]{1,0:T(8,128)(2,1)S(1)}, u32[]{:S(2)}, u32[]{:S(2)}) collective-permute-start(bf16[512,256]{1,0:T(8,128)(2,1)S(1)} %slice.18), channel_id=1, source_target_pairs={{0,1},{1,2},{2,3},{3,0},{4,5},{5,6},{6,7},{7,4},{8,9},{9,10},{10,1... | collective-permute-start | bytes 786440 | tf_op jit(solution)/shard_map/ppermute | solution.py:308
  121.1 13.6 %copy-start.11 = (bf16[1024,256]{1,0:T(8,128)(2,1)}, bf16[1024,256]{1,0:T(8,128)(2,1)S(1)}, u32[]{:S(2)}) copy-start(bf16[1024,256]{1,0:T(8,128)(2,1)S(1)} %collective-permute-done.3.refs_8_) | copy-start | bytes 1572868
  121.2 13.6 %copy-start.13 = (bf16[1024,256]{1,0:T(8,128)(2,1)}, bf16[1024,256]{1,0:T(8,128)(2,1)S(1)}, u32[]{:S(2)}) copy-start(bf16[1024,256]{1,0:T(8,128)(2,1)S(1)} %collective-permute-done.2.refs_7_) | copy-start | bytes 1572868
  121.2 13.6 %copy-start.19 = (bf16[512,256]{1,0:T(8,128)(2,1)}, bf16[512,256]{1,0:T(8,128)(2,1)S(1)}, u32[]{:S(2)}) copy-start(bf16[512,256]{1,0:T(8,128)(2,1)S(1)} %collective-permute-done.5.refs_6_) | copy-start | bytes 786436
  121.2 13.6 %copy-start.20 = (bf16[512,256]{1,0:T(8,128)(2,1)}, bf16[512,256]{1,0:T(8,128)(2,1)S(1)}, u32[]{:S(2)}) copy-start(bf16[512,256]{1,0:T(8,128)(2,1)S(1)} %collective-permute-done.4.refs_5_) | copy-start | bytes 786436
  134.8 27.4 %all-to-all-start.3 = ((bf16[64,16,256]{2,1,0:T(8,128)(2,1)}), bf16[64,16,256]{2,1,0:T(8,128)(2,1)S(1)}, u32[]{:S(2)}, u32[]{:S(2)}) async-start(bf16[64,16,256]{2,1,0:T(8,128)(2,1)} %bitcast.11), calls=%async_computation.3 | async-start | bytes 1048576 | tf_op jit(solution)/shard_map/all_to_all | solution.py:321
  144.6 34.9 %copy-start.14 = (bf16[1024,256]{1,0:T(8,128)(2,1)S(1)}, bf16[1024,256]{1,0:T(8,128)(2,1)}, u32[]{:S(2)}) copy-start(bf16[1024,256]{1,0:T(8,128)(2,1)} %copy-done.13) | copy-start | bytes 1572868
  144.6 34.9 %copy-start.12 = (bf16[1024,256]{1,0:T(8,128)(2,1)S(1)}, bf16[1024,256]{1,0:T(8,128)(2,1)}, u32[]{:S(2)}) copy-start(bf16[1024,256]{1,0:T(8,128)(2,1)} %copy-done.11) | copy-start | bytes 1572868
  144.7 14.3 %collective-permute-start.7 = (bf16[1024,256]{1,0:T(8,128)(2,1)}, bf16[1024,256]{1,0:T(8,128)(2,1)S(1)}, u32[]{:S(2)}, u32[]{:S(2)}) collective-permute-start(bf16[1024,256]{1,0:T(8,128)(2,1)} %get-tuple-element.36.refs_2_), channel_id=1, source_target_pairs={{0,3},{1,0},{2,1},{3,2},{4,7},{5,4},{6,5},{7,6},{8,11},{9,8},{10,9... | collective-permute-start | bytes 1572872 | tf_op jit(solution)/shard_map/ppermute | solution.py:308
  145.1 15.1 %collective-permute-start.6 = (bf16[1024,256]{1,0:T(8,128)(2,1)}, bf16[1024,256]{1,0:T(8,128)(2,1)S(1)}, u32[]{:S(2)}, u32[]{:S(2)}) collective-permute-start(bf16[1024,256]{1,0:T(8,128)(2,1)} %get-tuple-element.36.refs_2_), channel_id=1, source_target_pairs={{0,1},{1,2},{2,3},{3,0},{4,5},{5,6},{6,7},{7,4},{8,9},{9,10},{10,1... | collective-permute-start | bytes 1572872 | tf_op jit(solution)/shard_map/ppermute | solution.py:308
  158.9 26.7 %copy-start.17 = (bf16[1024,256]{1,0:T(8,128)(2,1)}, bf16[1024,256]{1,0:T(8,128)(2,1)S(1)}, u32[]{:S(2)}) copy-start(bf16[1024,256]{1,0:T(8,128)(2,1)S(1)} %collective-permute-done.7.refs_1_) | copy-start | bytes 1572868
  160.2 25.4 %copy-start.18 = (bf16[1024,256]{1,0:T(8,128)(2,1)}, bf16[1024,256]{1,0:T(8,128)(2,1)S(1)}, u32[]{:S(2)}) copy-start(bf16[1024,256]{1,0:T(8,128)(2,1)S(1)} %collective-permute-done.6.refs_0_) | copy-start | bytes 1572868
  171.1 28.5 %all-to-all-start.5 = ((bf16[64,16,256]{2,1,0:T(8,128)(2,1)}), bf16[64,16,256]{2,1,0:T(8,128)(2,1)S(1)}, u32[]{:S(2)}, u32[]{:S(2)}) async-start(bf16[64,16,256]{2,1,0:T(8,128)(2,1)} %broadcast_in_dim.10), calls=%async_computation.5 | async-start | bytes 1048576 | tf_op jit(solution)/shard_map/all_to_all | solution.py:321
  180.3 9.4 %collective-permute-start.11 = (bf16[512,256]{1,0:T(8,128)(2,1)}, bf16[512,256]{1,0:T(8,128)(2,1)S(1)}, u32[]{:S(2)}, u32[]{:S(2)}) collective-permute-start(bf16[512,256]{1,0:T(8,128)(2,1)} %slice.23), channel_id=1, source_target_pairs={{0,3},{1,0},{2,1},{3,2},{4,7},{5,4},{6,5},{7,6},{8,11},{9,8},{10,9... | collective-permute-start | bytes 786440 | tf_op jit(solution)/shard_map/ppermute | solution.py:308
  181.4 10.4 %collective-permute-start.10 = (bf16[512,256]{1,0:T(8,128)(2,1)S(1)}, bf16[512,256]{1,0:T(8,128)(2,1)S(1)}, u32[]{:S(2)}, u32[]{:S(2)}) collective-permute-start(bf16[512,256]{1,0:T(8,128)(2,1)S(1)} %slice.22), channel_id=1, source_target_pairs={{0,1},{1,2},{2,3},{3,0},{4,5},{5,6},{6,7},{7,4},{8,9},{9,10},{10,1... | collective-permute-start | bytes 786440 | tf_op jit(solution)/shard_map/ppermute | solution.py:308
  182.3 14.0 %collective-permute-start.8 = (bf16[512,256]{1,0:T(8,128)(2,1)S(1)}, bf16[512,256]{1,0:T(8,128)(2,1)S(1)}, u32[]{:S(2)}, u32[]{:S(2)}) collective-permute-start(bf16[512,256]{1,0:T(8,128)(2,1)S(1)} %slice.20), channel_id=1, source_target_pairs={{0,1},{1,2},{2,3},{3,0},{4,5},{5,6},{6,7},{7,4},{8,9},{9,10},{10,1... | collective-permute-start | bytes 786440 | tf_op jit(solution)/shard_map/ppermute | solution.py:308
  183.0 13.4 %collective-permute-start.9 = (bf16[512,256]{1,0:T(8,128)(2,1)S(1)}, bf16[512,256]{1,0:T(8,128)(2,1)S(1)}, u32[]{:S(2)}, u32[]{:S(2)}) collective-permute-start(bf16[512,256]{1,0:T(8,128)(2,1)S(1)} %slice.21), channel_id=1, source_target_pairs={{0,3},{1,0},{2,1},{3,2},{4,7},{5,4},{6,5},{7,6},{8,11},{9,8},{10,9... | collective-permute-start | bytes 786440 | tf_op jit(solution)/shard_map/ppermute | solution.py:308
  189.6 2.2 %copy-start.22 = (bf16[512,256]{1,0:T(8,128)(2,1)}, bf16[512,256]{1,0:T(8,128)(2,1)S(1)}, u32[]{:S(2)}) copy-start(bf16[512,256]{1,0:T(8,128)(2,1)S(1)} %collective-permute-done.11.refs_1_) | copy-start | bytes 786436
  191.8 0.7 copy-start.24
  196.3 0.7 copy-start.21
  197.0 0.7 copy-start.23
